TPU v7x, 128 devices: a whole 4x4x4 slice. The times are simulated.
128 devices in a mesh: row: 16 (over z_lo, x, core), col: 8 (over z_hi, y).
Axes of the slice: x: 4, y: 4, z: 4 (z_hi: 2, z_lo: 2; z = z_hi * 2 + z_lo), core: 2. Of those that a mesh axis runs over, the one named last changes fastest.
Arguments:
- features: bfloat16 [49152, 128], P(('row', 'col')), may hold values from -6 to 6
- weight: bfloat16 [128, 256], replicated, may hold values from -0.5 to 0.5
- tile_values: bfloat16 [16, 8, 512, 128, 128], P('row', 'col'), may hold values from -0.0390625 to 0.0390625
- tile_rows: int32 [16, 8, 512], P('row', 'col'), may hold values from 0 to 23
- tile_cols: int32 [16, 8, 512], P('row', 'col'), may hold values from 0 to 47
- tile_count: int32 [16, 8], P('row', 'col'), may hold values from 1 to 512, as said below
- cotangent: bfloat16 [49152, 256], P(('row', 'col')), may hold values from -6 to 6
Outputs:
- hidden: bfloat16 [49152, 256], P(('row', 'col'))
- grad_weight: float32 [128, 256], replicated
- grad_features: bfloat16 [49152, 128], P(('row', 'col'))
Inputs may be any that keep to these rules, and one draw needn't show every extreme that they name: `tile_count`: some device has all 512 slots live.
All inputs are finite; a program needn't handle non-finite values.
Results may differ from a plain program's by a relative error of at most 0.022.
Values may be sent and summed in bfloat16 or wider, within the bound.
No kernel may reach another device: no remote copies, remote signals or barrier semaphores. Data moves between devices by JAX's collectives and lax.ppermute only.
A program may use at most 128 MiB of HBM per device.

v0:
```python
import jax
import jax.numpy as jnp
from jax import lax
from jax.sharding import PartitionSpec as P

group_size = 64


def gelu_tanh(value):
    return jax.nn.gelu(value, approximate=True)


def block_product(tiles, gather_idx, place_idx, live, sources, out_blocks, transposed):
    slots = tiles.shape[0]
    width = sources[0].shape[2]
    step_size = min(group_size, slots)
    turns = slots // step_size
    form = "kba,kbf->kaf" if transposed else "kab,kbf->kaf"
    targets = jnp.arange(out_blocks, dtype=jnp.int32)

    def one_group(total, turn):
        start = turn * step_size
        part_tiles = lax.dynamic_slice_in_dim(tiles, start, step_size, 0)
        part_gather = lax.dynamic_slice_in_dim(gather_idx, start, step_size, 0)
        part_place = lax.dynamic_slice_in_dim(place_idx, start, step_size, 0)
        part_live = lax.dynamic_slice_in_dim(live, start, step_size, 0)
        prod = jnp.einsum(
            form, part_tiles, sources[0][part_gather], preferred_element_type=jnp.float32
        )
        placing = (targets[:, None] == part_place[None, :]).astype(jnp.float32) * part_live[None, :]
        added = jnp.einsum("ok,kaf->oaf", placing, prod, precision=lax.Precision.HIGHEST)
        return (total + added, None)

    start_total = jnp.zeros((out_blocks, tiles.shape[1], width), jnp.float32)
    total, _ = lax.scan(one_group, start_total, jnp.arange(turns, dtype=jnp.int32))
    return total


def local(features, weight, tile_values, tile_rows, tile_cols, tile_count, cotangent):
    block = tile_values.shape[3]
    slots = tile_values.shape[2]
    own_blocks = features.shape[0] // block
    row_blocks = own_blocks * lax.axis_size("col")
    col_blocks = own_blocks * lax.axis_size("row")
    tiles = tile_values[0, 0]
    rows = tile_rows[0, 0]
    cols = tile_cols[0, 0]
    live = (jnp.arange(slots, dtype=jnp.int32) < tile_count[0, 0]).astype(jnp.float32)
    gathered = lax.all_gather(features, "row", axis=0, tiled=True)
    source = gathered.reshape(col_blocks, block, features.shape[1])
    partial_value = block_product(tiles, cols, rows, live, (source,), row_blocks, False)
    partial_value = partial_value.reshape(row_blocks * block, features.shape[1])
    aggregated = lax.psum_scatter(partial_value, "col", scatter_dimension=0, tiled=True).astype(
        jnp.bfloat16
    )
    pre = jnp.dot(aggregated, weight, preferred_element_type=jnp.float32)
    hidden = gelu_tanh(pre).astype(jnp.bfloat16)
    deriv = jax.vjp(gelu_tanh, pre)[1](cotangent.astype(jnp.float32))[0]
    delta = deriv.astype(jnp.bfloat16)
    own_grad = jnp.dot(aggregated.T, delta, preferred_element_type=jnp.float32)
    grad_weight = lax.psum(own_grad, ("row", "col"))
    delta_group = lax.all_gather(delta, "col", axis=0, tiled=True)
    delta_source = delta_group.reshape(row_blocks, block, delta.shape[1])
    back = block_product(tiles, rows, cols, live, (delta_source,), col_blocks, True)
    back = back.reshape(col_blocks * block, delta.shape[1])
    summed = lax.psum_scatter(
        back.astype(jnp.bfloat16), "row", scatter_dimension=0, tiled=True
    ).astype(jnp.float32)
    grad_features = jnp.dot(
        summed, weight.astype(jnp.float32).T, precision=lax.Precision.HIGHEST
    ).astype(jnp.bfloat16)
    return (hidden, grad_weight, grad_features)


def solution(mesh):
    return jax.shard_map(
        local,
        mesh=mesh,
        in_specs=(
            P(("row", "col"), None),
            P(),
            P("row", "col", None, None, None),
            P("row", "col", None),
            P("row", "col", None),
            P("row", "col"),
            P(("row", "col"), None),
        ),
        out_specs=(P(("row", "col"), None), P(), P(("row", "col"), None)),
        check_vma=False,
    )
```

profile of v0, /device:TPU:0, one launch (start us, length us, event | category | flops | bytes accessed | tf_op | source)
XLA Modules:
  0.0 712.2 jit_solution(14716804511595618427)
XLA Ops:
  8.6 36.7 %all-gather.3.cloned.1.call-done = bf16[6144,128]{1,0:T(8,128)(2,1)} async-done(((bf16[384,128]{1,0:T(8,128)(2,1)}), bf16[6144,128]{1,0:T(8,128)(2,1)}) %all-gather.3.cloned.1.call-update) | async-done | bytes 1572880 | tf_op jit(solution)/shard_map/all_gather | solution.py:49
  45.4 109.0 %while.22 = (s32[]{:T(128)}, f32[24,128,128]{2,0,1:T(8,128)}, s32[8]{0:T(128)S(1)}, s32[512]{0:T(512)}, f32[512]{0:T(512)S(1)}, /*index=5*/bf16[512,128,128]{2,1...) while((s32[]{:T(128)}, f32[24,128,128]{2,0,1:T(8,128)}, ...), condition=%wide.region_1.2_spmd.clone, body=%wide.region_0.1_spmd.clone.sunk | while | flops 571216064 | bytes 32512776 | solution.py:35
  53.0 4.8 select_add_fusion.4
  66.6 4.8 select_add_fusion.4
  80.2 4.8 select_add_fusion.4
  93.8 4.8 select_add_fusion.4
  107.5 4.8 select_add_fusion.4
  121.1 4.8 select_add_fusion.4
  134.7 4.8 select_add_fusion.4
  148.3 4.8 select_add_fusion.4
  154.3 2.9 copy.10
  157.3 74.6 %reduce-scatter.3.cloned.1.call-done = f32[384,128]{1,0:T(8,128)} async-done(((f32[3072,128]{1,0:T(8,128)}), f32[384,128]{1,0:T(8,128)}) %reduce-scatter.3.cloned.1.call-update) | async-done | bytes 196624 | tf_op jit(solution)/shard_map/reduce_scatter | solution.py:53
  234.2 50.1 %all-gather.5.cloned.1.call-done = bf16[3072,256]{1,0:T(8,128)(2,1)} async-done(((bf16[384,256]{1,0:T(8,128)(2,1)}), bf16[3072,256]{1,0:T(8,128)(2,1)}) %all-gather.5.cloned.1.call-update) | async-done | bytes 1572880 | tf_op jit(solution)/shard_map/all_gather | solution.py:62
  284.3 204.1 %while.23 = (s32[]{:T(128)}, f32[48,128,256]{2,0,1:T(8,128)}, s32[8]{0:T(128)S(1)}, s32[512]{0:T(512)}, f32[512]{0:T(512)S(1)}, /*index=5*/bf16[512,128,128]{2,1...) while((s32[]{:T(128)}, f32[48,128,256]{2,0,1:T(8,128)}, ...), condition=%wide.region_5.6_spmd.clone, body=%wide.region_4.5_spmd.clone.sunk | while | flops 1747983616 | bytes 88087320 | solution.py:35
  287.1 4.4 gather_fusion.1
  291.5 4.3 fusion.70
  295.8 11.3 %select_add_fusion.5 = f32[48,128,256]{2,0,1:T(8,128)S(1)} fusion(f32[48,128,256]{2,0,1:T(8,128)S(1)} %bitcast.37, pred[]{:T(512)S(6)} %compare.7, f32[64,128,256]{2,1,0:T(8,128)S(1)} %fusion.70, f32[64]{0:T(128)S(1)} %dynamic_slice.65, s32[64]{0:T(128)S(1)} %dynamic_slice.66), kind=kOutput, calls=%fused_computation.21.clone.1 | convolution fusion | flops 1211111424 | bytes 20972032 | tf_op jit(solution)/shard_map/while/body/eval_jaxpr/ok,kaf->oaf/dot_general | solution.py:31
  307.2 2.7 copy-done.1
  312.6 4.4 gather_fusion.1
  317.1 4.3 fusion.70
  321.4 11.3 %select_add_fusion.5 = f32[48,128,256]{2,0,1:T(8,128)S(1)} fusion(f32[48,128,256]{2,0,1:T(8,128)S(1)} %bitcast.37, pred[]{:T(512)S(6)} %compare.7, f32[64,128,256]{2,1,0:T(8,128)S(1)} %fusion.70, f32[64]{0:T(128)S(1)} %dynamic_slice.65, s32[64]{0:T(128)S(1)} %dynamic_slice.66), kind=kOutput, calls=%fused_computation.21.clone.1 | convolution fusion | flops 1211111424 | bytes 20972032 | tf_op jit(solution)/shard_map/while/body/eval_jaxpr/ok,kaf->oaf/dot_general | solution.py:31
  332.7 2.7 copy-done.1
  338.2 4.4 gather_fusion.1
  342.6 4.3 fusion.70
  346.9 11.3 %select_add_fusion.5 = f32[48,128,256]{2,0,1:T(8,128)S(1)} fusion(f32[48,128,256]{2,0,1:T(8,128)S(1)} %bitcast.37, pred[]{:T(512)S(6)} %compare.7, f32[64,128,256]{2,1,0:T(8,128)S(1)} %fusion.70, f32[64]{0:T(128)S(1)} %dynamic_slice.65, s32[64]{0:T(128)S(1)} %dynamic_slice.66), kind=kOutput, calls=%fused_computation.21.clone.1 | convolution fusion | flops 1211111424 | bytes 20972032 | tf_op jit(solution)/shard_map/while/body/eval_jaxpr/ok,kaf->oaf/dot_general | solution.py:31
  358.2 2.7 copy-done.1
  363.7 4.4 gather_fusion.1
  368.1 4.3 fusion.70
  372.4 11.3 %select_add_fusion.5 = f32[48,128,256]{2,0,1:T(8,128)S(1)} fusion(f32[48,128,256]{2,0,1:T(8,128)S(1)} %bitcast.37, pred[]{:T(512)S(6)} %compare.7, f32[64,128,256]{2,1,0:T(8,128)S(1)} %fusion.70, f32[64]{0:T(128)S(1)} %dynamic_slice.65, s32[64]{0:T(128)S(1)} %dynamic_slice.66), kind=kOutput, calls=%fused_computation.21.clone.1 | convolution fusion | flops 1211111424 | bytes 20972032 | tf_op jit(solution)/shard_map/while/body/eval_jaxpr/ok,kaf->oaf/dot_general | solution.py:31
  383.7 2.7 copy-done.1
  389.2 4.4 gather_fusion.1
  393.6 4.3 fusion.70
  397.9 11.3 %select_add_fusion.5 = f32[48,128,256]{2,0,1:T(8,128)S(1)} fusion(f32[48,128,256]{2,0,1:T(8,128)S(1)} %bitcast.37, pred[]{:T(512)S(6)} %compare.7, f32[64,128,256]{2,1,0:T(8,128)S(1)} %fusion.70, f32[64]{0:T(128)S(1)} %dynamic_slice.65, s32[64]{0:T(128)S(1)} %dynamic_slice.66), kind=kOutput, calls=%fused_computation.21.clone.1 | convolution fusion | flops 1211111424 | bytes 20972032 | tf_op jit(solution)/shard_map/while/body/eval_jaxpr/ok,kaf->oaf/dot_general | solution.py:31
  409.2 2.7 copy-done.1
  414.7 4.4 gather_fusion.1
  419.1 4.3 fusion.70
  423.4 11.3 %select_add_fusion.5 = f32[48,128,256]{2,0,1:T(8,128)S(1)} fusion(f32[48,128,256]{2,0,1:T(8,128)S(1)} %bitcast.37, pred[]{:T(512)S(6)} %compare.7, f32[64,128,256]{2,1,0:T(8,128)S(1)} %fusion.70, f32[64]{0:T(128)S(1)} %dynamic_slice.65, s32[64]{0:T(128)S(1)} %dynamic_slice.66), kind=kOutput, calls=%fused_computation.21.clone.1 | convolution fusion | flops 1211111424 | bytes 20972032 | tf_op jit(solution)/shard_map/while/body/eval_jaxpr/ok,kaf->oaf/dot_general | solution.py:31
  434.7 2.7 copy-done.1
  440.2 4.4 gather_fusion.1
  444.6 4.3 fusion.70
  448.9 11.3 %select_add_fusion.5 = f32[48,128,256]{2,0,1:T(8,128)S(1)} fusion(f32[48,128,256]{2,0,1:T(8,128)S(1)} %bitcast.37, pred[]{:T(512)S(6)} %compare.7, f32[64,128,256]{2,1,0:T(8,128)S(1)} %fusion.70, f32[64]{0:T(128)S(1)} %dynamic_slice.65, s32[64]{0:T(128)S(1)} %dynamic_slice.66), kind=kOutput, calls=%fused_computation.21.clone.1 | convolution fusion | flops 1211111424 | bytes 20972032 | tf_op jit(solution)/shard_map/while/body/eval_jaxpr/ok,kaf->oaf/dot_general | solution.py:31
  460.2 2.7 copy-done.1
  465.7 4.4 gather_fusion.1
  470.2 4.3 fusion.70
  474.5 11.3 %select_add_fusion.5 = f32[48,128,256]{2,0,1:T(8,128)S(1)} fusion(f32[48,128,256]{2,0,1:T(8,128)S(1)} %bitcast.37, pred[]{:T(512)S(6)} %compare.7, f32[64,128,256]{2,1,0:T(8,128)S(1)} %fusion.70, f32[64]{0:T(128)S(1)} %dynamic_slice.65, s32[64]{0:T(128)S(1)} %dynamic_slice.66), kind=kOutput, calls=%fused_computation.21.clone.1 | convolution fusion | flops 1211111424 | bytes 20972032 | tf_op jit(solution)/shard_map/while/body/eval_jaxpr/ok,kaf->oaf/dot_general | solution.py:31
  488.4 7.9 %copy.23 = bf16[48,128,256]{2,1,0:T(8,128)(2,1)} copy(f32[48,128,256]{2,0,1:T(8,128)} %get-tuple-element.98) | data formatting | bytes 9437184 | tf_op jit(solution)/shard_map/while | solution.py:35
  497.3 62.8 %reduce-scatter.5.cloned.1.call-done = bf16[384,256]{1,0:T(8,128)(2,1)} async-done(((bf16[6144,256]{1,0:T(8,128)(2,1)}), bf16[384,256]{1,0:T(8,128)(2,1)}) %reduce-scatter.5.cloned.1.call-update) | async-done | bytes 196624 | tf_op jit(solution)/shard_map/reduce_scatter | solution.py:66
  561.9 142.1 %all-reduce.2.cloned.1.call-done = f32[128,256]{1,0:T(8,128)} async-done(((f32[128,256]{1,0:T(8,128)}), f32[128,256]{1,0:T(8,128)}) %all-reduce.2.cloned.1.call-update) | async-done | bytes 131088 | tf_op jit(solution)/shard_map/psum | solution.py:61
  (204 shorter events, 92.1 us)
Async XLA Ops:
  7.2 224.8 %copy-start = (bf16[128,256]{1,0:T(8,128)(2,1)S(1)}, bf16[128,256]{1,0:T(8,128)(2,1)}, u32[]{:S(2)}) copy-start(bf16[128,256]{1,0:T(8,128)(2,1)} %param.12) | copy-start | bytes 196612
  7.2 38.2 %all-gather.3.cloned.1.call-start = ((), (), s32[]{:S(2)}) async-start(), calls=%async_computation.2 | async-start | bytes 1671168 | tf_op jit(solution)/shard_map/all_gather | solution.py:49
  7.9 224.1 %reduce-scatter.3.cloned.1.call-start = ((), (), s32[]{:S(2)}) async-start(), calls=%async_computation.3 | async-start | bytes 1769472 | tf_op jit(solution)/shard_map/reduce_scatter | solution.py:53
  50.6 2.4 copy-start.2
  57.8 1.1 copy-start.3
  64.2 2.4 copy-start.2
  71.5 1.1 copy-start.3
  77.8 2.4 copy-start.2
  85.1 1.1 copy-start.3
  91.4 2.4 copy-start.2
  98.7 1.1 copy-start.3
  105.0 2.4 copy-start.2
  118.7 2.4 copy-start.2
  125.9 1.1 copy-start.3
  132.3 2.4 copy-start.2
  139.6 1.1 copy-start.3
  145.9 2.4 copy-start.2
  153.2 1.1 copy-start.3
  154.3 77.7 %copy-start.6 = (bf16[384,256]{1,0:T(8,128)(2,1)S(1)}, bf16[384,256]{1,0:T(8,128)(2,1)}, u32[]{:S(2)}) copy-start(bf16[384,256]{1,0:T(8,128)(2,1)} %param.17) | copy-start | bytes 589828
  157.3 127.0 %all-gather.5.cloned.1.call-start = ((), (), s32[]{:S(2)}) async-start(), calls=%async_computation.5 | async-start | bytes 1769472 | tf_op jit(solution)/shard_map/all_gather | solution.py:62
  234.1 326.1 %reduce-scatter.5.cloned.1.call-start = ((), (), s32[]{:S(2)}) async-start(), calls=%async_computation.6 | async-start | bytes 3342336 | tf_op jit(solution)/shard_map/reduce_scatter | solution.py:66
  287.1 8.7 %slice-start = ((s8[6291456]{0:T(1024)(128)(4,1)}), s8[2097152]{0:T(1024)(128)(4,1)S(1)}, s32[]{:S(2)}) async-start(s8[6291456]{0:T(1024)(128)(4,1)} %bitcast.36), calls=%async_computation.7 | async-start | bytes 4194304 | tf_op jit(solution)/shard_map/while
  291.5 4.3 slice-start.1
  307.1 2.7 copy-start.1
  312.6 8.7 %slice-start = ((s8[6291456]{0:T(1024)(128)(4,1)}), s8[2097152]{0:T(1024)(128)(4,1)S(1)}, s32[]{:S(2)}) async-start(s8[6291456]{0:T(1024)(128)(4,1)} %bitcast.36), calls=%async_computation.7 | async-start | bytes 4194304 | tf_op jit(solution)/shard_map/while
  317.1 4.3 slice-start.1
  332.7 2.7 copy-start.1
  338.2 8.7 %slice-start = ((s8[6291456]{0:T(1024)(128)(4,1)}), s8[2097152]{0:T(1024)(128)(4,1)S(1)}, s32[]{:S(2)}) async-start(s8[6291456]{0:T(1024)(128)(4,1)} %bitcast.36), calls=%async_computation.7 | async-start | bytes 4194304 | tf_op jit(solution)/shard_map/while
  342.6 4.3 slice-start.1
  358.2 2.7 copy-start.1
  363.7 8.7 %slice-start = ((s8[6291456]{0:T(1024)(128)(4,1)}), s8[2097152]{0:T(1024)(128)(4,1)S(1)}, s32[]{:S(2)}) async-start(s8[6291456]{0:T(1024)(128)(4,1)} %bitcast.36), calls=%async_computation.7 | async-start | bytes 4194304 | tf_op jit(solution)/shard_map/while
  368.1 4.3 slice-start.1
  383.7 2.7 copy-start.1
  389.2 8.7 %slice-start = ((s8[6291456]{0:T(1024)(128)(4,1)}), s8[2097152]{0:T(1024)(128)(4,1)S(1)}, s32[]{:S(2)}) async-start(s8[6291456]{0:T(1024)(128)(4,1)} %bitcast.36), calls=%async_computation.7 | async-start | bytes 4194304 | tf_op jit(solution)/shard_map/while
  393.6 4.3 slice-start.1
  409.2 2.7 copy-start.1
  414.7 8.7 %slice-start = ((s8[6291456]{0:T(1024)(128)(4,1)}), s8[2097152]{0:T(1024)(128)(4,1)S(1)}, s32[]{:S(2)}) async-start(s8[6291456]{0:T(1024)(128)(4,1)} %bitcast.36), calls=%async_computation.7 | async-start | bytes 4194304 | tf_op jit(solution)/shard_map/while
  419.1 4.3 slice-start.1
  434.7 2.7 copy-start.1
  440.2 8.7 %slice-start = ((s8[6291456]{0:T(1024)(128)(4,1)}), s8[2097152]{0:T(1024)(128)(4,1)S(1)}, s32[]{:S(2)}) async-start(s8[6291456]{0:T(1024)(128)(4,1)} %bitcast.36), calls=%async_computation.7 | async-start | bytes 4194304 | tf_op jit(solution)/shard_map/while
  444.6 4.3 slice-start.1
  460.2 2.7 copy-start.1
  465.7 8.7 %slice-start = ((s8[6291456]{0:T(1024)(128)(4,1)}), s8[2097152]{0:T(1024)(128)(4,1)S(1)}, s32[]{:S(2)}) async-start(s8[6291456]{0:T(1024)(128)(4,1)} %bitcast.36), calls=%async_computation.7 | async-start | bytes 4194304 | tf_op jit(solution)/shard_map/while
  470.2 4.3 slice-start.1
  485.8 2.7 copy-start.1
  488.4 8.0 %copy-start.4 = (bf16[384,256]{1,0:T(8,128)(2,1)S(1)}, bf16[384,256]{1,0:T(8,128)(2,1)}, u32[]{:S(2)}) copy-start(bf16[384,256]{1,0:T(8,128)(2,1)} %get-tuple-element.189) | copy-start | bytes 589828
  488.4 8.0 %copy-start.5 = (f32[384,128]{1,0:T(8,128)S(1)}, f32[384,128]{1,0:T(8,128)}, u32[]{:S(2)}) copy-start(f32[384,128]{1,0:T(8,128)} %reduce-scatter.3.cloned.1.call-done) | copy-start | bytes 589828
  496.4 207.7 %all-reduce.2.cloned.1.call-start = ((), (), s32[]{:S(2)}) async-start(), calls=%async_computation.4 | async-start | bytes 262144 | tf_op jit(solution)/shard_map/psum | solution.py:61
  (1 other events, 1.1 us)
Sparse Core Ops, SparseCore 0:
  9.7 35.5 all-gather.2
  157.4 74.5 reduce-scatter.2
  234.3 49.9 all-gather.4
  496.5 63.6 reduce-scatter.4
  565.3 138.6 all-reduce.1
where the time goes:
time: 714 us; the launch traced here: 712 us
  waiting for transfers between devices  367 us (51%)
  matrix products  187 us (26%)
  local copies, waits for them, and re-layouts  120 us (17%)
  between operations  14.5 us (2%)
  other arithmetic  12.3 us (2%)
  loops' own time  11.3 us (2%)
    psum x1, waiting for transfers between devices, local(): grad_weight = lax.psum(own_grad, ('row', 'col'))  142 us
    dot_general x16, matrix products, one_group(): jnp.einsum('ok,kaf->oaf', placing, prod, precision=lax.Precision.HIGHEST)  129 us
    reduce_scatter x1, waiting for transfers between devices, local(): lax.psum_scatter(partial_value, 'col', scatter_dimension=0, tiled=True)  74.6 us
    reduce_scatter x1, waiting for transfers between devices, local(): lax.psum_scatter(back.astype(jnp.bfloat16), 'row', scatter_dimension=0, t...  62.8 us
    gather x16, local copies, waits for them, and re-layouts, one_group(): sources[0][part_gather]  54.1 us
    dot_general x16, matrix products, one_group(): jnp.einsum(form, part_tiles, sources[0][part_gather], preferred_element_t...  53.4 us
    all_gather x1, waiting for transfers between devices, local(): delta_group = lax.all_gather(delta, 'col', axis=0, tiled=True)  50.1 us
    all_gather x1, waiting for transfers between devices, local(): gathered = lax.all_gather(features, 'row', axis=0, tiled=True)  36.7 us
  transfers between devices with their start and end apart: 5, of which 5 were waited for; matrix products, arithmetic and copies ran while one was open for 0% of the time, Pallas kernels for 0%

commit v1 on v0

v1 whole, which is shorter than its diff:
```python
import jax
import jax.numpy as jnp
from jax import lax
from jax.experimental import pallas as pl
from jax.experimental.pallas import tpu as pltpu
from jax.sharding import Mesh, PartitionSpec as P

AXES = ("zl", "x", "core", "zh", "y")
ROW = ("zl", "x", "core")
COL = ("zh", "y")
BS = 128
GROUP = 4
UNROLL = 4
CHUNK = 16
MIB = 1 << 20


def schedule(key, other, live, n_keys, zero_at):
    slots = key.shape[0]
    step = GROUP * UNROLL
    places = -(-(slots + n_keys * (GROUP - 1)) // step) * step
    k = jnp.arange(slots, dtype=jnp.int32)
    keys = jnp.arange(n_keys, dtype=jnp.int32)
    here = (key[None, :] == keys[:, None]) & live[None, :]
    count = jnp.sum(here.astype(jnp.int32), axis=1)
    padded = (count + GROUP - 1) // GROUP * GROUP
    start = jnp.sum(jnp.where(keys[None, :] < keys[:, None], padded[None, :], 0), axis=1)
    own_start = jnp.sum(jnp.where(here, start[:, None], 0), axis=0)
    before = (key[:, None] == key[None, :]) & live[None, :] & (k[None, :] < k[:, None])
    place = own_start + jnp.sum(before.astype(jnp.int32), axis=1)
    place = jnp.where(live, place, -1)
    hit = place[None, :] == jnp.arange(places, dtype=jnp.int32)[:, None]
    order = jnp.sum(jnp.where(hit, k[None, :], 0), axis=1)
    source = jnp.sum(jnp.where(hit, other[None, :] - zero_at, 0), axis=1) + zero_at
    first = jnp.arange(places // GROUP, dtype=jnp.int32)[:, None] * GROUP
    inside = (start[None, :] <= first) & (first < (start + padded)[None, :])
    target = jnp.sum(jnp.where(inside, keys[None, :], 0), axis=1)
    turns = (jnp.sum(padded) + step - 1) // step
    return order, source, target, turns.reshape(1)


def load_kernel(count, tiles, held, sem):
    chunks = (count[0] + CHUNK - 1) // CHUNK

    def copy(i):
        at = pl.ds(pl.multiple_of(i * CHUNK, CHUNK), CHUNK)
        return pltpu.make_async_copy(tiles.at[at], held.at[at], sem)

    @pl.loop(0, chunks)
    def _(i):
        copy(i).start()

    @pl.loop(0, chunks)
    def _(i):
        copy(i).wait()


def load_tiles(count, tiles):
    return pl.pallas_call(
        load_kernel,
        out_shape=pltpu.VMEM(tiles.shape, tiles.dtype),
        in_specs=[
            pl.BlockSpec(memory_space=pltpu.SMEM),
            pl.BlockSpec(memory_space=pl.ANY),
        ],
        out_specs=pl.BlockSpec(memory_space=pltpu.VMEM),
        scratch_shapes=[pltpu.SemaphoreType.DMA],
        compiler_params=pltpu.CompilerParams(vmem_limit_bytes=24 * MIB),
        cost_estimate=pl.CostEstimate(
            flops=0, bytes_accessed=tiles.size * 2, transcendentals=0
        ),
        name="load_tiles",
    )(count, tiles)


def forward_kernel(order, source, target, turns, tiles, own, sib, out, feats, total):
    half = own.shape[0]
    feats[0:half] = own[...]
    feats[half : 2 * half] = sib[...]
    feats[2 * half] = jnp.zeros((BS, BS), jnp.bfloat16)
    total[...] = jnp.zeros_like(total)

    @pl.loop(0, turns[0])
    def _(turn):
        for u in range(UNROLL):
            group = turn * UNROLL + u
            at = [group * GROUP + i for i in range(GROUP)]
            left = jnp.concatenate([tiles[order[p]] for p in at], axis=1)
            right = jnp.concatenate([feats[source[p]] for p in at], axis=0)
            total[target[group]] += jnp.dot(
                left, right, preferred_element_type=jnp.float32
            )

    out[...] = total[...].astype(jnp.bfloat16)


def backward_kernel(order, source, target, turns, tiles, grads, own, sib, held, total):
    rows = grads.shape[0]
    half = own.shape[0]
    held[0:rows] = grads[...]
    held[rows] = jnp.zeros((BS, BS), jnp.bfloat16)
    total[...] = jnp.zeros_like(total)

    @pl.loop(0, turns[0])
    def _(turn):
        for u in range(UNROLL):
            group = turn * UNROLL + u
            at = [group * GROUP + i for i in range(GROUP)]
            left = jnp.concatenate([held[source[p]] for p in at], axis=1)
            right = jnp.concatenate([tiles[order[p]] for p in at], axis=0)
            total[target[group]] += jnp.dot(
                left, right, preferred_element_type=jnp.float32
            )

    own[...] = total[0:half].astype(jnp.bfloat16)
    sib[...] = total[half : 2 * half].astype(jnp.bfloat16)


def smem():
    return pl.BlockSpec(memory_space=pltpu.SMEM)


def vmem():
    return pl.BlockSpec(memory_space=pltpu.VMEM)


def forward(plan, tiles, own, sib, row_blocks):
    half = own.shape[0]
    return pl.pallas_call(
        forward_kernel,
        out_shape=jax.ShapeDtypeStruct((row_blocks, BS, BS), jnp.bfloat16),
        in_specs=[smem()] * 4 + [vmem()] * 3,
        out_specs=vmem(),
        scratch_shapes=[
            pltpu.VMEM((2 * half + 1, BS, BS), jnp.bfloat16),
            pltpu.VMEM((row_blocks, BS, BS), jnp.float32),
        ],
        compiler_params=pltpu.CompilerParams(vmem_limit_bytes=30 * MIB),
        cost_estimate=pl.CostEstimate(
            flops=2 * tiles.size * BS, bytes_accessed=tiles.size * 2, transcendentals=0
        ),
        name="forward_tiles",
    )(*plan, tiles, own, sib)


def backward(plan, tiles, grads, col_blocks):
    half = col_blocks // 2
    shape = jax.ShapeDtypeStruct((half, BS, BS), jnp.bfloat16)
    return pl.pallas_call(
        backward_kernel,
        out_shape=(shape, shape),
        in_specs=[smem()] * 4 + [vmem()] * 2,
        out_specs=(vmem(), vmem()),
        scratch_shapes=[
            pltpu.VMEM((grads.shape[0] + 1, BS, BS), jnp.bfloat16),
            pltpu.VMEM((col_blocks, BS, BS), jnp.float32),
        ],
        compiler_params=pltpu.CompilerParams(vmem_limit_bytes=30 * MIB),
        cost_estimate=pl.CostEstimate(
            flops=2 * tiles.size * BS, bytes_accessed=tiles.size * 2, transcendentals=0
        ),
        name="backward_tiles",
    )(*plan, tiles, grads)


def middle_kernel(parts, weight, cot, hidden, back, grad):
    agg = jnp.sum(parts[...].astype(jnp.float32), axis=0).astype(jnp.bfloat16)
    w = weight[...]
    pre = jnp.dot(agg, w, preferred_element_type=jnp.float32)
    scale = 0.7978845608028654
    inner = scale * (pre + 0.044715 * (pre * pre * pre))
    t = jnp.tanh(inner)
    half = 0.5 * (1.0 + t)
    hidden[...] = (pre * half).astype(jnp.bfloat16)
    slope = half + 0.5 * pre * (1.0 - t * t) * (
        scale * (1.0 + (3 * 0.044715) * (pre * pre))
    )
    delta = (cot[...].astype(jnp.float32) * slope).astype(jnp.bfloat16)
    grad[...] = lax.dot_general(
        agg, delta, (((0,), (0,)), ((), ())), preferred_element_type=jnp.float32
    ).astype(jnp.bfloat16)
    for j in range(back.shape[0]):
        back[j] = lax.dot_general(
            w,
            delta[j * BS : (j + 1) * BS],
            (((1,), (1,)), ((), ())),
            preferred_element_type=jnp.float32,
        ).astype(jnp.bfloat16)


def middle(parts, weight, cot):
    nodes = cot.shape[0]
    f_in, f_hid = weight.shape
    return pl.pallas_call(
        middle_kernel,
        out_shape=(
            jax.ShapeDtypeStruct((nodes, f_hid), jnp.bfloat16),
            jax.ShapeDtypeStruct((nodes // BS, f_in, BS), jnp.bfloat16),
            jax.ShapeDtypeStruct((f_in, f_hid), jnp.bfloat16),
        ),
        in_specs=[vmem()] * 3,
        out_specs=(vmem(),) * 3,
        compiler_params=pltpu.CompilerParams(vmem_limit_bytes=30 * MIB),
        name="middle",
    )(parts, weight, cot)


def swap_core(value):
    return lax.ppermute(value, "core", [(0, 1), (1, 0)])


def local(features, weight, tile_values, tile_rows, tile_cols, tile_count, cotangent):
    f_in, f_hid = weight.shape
    own_blocks = features.shape[0] // BS
    n_row = lax.axis_size(ROW)
    n_col = lax.axis_size(COL)
    n_half = n_row // 2
    row_blocks = own_blocks * n_col
    col_blocks = own_blocks * n_row
    tiles = tile_values[0, 0]
    count = tile_count.reshape(1)
    rows = tile_rows[0, 0]
    cols = tile_cols[0, 0]
    live = jnp.arange(tiles.shape[0], dtype=jnp.int32) < count[0]
    owner = cols // own_blocks
    side = lax.rem(owner, 2) ^ lax.axis_index("core")
    place = (side * n_half + owner // 2) * own_blocks + cols % own_blocks

    own = lax.all_to_all(
        jnp.tile(features, (n_half, 1)), ("zl", "x"), 0, 0, tiled=True
    )
    held = load_tiles(count, tiles)
    plan_f = schedule(rows, place, live, row_blocks, col_blocks)
    plan_b = schedule(place, rows, live, col_blocks, row_blocks)
    sib = swap_core(own)
    shape = (col_blocks // 2, BS, f_in)
    part = forward(plan_f, held, own.reshape(shape), sib.reshape(shape), row_blocks)
    parts = lax.all_to_all(part.reshape(row_blocks * BS, f_in), COL, 0, 0, tiled=True)
    hidden, back, grad = middle(
        parts.reshape(n_col, own_blocks * BS, f_in), weight, cotangent
    )

    lines = f_in * f_hid // (n_col * BS)
    back = back.reshape(own_blocks * BS, BS)
    send = jnp.concatenate(
        [
            jnp.broadcast_to(back[None], (n_col,) + back.shape),
            grad.reshape(n_col, lines, BS),
        ],
        axis=1,
    )
    got = lax.all_to_all(send.reshape(-1, BS), COL, 0, 0, tiled=True)
    got = got.reshape(n_col, own_blocks * BS + lines, BS)
    grads = got[:, : own_blocks * BS].reshape(row_blocks, BS, BS)
    grad_part = jnp.sum(got[:, own_blocks * BS :].astype(jnp.float32), axis=0)
    grad_part = grad_part.astype(jnp.bfloat16)

    own_sum, sib_sum = backward(plan_b, held, grads, col_blocks)
    nodes = own_blocks * BS
    sent = jnp.concatenate([sib_sum.reshape(-1, BS), grad_part], axis=0)
    other = swap_core(sent)
    pair = own_sum.reshape(-1, BS).astype(jnp.float32) + other[: -lines].astype(jnp.float32)
    grad_pair = grad_part.astype(jnp.float32) + other[-lines:].astype(jnp.float32)
    send = jnp.concatenate(
        [
            pair.astype(jnp.bfloat16).reshape(n_half, nodes, BS),
            jnp.broadcast_to(
                grad_pair.astype(jnp.bfloat16)[None], (n_half, lines, BS)
            ),
        ],
        axis=1,
    )
    got = lax.all_to_all(send.reshape(-1, BS), ("zl", "x"), 0, 0, tiled=True)
    got = jnp.sum(got.reshape(n_half, nodes + lines, BS).astype(jnp.float32), axis=0)
    grad_features = got[:nodes].astype(jnp.bfloat16).reshape(own_blocks, f_in, BS)
    grad_features = jnp.swapaxes(grad_features, 1, 2).reshape(nodes, f_in)
    grad_col = got[nodes:]
    grad_weight = lax.all_to_all(
        jnp.tile(grad_col, (n_col, 1)), COL, 0, 0, tiled=True
    ).reshape(f_in, f_hid)
    return hidden, grad_weight, grad_features


def solution(mesh):
    fine = Mesh(mesh.devices.reshape(2, 4, 2, 2, 4), AXES)
    nodes = P(AXES, None)
    mapped = jax.shard_map(
        local,
        mesh=fine,
        in_specs=(
            nodes,
            P(),
            P(ROW, COL, None, None, None),
            P(ROW, COL, None),
            P(ROW, COL, None),
            P(ROW, COL),
            nodes,
        ),
        out_specs=(nodes, P(), nodes),
        check_vma=False,
    )
    return mapped
```

time: 714 us -> 126 us (0.18)
  waiting for transfers between devices: 367 us -> 34.2 us
  matrix products: 187 us -> 0 us
  local copies, waits for them, and re-layouts: 120 us -> 9.99 us
  blocking collectives: 0 us -> 35.6 us
  Pallas kernels: 0 us -> 21.8 us
  starting transfers between devices: 0.2 us -> 17.2 us
  between operations: 14.5 us -> 2.92 us
  loops' own time: 11.3 us -> 0 us
  other arithmetic: 12.3 us -> 4.99 us
    dot_general x35 -> x0, matrix products: 187 us -> none  [the longest x16 129 us: one_group(): jnp.einsum('ok,kaf->oaf', placing, prod, precision=lax.Precision.HIGHEST)]
    psum x1 -> x0, waiting for transfers between devices: 142 us -> none  [local(): grad_weight = lax.psum(own_grad, ('row', 'col'))]
    reduce_scatter x2 -> x0, waiting for transfers between devices: 137 us -> none  [the longest x1 74.6 us: local(): lax.psum_scatter(partial_value, 'col', scatter_dimension=0, tiled=True)]
    all_gather x2 -> x0, waiting for transfers between devices: 86.8 us -> none  [the longest x1 50.1 us: local(): delta_group = lax.all_gather(delta, 'col', axis=0, tiled=True)]
    gather x16 -> x0, local copies, waits for them, and re-layouts: 54.1 us -> none  [one_group(): sources[0][part_gather]]
    while x82 -> x0, local copies, waits for them, and re-layouts: 41.3 us -> none
    all_to_all x0 -> x2, blocking collectives: none -> 35.6 us  [the longest x1 20.1 us: local(): got = lax.all_to_all(send.reshape(-1, BS), ('zl', 'x'), 0, 0, tiled=True)]
    all_to_all x0 -> x3, waiting for transfers between devices: none -> 31.9 us  [the longest x1 14.4 us: local(): got = lax.all_to_all(send.reshape(-1, BS), COL, 0, 0, tiled=True)]
  transfers between devices with their start and end apart: 5 -> 5, of which waited for: 5 -> 4; matrix products, arithmetic and copies ran while one was open for 0% -> 3% of each run, Pallas kernels for 0% -> 3%
where the time goes in v1:
time: 126 us; the launch traced here: 127 us
  blocking collectives  35.6 us (28%)
  waiting for transfers between devices  34.2 us (27%)
  Pallas kernels  21.8 us (17%)
  starting transfers between devices  17.2 us (14%)
  local copies, waits for them, and re-layouts  9.99 us (8%)
  other arithmetic  4.99 us (4%)
  between operations  2.92 us (2%)
    all_to_all x1, blocking collectives, local(): got = lax.all_to_all(send.reshape(-1, BS), ('zl', 'x'), 0, 0, tiled=True)  20.1 us
    all_to_all x1, blocking collectives, local(): lax.all_to_all(part.reshape(row_blocks * BS, f_in), COL, 0, 0, tiled=True)  15.5 us
    all_to_all x1, waiting for transfers between devices, local(): got = lax.all_to_all(send.reshape(-1, BS), COL, 0, 0, tiled=True)  14.4 us
    all_to_all x1, waiting for transfers between devices, local(): lax.all_to_all(jnp.tile(features, (n_half, 1)), ('zl', 'x'), 0, 0, tiled=...  10.2 us
    pallas_call x1, Pallas kernels, backward(): pl.pallas_call(backward_kernel, out_shape=(shape, shape), in_specs=[smem(...  8.57 us
    pallas_call x1, Pallas kernels, forward(): pl.pallas_call(forward_kernel, out_shape=jax.ShapeDtypeStruct((row_blocks...  7.85 us
    all_to_all x1, starting transfers between devices, local(): lax.all_to_all(jnp.tile(grad_col, (n_col, 1)), COL, 0, 0, tiled=True)  7.84 us
    all_to_all x1, waiting for transfers between devices, local(): lax.all_to_all(jnp.tile(grad_col, (n_col, 1)), COL, 0, 0, tiled=True)  7.32 us
  transfers between devices with their start and end apart: 5, of which 4 were waited for; matrix products, arithmetic and copies ran while one was open for 3% of the time, Pallas kernels for 3%

profile of v1, /device:TPU:0, one launch (start us, length us, event | category | flops | bytes accessed | tf_op | source)
XLA Modules:
  0.0 126.8 jit_solution(12446867260430860950)
XLA Ops:
  0.6 0.0 copy-start.5
  0.6 0.0 copy-start.4
  0.7 1.9 %tile.4 = bf16[8,384,128]{2,1,0:T(8,128)(2,1)} broadcast(bf16[384,128]{1,0:T(8,128)(2,1)} %param.7), dimensions={1,2} | broadcast | bytes 884736 | tf_op jit(solution)/shard_map/tile | solution.py:230
  2.5 5.7 %all-to-all-start = ((bf16[8,384,128]{2,1,0:T(8,128)(2,1)}), bf16[8,384,128]{2,1,0:T(8,128)(2,1)S(1)}, u32[]{:S(2)}, u32[]{:S(2)}) async-start(bf16[8,384,128]{2,1,0:T(8,128)(2,1)} %tile.4), calls=%async_computation | async-start | bytes 1572864 | tf_op jit(solution)/shard_map/all_to_all | solution.py:229
  8.3 0.0 copy-done.5
  9.0 0.1 convert_reduce_fusion.4
  9.1 0.6 fusion.14
  9.8 0.1 select_reduce_fusion.9
  9.9 0.1 convert_reduce_fusion.3
  10.0 0.6 fusion.12
  10.7 0.1 select_reduce_fusion.7
  10.8 0.1 select_reduce_fusion.8.target
  10.9 0.1 select_reduce_fusion.4
  11.0 10.2 %all-to-all-done = bf16[8,384,128]{2,1,0:T(8,128)(2,1)S(1)} async-done(((bf16[8,384,128]{2,1,0:T(8,128)(2,1)}), bf16[8,384,128]{2,1,0:T(8,128)(2,1)S(1)}, u32[]{:S(2)}, u32[]{:S(2)}) %all-to-all-start) | async-done | bytes 786464 | tf_op jit(solution)/shard_map/all_to_all | solution.py:229
  21.2 0.0 collective-permute-start
  21.2 0.1 select_reduce_fusion.6
  21.9 4.3 %load_tiles.1.tiles = bf16[512,128,128]{2,1,0:T(8,128)(2,1)S(1)} custom-call(s32[1]{0:T(128)} %bitcast.25.count, bf16[512,128,128]{2,1,0:T(8,128)(2,1)} %bitcast.33), custom_call_target="tpu_custom_call" | custom-call | bytes 16777216 | tf_op jit(solution)/shard_map/load_tiles/pallas_call | solution.py:59
  26.3 0.4 convert_reduce_fusion.1
  26.7 0.4 select_reduce_fusion.2
  27.2 0.0 collective-permute-done
  27.2 7.9 %forward_tiles.1 = bf16[24,128,128]{2,1,0:T(8,128)(2,1)S(1)} custom-call(s32[592]{0:T(1024)S(1)} %get-tuple-element.16.order, s32[592]{0:T(1024)S(1)} %broadcast_add_fusion.1.source, s32[148]{0:T(256)S(1)} %select_reduce_fusion.8.target, s32[1]{0:T(128)} %bitcast.4.turns, bf16[512,128,128]{2,1,0:T(8,128)(2,1)S(1)} %load_tiles.1.tiles, ...), custom_call_target="tpu_custom_call" | custom-call | flops 2147483648 | bytes 16777216 | tf_op jit(solution)/shard_map/forward_tiles/pallas_call | solution.py:129
  35.0 0.0 copy-done
  35.0 0.0 copy-start.2
  35.1 0.0 copy-start.3
  35.1 15.5 %all_to_all.36.parts = bf16[8,384,128]{2,1,0:T(8,128)(2,1)S(1)} all-to-all(bf16[8,384,128]{2,1,0:T(8,128)(2,1)S(1)} %bitcast.29), channel_id=1, replica_groups=mesh['zl'=2,'x'=4,'core'=2,'zh'=2,'y'=4] {'zh','y'}, dimensions={0} | all-to-all | bytes 1572864 | tf_op jit(solution)/shard_map/all_to_all | solution.py:238
  50.6 0.0 copy-done.2
  50.6 1.1 middle.1
  51.7 0.1 broadcast_in_dim.182
  51.8 1.0 pad_maximum_fusion
  52.8 3.5 %all-to-all-start.2 = ((bf16[8,416,128]{2,1,0:T(8,128)(2,1)}), bf16[8,416,128]{2,1,0:T(8,128)(2,1)S(1)}, u32[]{:S(2)}, u32[]{:S(2)}) async-start(bf16[8,416,128]{2,1,0:T(8,128)(2,1)} %pad_maximum_fusion), calls=%async_computation.2 | async-start | bytes 1703936 | tf_op jit(solution)/shard_map/all_to_all | solution.py:252
  57.1 0.1 select_reduce_fusion.5.target
  57.2 0.4 select_reduce_fusion
  57.6 14.4 %all-to-all-done.2 = bf16[8,416,128]{2,1,0:T(8,128)(2,1)S(1)} async-done(((bf16[8,416,128]{2,1,0:T(8,128)(2,1)}), bf16[8,416,128]{2,1,0:T(8,128)(2,1)S(1)}, u32[]{:S(2)}, u32[]{:S(2)}) %all-to-all-start.2) | async-done | bytes 852000 | tf_op jit(solution)/shard_map/all_to_all | solution.py:252
  72.0 0.1 slice.25
  72.1 5.8 %copy-done.1 = bf16[512,128,128]{2,1,0:T(8,128)(2,1)S(1)} copy-done((bf16[512,128,128]{2,1,0:T(8,128)(2,1)S(1)}, bf16[512,128,128]{2,1,0:T(8,128)(2,1)}, u32[]{:S(2)}) %copy-start.1) | copy-done | bytes 16777240
  77.9 8.6 %backward_tiles.1 = (bf16[24,128,128]{2,1,0:T(8,128)(2,1)S(1)}, bf16[24,128,128]{2,1,0:T(8,128)(2,1)S(1)}) custom-call(s32[656]{0:T(1024)S(1)} %get-tuple-element.14.order, s32[656]{0:T(1024)S(1)} %broadcast_add_fusion.source, s32[164]{0:T(256)S(1)} %select_reduce_fusion.5.target, s32[1]{0:T(128)} %bitcast.11.turns, bf16[512,128,128]{2,1,0:T(8,128)(2,1)S(1)} %copy-done.1, ...), custom_call_target="tpu_custom_call" | custom-call | flops 2147483648 | bytes 16777216 | tf_op jit(solution)/shard_map/backward_tiles/pallas_call | solution.py:149
  86.5 0.1 pad_maximum_fusion.2
  86.5 0.1 collective-permute-start.1
  86.6 2.3 %collective-permute-done.1 = bf16[3104,128]{1,0:T(8,128)(2,1)S(1)} collective-permute-done((bf16[3104,128]{1,0:T(8,128)(2,1)S(1)}, bf16[3104,128]{1,0:T(8,128)(2,1)S(1)}, u32[]{:S(2)}, u32[]{:S(2)}) %collective-permute-start.1) | collective-permute-done | bytes 794656 | tf_op jit(solution)/shard_map/ppermute | solution.py:209
  88.9 0.3 fusion
  89.2 0.1 pad_maximum_fusion.1
  89.3 20.1 %all_to_all.37 = bf16[8,416,128]{2,1,0:T(8,128)(2,1)S(1)} all-to-all(bf16[8,416,128]{2,1,0:T(8,128)(2,1)S(1)} %pad_maximum_fusion.1), channel_id=1, replica_groups=mesh['zl'=2,'x'=4,'core'=2,'zh'=2,'y'=4] {'zl','x'}, dimensions={0} | all-to-all | bytes 1703936 | tf_op jit(solution)/shard_map/all_to_all | solution.py:273
  109.4 0.1 convert_reduce_fusion
  109.5 0.7 tile.5
  110.2 7.8 %all-to-all-start.4 = ((f32[8,32,128]{2,1,0:T(8,128)}), f32[8,32,128]{2,1,0:T(8,128)S(1)}, u32[]{:S(2)}, u32[]{:S(2)}) async-start(f32[8,32,128]{2,1,0:T(8,128)} %tile.5), calls=%async_computation.4 | async-start | bytes 262144 | tf_op jit(solution)/shard_map/all_to_all | solution.py:278
  118.0 0.8 copy.11
  118.8 7.3 %all-to-all-done.4 = f32[8,32,128]{2,1,0:T(8,128)S(1)} async-done(((f32[8,32,128]{2,1,0:T(8,128)}), f32[8,32,128]{2,1,0:T(8,128)S(1)}, u32[]{:S(2)}, u32[]{:S(2)}) %all-to-all-start.4) | async-done | bytes 131104 | tf_op jit(solution)/shard_map/all_to_all | solution.py:278
  126.1 0.7 reshape.281
  (22 shorter events, 0.2 us)
Async XLA Ops:
  0.6 7.6 %copy-start.5 = (s32[1,1,512]{2,1,0:T(1,128)S(1)}, s32[1,1,512]{2,1,0:T(1,128)}, u32[]{:S(2)}) copy-start(s32[1,1,512]{2,1,0:T(1,128)} %param.11) | copy-start | bytes 6148
  0.6 8.3 %copy-start.4 = (s32[1,1,512]{2,1,0:T(1,128)S(1)}, s32[1,1,512]{2,1,0:T(1,128)}, u32[]{:S(2)}) copy-start(s32[1,1,512]{2,1,0:T(1,128)} %param.10) | copy-start | bytes 6148
  2.5 18.6 %all-to-all-start = ((bf16[8,384,128]{2,1,0:T(8,128)(2,1)}), bf16[8,384,128]{2,1,0:T(8,128)(2,1)S(1)}, u32[]{:S(2)}, u32[]{:S(2)}) async-start(bf16[8,384,128]{2,1,0:T(8,128)(2,1)} %tile.4), calls=%async_computation | async-start | bytes 1572864 | tf_op jit(solution)/shard_map/all_to_all | solution.py:229
  21.2 6.0 %collective-permute-start = (bf16[3072,128]{1,0:T(8,128)(2,1)S(1)}, bf16[3072,128]{1,0:T(8,128)(2,1)S(1)}, u32[]{:S(2)}, u32[]{:S(2)}) collective-permute-start(bf16[3072,128]{1,0:T(8,128)(2,1)S(1)} %bitcast.27), channel_id=1, source_target_pairs={{0,8},{8,0},{1,9},{9,1},{2,10},{10,2},{3,11},{11,3},{4,12},{12,4},... | collective-permute-start | bytes 2359304 | tf_op jit(solution)/shard_map/ppermute | solution.py:209
  26.3 8.8 %copy-start = (bf16[512,128,128]{2,1,0:T(8,128)(2,1)}, bf16[512,128,128]{2,1,0:T(8,128)(2,1)S(1)}, u32[]{:S(2)}) copy-start(bf16[512,128,128]{2,1,0:T(8,128)(2,1)S(1)} %load_tiles.1.tiles) | copy-start | bytes 50331652
  35.0 15.5 %copy-start.2 = (bf16[384,256]{1,0:T(8,128)(2,1)S(1)}, bf16[384,256]{1,0:T(8,128)(2,1)}, u32[]{:S(2)}) copy-start(bf16[384,256]{1,0:T(8,128)(2,1)} %cot.1) | copy-start | bytes 589828
  35.1 15.5 %copy-start.3 = (bf16[128,256]{1,0:T(8,128)(2,1)S(1)}, bf16[128,256]{1,0:T(8,128)(2,1)}, u32[]{:S(2)}) copy-start(bf16[128,256]{1,0:T(8,128)(2,1)} %weight.1) | copy-start | bytes 196612
  52.8 19.2 %all-to-all-start.2 = ((bf16[8,416,128]{2,1,0:T(8,128)(2,1)}), bf16[8,416,128]{2,1,0:T(8,128)(2,1)S(1)}, u32[]{:S(2)}, u32[]{:S(2)}) async-start(bf16[8,416,128]{2,1,0:T(8,128)(2,1)} %pad_maximum_fusion), calls=%async_computation.2 | async-start | bytes 1703936 | tf_op jit(solution)/shard_map/all_to_all | solution.py:252
  72.1 5.8 %copy-start.1 = (bf16[512,128,128]{2,1,0:T(8,128)(2,1)S(1)}, bf16[512,128,128]{2,1,0:T(8,128)(2,1)}, u32[]{:S(2)}) copy-start(bf16[512,128,128]{2,1,0:T(8,128)(2,1)} %copy-done) | copy-start | bytes 50331652
  86.5 2.4 %collective-permute-start.1 = (bf16[3104,128]{1,0:T(8,128)(2,1)S(1)}, bf16[3104,128]{1,0:T(8,128)(2,1)S(1)}, u32[]{:S(2)}, u32[]{:S(2)}) collective-permute-start(bf16[3104,128]{1,0:T(8,128)(2,1)S(1)} %pad_maximum_fusion.2), channel_id=1, source_target_pairs={{0,8},{8,0},{1,9},{9,1},{2,10},{10,2},{3,11},{11,3},{4,12},{12,4},... | collective-permute-start | bytes 2383880 | tf_op jit(solution)/shard_map/ppermute | solution.py:209
  110.2 15.9 %all-to-all-start.4 = ((f32[8,32,128]{2,1,0:T(8,128)}), f32[8,32,128]{2,1,0:T(8,128)S(1)}, u32[]{:S(2)}, u32[]{:S(2)}) async-start(f32[8,32,128]{2,1,0:T(8,128)} %tile.5), calls=%async_computation.4 | async-start | bytes 262144 | tf_op jit(solution)/shard_map/all_to_all | solution.py:278

commit v2 on v0

v2 whole, which is shorter than its diff:
```python
import functools

import jax
import jax.numpy as jnp
from jax import lax
from jax.experimental import pallas as pl
from jax.experimental.pallas import tpu as pltpu
from jax.sharding import Mesh, PartitionSpec as P

AXES = ("zl", "x", "core", "zh", "y")
ROW = ("zl", "x", "core")
COL = ("zh", "y")
BS = 128
SHIFT = 10
FORWARD = (2, 32)
BACKWARD = (2, 32)
LIMIT = 24 << 20
CHUNK = 16
SMALL = pl.CostEstimate(flops=BS, bytes_accessed=BS, transcendentals=0)


def smem():
    return pl.BlockSpec(memory_space=pltpu.SMEM)


def vmem():
    return pl.BlockSpec(memory_space=pltpu.VMEM)


def hbm():
    return pl.BlockSpec(memory_space=pltpu.HBM)


def iota(shape, dim):
    return lax.broadcasted_iota(jnp.int32, shape, dim)


def places_of(slots, bounds, form):
    group, unroll = form
    groups = (slots + bounds[-1] * (group - 1)) // group
    groups += (len(bounds) - 1) * (unroll - 1)
    return -(-groups // 128) * 128 * group


def plan_size(places, form):
    return places + places // form[0] + 128


def places_in(plan, form):
    group, _ = form
    return (plan.shape[1] - 128) // (group + 1) * group


def make_plan(key, bounds, other, live, form, plan):
    group, unroll = form
    n_keys = bounds[-1]
    slots = key.shape[1]
    places = places_in(plan, form)
    targets = places // group
    here = (iota((n_keys, slots), 0) == key) & live
    marks = jnp.where(here, 1.0, 0.0)
    earlier = iota((slots, slots), 0) < iota((slots, slots), 1)
    rank = jnp.dot(
        marks.astype(jnp.bfloat16),
        jnp.where(earlier, 1.0, 0.0).astype(jnp.bfloat16),
        preferred_element_type=jnp.float32,
    )
    count = jnp.sum(marks, axis=1, keepdims=True).astype(jnp.int32)
    groups = lax.div(count + (group - 1), group)
    lower = iota((n_keys, n_keys), 1) < iota((n_keys, n_keys), 0)
    start = jnp.dot(
        jnp.where(lower, 1.0, 0.0).astype(jnp.bfloat16),
        jnp.broadcast_to(groups, (n_keys, 128)).astype(jnp.bfloat16),
        preferred_element_type=jnp.float32,
    )[:, :1].astype(jnp.int32)
    name = iota((n_keys, 1), 0)
    done = turns = jnp.zeros((1, 1), jnp.int32)
    ends = []
    for lo, hi in zip(bounds, bounds[1:]):
        inside = (name >= lo) & (name < hi)
        start = start + jnp.where(inside, turns * unroll - done, 0)
        here_now = jnp.sum(jnp.where(inside, groups, 0), axis=0, keepdims=True)
        done = done + here_now
        turns = turns + lax.div(here_now + (unroll - 1), unroll)
        ends.append(turns)
    place = jnp.where(here, rank.astype(jnp.int32) + start * group, 0)
    place = jnp.where(live, jnp.sum(place, axis=0, keepdims=True), -1)
    hit = iota((places, slots), 0) == place
    hit = jnp.where(hit, 1.0, 0.0).astype(jnp.bfloat16)
    row = iota((8, slots), 0)
    ids = iota((8, slots), 1) - slots
    low = ids & 127
    values = jnp.where(row == 1, ids - low, jnp.where(row == 2, other, 0))
    values = jnp.where(row == 0, low, values)
    found = lax.dot_general(
        values.astype(jnp.float32).astype(jnp.bfloat16),
        hit,
        (((1,), (1,)), ((), ())),
        preferred_element_type=jnp.float32,
    ).astype(jnp.int32)
    at = iota((n_keys, targets), 1)
    inside = (start <= at) & (at < start + groups)
    names = iota((n_keys, targets), 0)
    base = jnp.zeros_like(names)
    for lo in bounds[1:-1]:
        base = jnp.where(names >= lo, lo, base)
    names = names - base
    tile = found[0:1] + found[1:2] + slots
    plan[0:1, 0:places] = tile + (found[2:3] << SHIFT)
    plan[0:1, places : places + targets] = jnp.sum(
        jnp.where(inside, names, 0), axis=0, keepdims=True
    )
    lane = iota((1, 128), 1)
    last = jnp.zeros((1, 128), jnp.int32)
    for n, end in enumerate(ends):
        last = jnp.where(lane == n + 1, end, last)
    plan[0:1, places + targets :] = last


def divided(value, by, most):
    return sum(jnp.where(value >= by * t, 1, 0) for t in range(1, most // by + 1))


def plan_kernel(
    sizes, where, count, rows, cols, tiles, plan_f, plan_b, held, row_in, col_in, sem
):
    lo, hi = chunks_of(count, tiles, 0)

    copies = [
        pltpu.make_async_copy(rows, row_in, sem.at[0]),
        pltpu.make_async_copy(cols, col_in, sem.at[1]),
    ]
    for copy in copies:
        copy.start()

    @pl.loop(lo, hi)
    def _(i):
        chunk_copy(tiles, held, sem.at[2], i).start()

    held[tiles.shape[0]] = jnp.zeros((BS, BS), jnp.bfloat16)
    for copy in copies:
        copy.wait()
    own_blocks, row_blocks, col_blocks = sizes
    core, x, zl, y, zh = [where[i] for i in range(5)]
    row, col = row_in[...], col_in[...]
    live = iota(row.shape, 1) < count[0, 0]
    owner = divided(col, own_blocks, col_blocks - 1)
    inner = col - owner * own_blocks
    side = (owner & 1) ^ core
    half = col_blocks // 2
    owner = owner >> 1
    turned = ((owner >> 2) ^ zl) * 4 + ((x - (owner & 3)) & 3)
    spot = side * half + turned * own_blocks + inner
    dest = (1 - side) * half + owner * own_blocks + inner

    owner = divided(row, own_blocks, row_blocks - 1)
    inner = row - owner * own_blocks
    inner = inner + ((owner >> 2) ^ zh) * own_blocks
    each = row_blocks // 4
    later = jnp.where(iota(row.shape, 1) >= row.shape[1] // 2, 2, 0)
    ahead = ((owner & 3) - y) & 3
    turn = jnp.where(ahead == 2, later, jnp.where(ahead == 1, later + 1, 4))
    key = jnp.where(ahead == 0, 5, turn) * each + inner
    make_plan(key, forward_bounds(sizes), spot, live, FORWARD, plan_f)
    behind = (y - (owner & 3)) & 3
    spot = (behind & 1) * each + inner
    key = dest + jnp.where(behind >= 2, col_blocks, 0)
    make_plan(key, backward_bounds(sizes), spot, live, BACKWARD, plan_b)

    @pl.loop(lo, hi)
    def _(i):
        chunk_copy(tiles, held, sem.at[2], i).wait()


def forward_bounds(sizes):
    each = sizes[1] // 4
    return (0, 2 * each, 4 * each, 5 * each, 6 * each)


def backward_bounds(sizes):
    columns = sizes[2]
    return (0, columns, columns + columns // 2, 2 * columns)


def make_plans(sizes, where, count, rows, cols, tiles):
    slots = rows.shape[1]
    places_f = places_of(slots, forward_bounds(sizes), FORWARD)
    places_b = places_of(slots, backward_bounds(sizes), BACKWARD)
    return pl.pallas_call(
        functools.partial(plan_kernel, sizes),
        out_shape=(
            jax.ShapeDtypeStruct((1, plan_size(places_f, FORWARD)), jnp.int32),
            jax.ShapeDtypeStruct((1, plan_size(places_b, BACKWARD)), jnp.int32),
            pltpu.VMEM((tiles.shape[0] + 1, BS, BS), tiles.dtype),
        ),
        in_specs=[smem()] * 2 + [hbm()] * 3,
        out_specs=(vmem(),) * 3,
        scratch_shapes=[pltpu.VMEM(rows.shape, jnp.int32)] * 2
        + [pltpu.SemaphoreType.DMA((3,))],
        compiler_params=pltpu.CompilerParams(vmem_limit_bytes=LIMIT),
        cost_estimate=pl.CostEstimate(
            flops=0, bytes_accessed=tiles.size, transcendentals=0
        ),
        name="make_plans",
    )(where, count, rows, cols, tiles)


def chunks_of(count, tiles, part):
    most = tiles.shape[0] // CHUNK // 2
    live = lax.div(count[0, 0] + (CHUNK - 1), CHUNK)
    return part * most, jnp.minimum(live, (part + 1) * most)


def chunk_copy(tiles, held, sem, i):
    at = pl.ds(pl.multiple_of(i * CHUNK, CHUNK), CHUNK)
    return pltpu.make_async_copy(tiles.at[at], held.at[at], sem)


def multiply(plan, phases, form, tiles, source, tile_first, total):
    group, unroll = form
    places = places_in(plan, form)
    targets = places // group
    lo, hi = [plan[0, places + targets + phase] for phase in phases]

    @pl.loop(lo, hi)
    def _(turn):
        for u in range(unroll):
            at = turn * unroll + u
            spots = [plan[0, at * group + i] for i in range(group)]
            left = [tiles[spot & ((1 << SHIFT) - 1)] for spot in spots]
            right = [source[spot >> SHIFT] for spot in spots]
            if not tile_first:
                left, right = right, left
            total[plan[0, places + at]] += jnp.dot(
                jnp.concatenate(left, axis=1),
                jnp.concatenate(right, axis=0),
                preferred_element_type=jnp.float32,
            )


def forward_first_kernel(plan, count, tiles, _, *refs):
    blocks, (out, after, held, feats, total, sem) = refs[:-6], refs[-6:]
    lo, hi = chunks_of(count, tiles, 1)

    @pl.loop(lo, hi)
    def _(i):
        chunk_copy(tiles, held, sem, i).start()

    each = blocks[0].shape[0]
    for n, block in enumerate(blocks):
        feats[n * each : (n + 1) * each] = block[...]
    total[...] = jnp.zeros_like(total)

    multiply(plan, (0, 1), FORWARD, held, feats, True, total)

    @pl.loop(lo, hi)
    def _(i):
        chunk_copy(tiles, held, sem, i).wait()

    multiply(plan, (1, 2), FORWARD, held, feats, True, total)
    half = out.shape[0]
    out[...] = total[0:half].astype(jnp.bfloat16)
    after[...] = total[half : 2 * half].astype(jnp.bfloat16)


def forward_next_kernel(phase, plan, held, feats, out, *scratch):
    total = scratch[0] if scratch else out
    total[...] = jnp.zeros_like(total)
    multiply(plan, (phase, phase + 1), FORWARD, held, feats, True, total)
    if scratch:
        out[...] = total[...].astype(jnp.bfloat16)


def put_sources(source, first, second):
    each = source.shape[0] // 2
    source[0:each] = first[0:each]
    source[each : 2 * each] = second[0:each]


def backward_near_kernel(plan, held, first, second, total, source):
    put_sources(source, first, second)
    total[...] = jnp.zeros_like(total)
    multiply(plan, (0, 1), BACKWARD, held, source, False, total)


def backward_sib_kernel(plan, held, first, second, before, near, next_, out, both, source, total):
    put_sources(source, first, second)
    each = source.shape[0] // 2
    parts = [block[each:].astype(jnp.float32) for block in (near, next_, first, second)]
    both[...] = sum(parts).astype(jnp.bfloat16)
    total[...] = before[0 : total.shape[0]]
    multiply(plan, (1, 2), BACKWARD, held, source, False, total)
    out[...] = total[...].astype(jnp.bfloat16)


def backward_own_kernel(plan, held, first, second, before, out, source, total):
    put_sources(source, first, second)
    half = total.shape[0]
    total[...] = before[half : 2 * half]
    multiply(plan, (2, 3), BACKWARD, held, source, False, total)
    out[...] = total[...].astype(jnp.bfloat16)


def add_kernel(total, first, second, third, keep, send):
    parts = [part[...].astype(jnp.float32) for part in (first, second, third)]
    total = total[...] + sum(parts)
    each = keep.shape[0]
    keep[...] = total[0:each]
    send[...] = total[each : 2 * each].astype(jnp.bfloat16)


def collect_kernel(own, other, send):
    each = send.shape[0] - own.shape[0]
    send[0:each] = own[0:each]
    send[each : 2 * each] = other[0:each]
    grad = own[each:].astype(jnp.float32) + other[each:].astype(jnp.float32)
    send[2 * each :] = grad.astype(jnp.bfloat16)


def kernel_call(kernel, name, outs, n_smem, *args, scratch=(), aliases={}, in_hbm=()):
    specs = [smem() if n < n_smem else vmem() for n in range(len(args))]
    specs = [hbm() if n in in_hbm else spec for n, spec in enumerate(specs)]
    return pl.pallas_call(
        kernel,
        out_shape=tuple(outs),
        in_specs=specs,
        out_specs=(vmem(),) * len(outs),
        scratch_shapes=list(scratch),
        input_output_aliases=aliases,
        compiler_params=pltpu.CompilerParams(vmem_limit_bytes=LIMIT),
        cost_estimate=SMALL,
        name=name,
    )(*args)


def of_blocks(n, dtype=jnp.bfloat16):
    return jax.ShapeDtypeStruct((n, BS, BS), dtype)


def sums(n):
    return pltpu.VMEM((n, BS, BS), jnp.float32)


def middle_kernel(weight, cot, *refs):
    parts, (hidden, send) = refs[:-2], refs[-2:]
    agg = sum(part[...].astype(jnp.float32) for part in parts).astype(jnp.bfloat16)
    w = weight[...]
    pre = jnp.dot(agg, w, preferred_element_type=jnp.float32)
    scale = 0.7978845608028654
    inner = scale * (pre + 0.044715 * (pre * pre * pre))
    t = jnp.tanh(inner)
    half = 0.5 * (1.0 + t)
    hidden[...] = (pre * half).astype(jnp.bfloat16)
    slope = half + 0.5 * pre * (1.0 - t * t) * (
        scale * (1.0 + (3 * 0.044715) * (pre * pre))
    )
    delta = (cot[...].astype(jnp.float32) * slope).astype(jnp.bfloat16)
    grad = lax.dot_general(
        agg, delta, (((0,), (0,)), ((), ())), preferred_element_type=jnp.float32
    ).astype(jnp.bfloat16)
    each = agg.shape[0] // BS
    for j in range(each):
        send[j] = lax.dot_general(
            w,
            delta[j * BS : (j + 1) * BS],
            (((1,), (1,)), ((), ())),
            preferred_element_type=jnp.float32,
        ).astype(jnp.bfloat16)
    for i in range(grad.shape[1] // BS):
        send[each + i] = grad[:, i * BS : (i + 1) * BS]


def pair_kernel(own, sib, grad, other_grad, send):
    n_half, lines, _ = send.shape
    each = own.shape[0] // n_half
    both = grad[...].astype(jnp.float32) + other_grad[...].astype(jnp.float32)
    both = both.astype(jnp.bfloat16).reshape(-1, BS)
    for n in range(n_half):
        for j in range(each):
            at = n * each + j
            total = own[at].astype(jnp.float32) + sib[at].astype(jnp.float32)
            send[n, j * BS : (j + 1) * BS] = total.astype(jnp.bfloat16)
        send[n, each * BS : lines] = both


def pair(own, sib, grad, other_grad, n_half):
    lines = (own.shape[0] // n_half + grad.shape[0]) * BS
    return pl.pallas_call(
        pair_kernel,
        out_shape=jax.ShapeDtypeStruct((n_half, lines, BS), jnp.bfloat16),
        in_specs=[vmem()] * 4,
        out_specs=vmem(),
        compiler_params=pltpu.CompilerParams(vmem_limit_bytes=LIMIT),
        name="pair",
    )(own, sib, grad, other_grad)


def last_kernel(got, grad_features, grad_weight):
    nodes = grad_features.shape[0]
    total = jnp.sum(got[...].astype(jnp.float32), axis=0)
    for j in range(nodes // BS):
        at = slice(j * BS, (j + 1) * BS)
        grad_features[at] = total[at].T.astype(jnp.bfloat16)
    rows = grad_weight.shape[0]
    for i in range(grad_weight.shape[1] // BS):
        at = slice(nodes + i * rows, nodes + (i + 1) * rows)
        grad_weight[:, i * BS : (i + 1) * BS] = total[at]


def last(got, nodes, f_in, f_hid):
    return pl.pallas_call(
        last_kernel,
        out_shape=(
            jax.ShapeDtypeStruct((nodes, f_in), jnp.bfloat16),
            jax.ShapeDtypeStruct((f_in, f_hid), jnp.float32),
        ),
        in_specs=[vmem()],
        out_specs=(vmem(),) * 2,
        compiler_params=pltpu.CompilerParams(vmem_limit_bytes=LIMIT),
        name="last",
    )(got)


def swap_core(value):
    return lax.ppermute(value, "core", [(0, 1), (1, 0)])


def shift(value, axis, by):
    n = lax.axis_size(axis)
    return lax.ppermute(value, axis, [(i, (i + by) % n) for i in range(n)])


def local(features, weight, tile_values, tile_rows, tile_cols, tile_count, cotangent):
    f_in, f_hid = weight.shape
    nodes = features.shape[0]
    own_blocks = nodes // BS
    n_x, n_zl = lax.axis_size("x"), lax.axis_size("zl")
    n_col = lax.axis_size(COL)
    n_half = n_x * n_zl
    row_blocks = own_blocks * n_col
    col_blocks = own_blocks * n_half * 2
    tiles = pltpu.with_memory_space_constraint(tile_values[0, 0], pltpu.HBM)
    sent_blocks = own_blocks + f_in * f_hid // (BS * BS)
    sizes = (own_blocks, row_blocks, col_blocks)
    rows = pltpu.with_memory_space_constraint(tile_rows[0], pltpu.HBM)
    cols = pltpu.with_memory_space_constraint(tile_cols[0], pltpu.HBM)
    where = jnp.stack([lax.axis_index(a) for a in ("core", "x", "zl", "y", "zh")])

    near = [features] + [shift(features, "x", by) for by in range(1, n_x)]
    far = [shift(features, "zl", 1)]
    plan_f, plan_b, held = make_plans(sizes, where, tile_count, rows, cols, tiles)
    near, far, held = lax.optimization_barrier((near, far, held))
    far += [shift(near[1], "zl", 1), shift(far[0], "x", 2), shift(near[3], "zl", 1)]
    other = [swap_core(block) for block in near + far]
    blocks = [b.reshape(own_blocks, BS, f_in) for b in near + far + other]

    each = row_blocks // 4
    first, second, held, feats = kernel_call(
        forward_first_kernel,
        "forward_first",
        [
            of_blocks(each),
            of_blocks(each),
            pltpu.VMEM(held.shape, held.dtype),
            of_blocks(col_blocks),
        ],
        2,
        plan_f,
        tile_count,
        tiles,
        held,
        *blocks,
        scratch=[sums(2 * each), pltpu.SemaphoreType.DMA],
        aliases={3: 2},
        in_hbm=(2,),
    )
    got = [shift(first, "y", 2), shift(second, "y", 1)]
    (third,) = kernel_call(
        functools.partial(forward_next_kernel, 2),
        "forward_next",
        [of_blocks(each)],
        1,
        plan_f,
        held,
        feats,
        scratch=[sums(each)],
    )
    got.append(shift(third, "y", 3))
    held, feats, third = lax.optimization_barrier((held, feats, third))
    (total,) = kernel_call(
        functools.partial(forward_next_kernel, 3),
        "forward_here",
        [of_blocks(each, jnp.float32)],
        1,
        plan_f,
        held,
        feats,
    )
    keep, send = kernel_call(
        add_kernel,
        "add",
        [of_blocks(own_blocks, jnp.float32), of_blocks(own_blocks)],
        0,
        total,
        *got,
    )
    parts = [part.reshape(nodes, f_in) for part in (keep, shift(send, "zh", 1))]
    hidden, send = kernel_call(
        middle_kernel,
        "middle",
        [
            jax.ShapeDtypeStruct((nodes, f_hid), jnp.bfloat16),
            of_blocks(sent_blocks),
        ],
        0,
        weight,
        cotangent,
        *parts,
    )

    (send,) = kernel_call(
        collect_kernel,
        "collect",
        [of_blocks(sent_blocks + own_blocks)],
        0,
        send,
        shift(send, "zh", 1),
    )
    near = [send] + [shift(send, "y", by) for by in (1, 2, 3)]
    (total,) = kernel_call(
        backward_near_kernel,
        "backward_near",
        [of_blocks(col_blocks, jnp.float32)],
        1,
        plan_b,
        held,
        *near[:2],
        scratch=[pltpu.VMEM((2 * each, BS, BS), jnp.bfloat16)],
    )
    half = col_blocks // 2
    sib, grad = kernel_call(
        backward_sib_kernel,
        "backward_sib",
        [of_blocks(half), of_blocks(sent_blocks - own_blocks)],
        1,
        plan_b,
        held,
        *near[2:],
        total,
        *near[:2],
        scratch=[pltpu.VMEM((2 * each, BS, BS), jnp.bfloat16), sums(half)],
    )
    other_sib, other_grad = swap_core(sib), swap_core(grad)
    (own,) = kernel_call(
        backward_own_kernel,
        "backward_own",
        [of_blocks(half)],
        1,
        plan_b,
        held,
        *near[2:],
        total,
        scratch=[pltpu.VMEM((2 * each, BS, BS), jnp.bfloat16), sums(half)],
    )
    other_sib, other_grad, own = lax.optimization_barrier((other_sib, other_grad, own))
    send = pair(own, other_sib, grad, other_grad, n_half)
    got = lax.all_to_all(send.reshape(-1, BS), ("zl", "x"), 0, 0, tiled=True)
    grad_features, grad_weight = last(got.reshape(send.shape), nodes, f_in, f_hid)
    return hidden, grad_weight, grad_features


def solution(mesh):
    fine = Mesh(mesh.devices.reshape(2, 4, 2, 2, 4), AXES)
    nodes = P(AXES, None)
    mapped = jax.shard_map(
        local,
        mesh=fine,
        in_specs=(
            nodes,
            P(),
            P(ROW, COL, None, None, None),
            P(ROW, COL, None),
            P(ROW, COL, None),
            P(ROW, COL),
            nodes,
        ),
        out_specs=(nodes, P(), nodes),
        check_vma=False,
    )
    return mapped
```

time: 714 us -> 103 us (0.14)
  waiting for transfers between devices: 367 us -> 27.3 us
  matrix products: 187 us -> 0 us
  local copies, waits for them, and re-layouts: 120 us -> 0.1 us
  starting transfers between devices: 0.2 us -> 31.9 us
  blocking collectives: 0 us -> 26 us
  Pallas kernels: 0 us -> 14.5 us
  between operations: 14.5 us -> 1.43 us
  other arithmetic: 12.3 us -> 0 us
  loops' own time: 11.3 us -> 0 us
    dot_general x35 -> x0, matrix products: 187 us -> none  [the longest x16 129 us: one_group(): jnp.einsum('ok,kaf->oaf', placing, prod, precision=lax.Precision.HIGHEST)]
    psum x1 -> x0, waiting for transfers between devices: 142 us -> none  [local(): grad_weight = lax.psum(own_grad, ('row', 'col'))]
    reduce_scatter x2 -> x0, waiting for transfers between devices: 137 us -> none  [the longest x1 74.6 us: local(): lax.psum_scatter(partial_value, 'col', scatter_dimension=0, tiled=True)]
    all_gather x2 -> x0, waiting for transfers between devices: 86.8 us -> none  [the longest x1 50.1 us: local(): delta_group = lax.all_gather(delta, 'col', axis=0, tiled=True)]
    gather x16 -> x0, local copies, waits for them, and re-layouts: 54.1 us -> none  [one_group(): sources[0][part_gather]]
    while x82 -> x0, local copies, waits for them, and re-layouts: 41.3 us -> none
    ppermute x0 -> x25, starting transfers between devices: none -> 31.9 us  [the longest x15 30.2 us: shift(): return lax.ppermute(value, axis, [(i, (i + by) % n) for i in range(n)])]
    ppermute x0 -> x25, waiting for transfers between devices: none -> 27.3 us  [the longest x15 25.8 us: shift(): return lax.ppermute(value, axis, [(i, (i + by) % n) for i in range(n)])]
  transfers between devices with their start and end apart: 5 -> 25, of which waited for: 5 -> 13; matrix products, arithmetic and copies ran while one was open for 0% -> 0% of each run, Pallas kernels for 0% -> 7%
where the time goes in v2:
time: 103 us; the launch traced here: 101 us
  starting transfers between devices  31.9 us (31%)
  waiting for transfers between devices  27.3 us (27%)
  blocking collectives  26 us (25%)
  Pallas kernels  14.5 us (14%)
  between operations  1.43 us (1%)
    ppermute x15, starting transfers between devices, shift(): return lax.ppermute(value, axis, [(i, (i + by) % n) for i in range(n)])  30.2 us
    all_to_all x1, blocking collectives, local(): got = lax.all_to_all(send.reshape(-1, BS), ('zl', 'x'), 0, 0, tiled=True)  26 us
    ppermute x15, waiting for transfers between devices, shift(): return lax.ppermute(value, axis, [(i, (i + by) % n) for i in range(n)])  25.8 us
    pallas_call x9, Pallas kernels, kernel_call(): pl.pallas_call(kernel, out_shape=tuple(outs), in_specs=specs, out_specs=(...  10.7 us
    pallas_call x1, Pallas kernels, make_plans(): pl.pallas_call(functools.partial(plan_kernel, sizes), out_shape=(jax.Shap...  2.7 us
  transfers between devices with their start and end apart: 25, of which 13 were waited for; matrix products, arithmetic and copies ran while one was open for 0% of the time, Pallas kernels for 7%

profile of v2, /device:TPU:0, one launch (start us, length us, event | category | flops | bytes accessed | tf_op | source)
XLA Modules:
  0.0 101.2 jit_solution(14256653975647319060)
XLA Ops:
  0.6 2.9 %collective-permute-start.2 = (bf16[384,128]{1,0:T(8,128)(2,1)}, bf16[384,128]{1,0:T(8,128)(2,1)S(1)}, u32[]{:S(2)}, u32[]{:S(2)}) collective-permute-start(bf16[384,128]{1,0:T(8,128)(2,1)} %param.7), channel_id=1, source_target_pairs={{0,48},{16,0},{32,16},{48,32},{1,49},{17,1},{33,17},{49,33},{2,50}... | collective-permute-start | bytes 294920 | tf_op jit(solution)/shard_map/ppermute | solution.py:430
  3.5 0.8 collective-permute-start.1
  4.3 0.9 collective-permute-start
  5.2 1.9 %collective-permute-start.3 = (bf16[384,128]{1,0:T(8,128)(2,1)}, bf16[384,128]{1,0:T(8,128)(2,1)S(1)}, u32[]{:S(2)}, u32[]{:S(2)}) collective-permute-start(bf16[384,128]{1,0:T(8,128)(2,1)} %param.7), channel_id=1, source_target_pairs={{0,64},{64,0},{1,65},{65,1},{2,66},{66,2},{3,67},{67,3},{4,68},{68... | collective-permute-start | bytes 294920 | tf_op jit(solution)/shard_map/ppermute | solution.py:430
  7.8 0.1 stack.23.where
  7.9 2.7 %make_plans.1 = (s32[1,1664]{1,0:T(1,128)S(1)}, s32[1,1664]{1,0:T(1,128)S(1)}, bf16[513,128,128]{2,1,0:T(8,128)(2,1)S(1)}) custom-call(s32[5]{0:T(128)S(1)} %stack.23.where, s32[1,1]{1,0:T(1,128)S(6)} %copy.12.count, s32[1,512]{1,0:T(1,128)} %bitcast.46, s32[1,512]{1,0:T(1,128)} %bitcast.47, bf16[512,128,128]{2,1,0:T(8,128)(2,1)} %bitcast.44), custom_call_target="tpu_custom_call" | custom-call | bytes 8388608 | tf_op jit(solution)/shard_map/make_plans/pallas_call | solution.py:189
  10.6 1.0 collective-permute-done
  11.6 0.0 collective-permute-done.3
  11.6 0.5 collective-permute-start.9
  12.1 0.1 collective-permute-start.8
  12.2 1.9 %collective-permute-start.4 = (bf16[384,128]{1,0:T(8,128)(2,1)S(1)}, bf16[384,128]{1,0:T(8,128)(2,1)S(1)}, u32[]{:S(2)}, u32[]{:S(2)}) collective-permute-start(bf16[384,128]{1,0:T(8,128)(2,1)S(1)} %collective-permute-done), channel_id=1, source_target_pairs={{0,64},{64,0},{1,65},{65,1},{2,66},{66,2},{3,67},{67,3},{4,68},{68... | collective-permute-start | bytes 294920 | tf_op jit(solution)/shard_map/ppermute | solution.py:430
  14.1 0.1 collective-permute-start.6
  14.3 1.0 collective-permute-start.5
  15.2 0.0 collective-permute-done.9
  15.2 0.5 collective-permute-start.11
  15.7 2.1 %collective-permute-done.4 = bf16[384,128]{1,0:T(8,128)(2,1)S(1)} collective-permute-done((bf16[384,128]{1,0:T(8,128)(2,1)S(1)}, bf16[384,128]{1,0:T(8,128)(2,1)S(1)}, u32[]{:S(2)}, u32[]{:S(2)}) %collective-permute-start.4) | collective-permute-done | bytes 98336 | tf_op jit(solution)/shard_map/ppermute | solution.py:430
  17.8 1.8 %collective-permute-done.6 = bf16[384,128]{1,0:T(8,128)(2,1)S(1)} collective-permute-done((bf16[384,128]{1,0:T(8,128)(2,1)S(1)}, bf16[384,128]{1,0:T(8,128)(2,1)S(1)}, u32[]{:S(2)}, u32[]{:S(2)}) %collective-permute-start.6) | collective-permute-done | bytes 98336 | tf_op jit(solution)/shard_map/ppermute | solution.py:430
  19.6 0.9 collective-permute-done.5
  20.5 0.4 collective-permute-done.14
  20.9 0.9 collective-permute-done.13
  21.8 1.6 %forward_first.1 = (bf16[6,128,128]{2,1,0:T(8,128)(2,1)S(1)}, bf16[6,128,128]{2,1,0:T(8,128)(2,1)S(1)}, bf16[513,128,128]{2,1,0:T(8,128)(2,1)S(1)}, bf16[48,128,128]{2,1,0:T(8,128)(2,1)S(1)}) custom-call(s32[1,1664]{1,0:T(1,128)S(1)} %get-tuple-element.29.plan, s32[1,1]{1,0:T(1,128)S(6)} %copy.12.count, ...), custom_call_target="tpu_custom_call", output_to_operand_aliasing={{2}: (3, {})} | custom-call | flops 128 | bytes 128 | tf_op jit(solution)/shard_map/forward_first/pallas_call | solution.py:323
  23.5 1.5 %forward_next.1 = bf16[6,128,128]{2,1,0:T(8,128)(2,1)S(1)} custom-call(s32[1,1664]{1,0:T(1,128)S(1)} %get-tuple-element.29.plan, bf16[513,128,128]{2,1,0:T(8,128)(2,1)S(1)} %get-tuple-element.39.held, bf16[48,128,128]{2,1,0:T(8,128)(2,1)S(1)} %get-tuple-element.40.feats), custom_call_target="tpu_custom_call" | custom-call | flops 128 | bytes 128 | tf_op jit(solution)/shard_map/forward_next/pallas_call | solution.py:323
  25.0 3.1 %collective-permute-start.17 = (bf16[6,128,128]{2,1,0:T(8,128)(2,1)S(1)}, bf16[6,128,128]{2,1,0:T(8,128)(2,1)S(1)}, u32[]{:S(2)}, u32[]{:S(2)}) collective-permute-start(bf16[6,128,128]{2,1,0:T(8,128)(2,1)S(1)} %forward_next.1), channel_id=1, source_target_pairs={{0,3},{1,0},{2,1},{3,2},{4,7},{5,4},{6,5},{7,6},{8,11},{9,8},{10,9... | collective-permute-start | bytes 589832 | tf_op jit(solution)/shard_map/ppermute | solution.py:430
  28.0 4.8 %collective-permute-start.15 = (bf16[6,128,128]{2,1,0:T(8,128)(2,1)S(1)}, bf16[6,128,128]{2,1,0:T(8,128)(2,1)S(1)}, u32[]{:S(2)}, u32[]{:S(2)}) collective-permute-start(bf16[6,128,128]{2,1,0:T(8,128)(2,1)S(1)} %get-tuple-element.41), channel_id=1, source_target_pairs={{0,2},{1,3},{2,0},{3,1},{4,6},{5,7},{6,4},{7,5},{8,10},{9,11},{10,... | collective-permute-start | bytes 589832 | tf_op jit(solution)/shard_map/ppermute | solution.py:430
  32.9 1.3 %collective-permute-start.16 = (bf16[6,128,128]{2,1,0:T(8,128)(2,1)S(1)}, bf16[6,128,128]{2,1,0:T(8,128)(2,1)S(1)}, u32[]{:S(2)}, u32[]{:S(2)}) collective-permute-start(bf16[6,128,128]{2,1,0:T(8,128)(2,1)S(1)} %get-tuple-element.42), channel_id=1, source_target_pairs={{0,1},{1,2},{2,3},{3,0},{4,5},{5,6},{6,7},{7,4},{8,9},{9,10},{10,1... | collective-permute-start | bytes 589832 | tf_op jit(solution)/shard_map/ppermute | solution.py:430
  34.2 1.4 %forward_here.1.total = f32[6,128,128]{2,1,0:T(8,128)S(1)} custom-call(s32[1,1664]{1,0:T(1,128)S(1)} %get-tuple-element.29.plan, bf16[513,128,128]{2,1,0:T(8,128)(2,1)S(1)} %get-tuple-element.39.held, bf16[48,128,128]{2,1,0:T(8,128)(2,1)S(1)} %get-tuple-element.40.feats), custom_call_target="tpu_custom_call" | custom-call | flops 128 | bytes 128 | tf_op jit(solution)/shard_map/forward_here/pallas_call | solution.py:323
  35.6 1.9 %collective-permute-done.17.third = bf16[6,128,128]{2,1,0:T(8,128)(2,1)S(1)} collective-permute-done((bf16[6,128,128]{2,1,0:T(8,128)(2,1)S(1)}, bf16[6,128,128]{2,1,0:T(8,128)(2,1)S(1)}, u32[]{:S(2)}, u32[]{:S(2)}) %collective-permute-start.17) | collective-permute-done | bytes 196640 | tf_op jit(solution)/shard_map/ppermute | solution.py:430
  37.6 1.2 %collective-permute-done.15.first = bf16[6,128,128]{2,1,0:T(8,128)(2,1)S(1)} collective-permute-done((bf16[6,128,128]{2,1,0:T(8,128)(2,1)S(1)}, bf16[6,128,128]{2,1,0:T(8,128)(2,1)S(1)}, u32[]{:S(2)}, u32[]{:S(2)}) %collective-permute-start.15) | collective-permute-done | bytes 196640 | tf_op jit(solution)/shard_map/ppermute | solution.py:430
  38.7 2.2 %collective-permute-done.16.second = bf16[6,128,128]{2,1,0:T(8,128)(2,1)S(1)} collective-permute-done((bf16[6,128,128]{2,1,0:T(8,128)(2,1)S(1)}, bf16[6,128,128]{2,1,0:T(8,128)(2,1)S(1)}, u32[]{:S(2)}, u32[]{:S(2)}) %collective-permute-start.16) | collective-permute-done | bytes 196640 | tf_op jit(solution)/shard_map/ppermute | solution.py:430
  40.9 0.1 add.1
  41.0 4.1 %collective-permute-start.18 = (bf16[3,128,128]{2,1,0:T(8,128)(2,1)S(1)}, bf16[3,128,128]{2,1,0:T(8,128)(2,1)S(1)}, u32[]{:S(2)}, u32[]{:S(2)}) collective-permute-start(bf16[3,128,128]{2,1,0:T(8,128)(2,1)S(1)} %get-tuple-element.44), channel_id=1, source_target_pairs={{0,4},{4,0},{1,5},{5,1},{2,6},{6,2},{3,7},{7,3},{8,12},{12,8},{9,1... | collective-permute-start | bytes 294920 | tf_op jit(solution)/shard_map/ppermute | solution.py:430
  45.1 2.6 %collective-permute-done.18 = bf16[3,128,128]{2,1,0:T(8,128)(2,1)S(1)} collective-permute-done((bf16[3,128,128]{2,1,0:T(8,128)(2,1)S(1)}, bf16[3,128,128]{2,1,0:T(8,128)(2,1)S(1)}, u32[]{:S(2)}, u32[]{:S(2)}) %collective-permute-start.18) | collective-permute-done | bytes 98336 | tf_op jit(solution)/shard_map/ppermute | solution.py:430
  47.7 1.1 %middle.1 = (bf16[384,256]{1,0:T(8,128)(2,1)}, bf16[5,128,128]{2,1,0:T(8,128)(2,1)S(1)}) custom-call(bf16[128,256]{1,0:T(8,128)(2,1)S(1)} %copy-done.2, bf16[384,256]{1,0:T(8,128)(2,1)S(1)} %copy-done, f32[384,128]{1,0:T(8,128)S(1)} %bitcast.26, bf16[384,128]{1,0:T(8,128)(2,1)S(1)} %bitcast.43), custom_call_target="tpu_custom_call" | custom-call | flops 128 | bytes 128 | tf_op jit(solution)/shard_map/middle/pallas_call | solution.py:323
  48.8 3.5 %collective-permute-start.19 = (bf16[5,128,128]{2,1,0:T(8,128)(2,1)S(1)}, bf16[5,128,128]{2,1,0:T(8,128)(2,1)S(1)}, u32[]{:S(2)}, u32[]{:S(2)}) collective-permute-start(bf16[5,128,128]{2,1,0:T(8,128)(2,1)S(1)} %get-tuple-element.47.own), channel_id=1, source_target_pairs={{0,4},{4,0},{1,5},{5,1},{2,6},{6,2},{3,7},{7,3},{8,12},{12,8},{9,1... | collective-permute-start | bytes 491528 | tf_op jit(solution)/shard_map/ppermute | solution.py:430
  52.3 3.3 %collective-permute-done.19.other = bf16[5,128,128]{2,1,0:T(8,128)(2,1)S(1)} collective-permute-done((bf16[5,128,128]{2,1,0:T(8,128)(2,1)S(1)}, bf16[5,128,128]{2,1,0:T(8,128)(2,1)S(1)}, u32[]{:S(2)}, u32[]{:S(2)}) %collective-permute-start.19) | collective-permute-done | bytes 163872 | tf_op jit(solution)/shard_map/ppermute | solution.py:430
  55.7 1.7 %collective-permute-start.22 = (bf16[8,128,128]{2,1,0:T(8,128)(2,1)S(1)}, bf16[8,128,128]{2,1,0:T(8,128)(2,1)S(1)}, u32[]{:S(2)}, u32[]{:S(2)}) collective-permute-start(bf16[8,128,128]{2,1,0:T(8,128)(2,1)S(1)} %collect.1.first.near), channel_id=1, source_target_pairs={{0,1},{1,2},{2,3},{3,0},{4,5},{5,6},{6,7},{7,4},{8,9},{9,10},{10,1... | collective-permute-start | bytes 786440 | tf_op jit(solution)/shard_map/ppermute | solution.py:430
  57.4 1.6 %collective-permute-start.21 = (bf16[8,128,128]{2,1,0:T(8,128)(2,1)S(1)}, bf16[8,128,128]{2,1,0:T(8,128)(2,1)S(1)}, u32[]{:S(2)}, u32[]{:S(2)}) collective-permute-start(bf16[8,128,128]{2,1,0:T(8,128)(2,1)S(1)} %collect.1.first.near), channel_id=1, source_target_pairs={{0,3},{1,0},{2,1},{3,2},{4,7},{5,4},{6,5},{7,6},{8,11},{9,8},{10,9... | collective-permute-start | bytes 786440 | tf_op jit(solution)/shard_map/ppermute | solution.py:430
  59.0 0.6 collective-permute-start.20
  59.5 8.8 %collective-permute-done.22.second.next_ = bf16[8,128,128]{2,1,0:T(8,128)(2,1)S(1)} collective-permute-done((bf16[8,128,128]{2,1,0:T(8,128)(2,1)S(1)}, bf16[8,128,128]{2,1,0:T(8,128)(2,1)S(1)}, u32[]{:S(2)}, u32[]{:S(2)}) %collective-permute-start.22) | collective-permute-done | bytes 262176 | tf_op jit(solution)/shard_map/ppermute | solution.py:430
  68.3 1.7 %backward_near.1.before = f32[48,128,128]{2,1,0:T(8,128)S(1)} custom-call(s32[1,1664]{1,0:T(1,128)S(1)} %get-tuple-element.46.plan, bf16[513,128,128]{2,1,0:T(8,128)(2,1)S(1)} %get-tuple-element.39.held, bf16[8,128,128]{2,1,0:T(8,128)(2,1)S(1)} %collect.1.first.near, bf16[8,128,128]{2,1,0:T(8,128)(2,1)S(1)} %collective-permute-done.22.second.next_), custom_call_target="tpu_custom_call" | custom-call | flops 128 | bytes 128 | tf_op jit(solution)/shard_map/backward_near/pallas_call | solution.py:323
  70.0 1.7 %backward_sib.1 = (bf16[24,128,128]{2,1,0:T(8,128)(2,1)S(1)}, bf16[2,128,128]{2,1,0:T(8,128)(2,1)S(1)}) custom-call(s32[1,1664]{1,0:T(1,128)S(1)} %get-tuple-element.46.plan, bf16[513,128,128]{2,1,0:T(8,128)(2,1)S(1)} %get-tuple-element.39.held, bf16[8,128,128]{2,1,0:T(8,128)(2,1)S(1)} %collective-permute-done.20.first, ...), custom_call_target="tpu_custom_call" | custom-call | flops 128 | bytes 128 | tf_op jit(solution)/shard_map/backward_sib/pallas_call | solution.py:323
  71.7 0.1 collective-permute-start.23
  71.8 0.5 collective-permute-start.24
  72.3 1.6 %backward_own.1.own = bf16[24,128,128]{2,1,0:T(8,128)(2,1)S(1)} custom-call(s32[1,1664]{1,0:T(1,128)S(1)} %get-tuple-element.46.plan, bf16[513,128,128]{2,1,0:T(8,128)(2,1)S(1)} %get-tuple-element.39.held, bf16[8,128,128]{2,1,0:T(8,128)(2,1)S(1)} %collective-permute-done.20.first, bf16[8,128,128]{2,1,0:T(8,128)(2,1)S(1)} %collective-permute-done.21.second, ...), custom_call_target="tpu_custom_call" | custom-call | flops 128 | bytes 128 | tf_op jit(solution)/shard_map/backward_own/pallas_call | solution.py:323
  73.9 0.2 collective-permute-done.24.other_grad
  74.1 0.2 pair.1
  74.3 26.0 %all_to_all.6.got = bf16[8,640,128]{2,1,0:T(8,128)(2,1)S(1)} all-to-all(bf16[8,640,128]{2,1,0:T(8,128)(2,1)S(1)} %pair.1), channel_id=1, replica_groups=mesh['zl'=2,'x'=4,'core'=2,'zh'=2,'y'=4] {'zl','x'}, dimensions={0} | all-to-all | bytes 2621440 | tf_op jit(solution)/shard_map/all_to_all | solution.py:567
  100.3 0.9 last.1
  (22 shorter events, 0.1 us)
Async XLA Ops:
  0.6 10.0 %collective-permute-start.2 = (bf16[384,128]{1,0:T(8,128)(2,1)}, bf16[384,128]{1,0:T(8,128)(2,1)S(1)}, u32[]{:S(2)}, u32[]{:S(2)}) collective-permute-start(bf16[384,128]{1,0:T(8,128)(2,1)} %param.7), channel_id=1, source_target_pairs={{0,48},{16,0},{32,16},{48,32},{1,49},{17,1},{33,17},{49,33},{2,50}... | collective-permute-start | bytes 294920 | tf_op jit(solution)/shard_map/ppermute | solution.py:430
  3.5 7.1 %collective-permute-start.1 = (bf16[384,128]{1,0:T(8,128)(2,1)}, bf16[384,128]{1,0:T(8,128)(2,1)S(1)}, u32[]{:S(2)}, u32[]{:S(2)}) collective-permute-start(bf16[384,128]{1,0:T(8,128)(2,1)} %param.7), channel_id=1, source_target_pairs={{0,32},{16,48},{32,0},{48,16},{1,33},{17,49},{33,1},{49,17},{2,34}... | collective-permute-start | bytes 294920 | tf_op jit(solution)/shard_map/ppermute | solution.py:430
  4.3 7.3 %collective-permute-start = (bf16[384,128]{1,0:T(8,128)(2,1)}, bf16[384,128]{1,0:T(8,128)(2,1)S(1)}, u32[]{:S(2)}, u32[]{:S(2)}) collective-permute-start(bf16[384,128]{1,0:T(8,128)(2,1)} %param.7), channel_id=1, source_target_pairs={{0,16},{16,32},{32,48},{48,0},{1,17},{17,33},{33,49},{49,1},{2,18}... | collective-permute-start | bytes 294920 | tf_op jit(solution)/shard_map/ppermute | solution.py:430
  5.2 6.4 %collective-permute-start.3 = (bf16[384,128]{1,0:T(8,128)(2,1)}, bf16[384,128]{1,0:T(8,128)(2,1)S(1)}, u32[]{:S(2)}, u32[]{:S(2)}) collective-permute-start(bf16[384,128]{1,0:T(8,128)(2,1)} %param.7), channel_id=1, source_target_pairs={{0,64},{64,0},{1,65},{65,1},{2,66},{66,2},{3,67},{67,3},{4,68},{68... | collective-permute-start | bytes 294920 | tf_op jit(solution)/shard_map/ppermute | solution.py:430
  7.9 3.7 %copy-start.1 = (bf16[384,128]{1,0:T(8,128)(2,1)S(1)}, bf16[384,128]{1,0:T(8,128)(2,1)}, u32[]{:S(2)}) copy-start(bf16[384,128]{1,0:T(8,128)(2,1)} %param.7) | copy-start | bytes 294916
  11.6 2.6 %collective-permute-start.7 = (bf16[384,128]{1,0:T(8,128)(2,1)S(1)}, bf16[384,128]{1,0:T(8,128)(2,1)S(1)}, u32[]{:S(2)}, u32[]{:S(2)}) collective-permute-start(bf16[384,128]{1,0:T(8,128)(2,1)S(1)} %copy-done.1), channel_id=1, source_target_pairs={{0,8},{8,0},{1,9},{9,1},{2,10},{10,2},{3,11},{11,3},{4,12},{12,4},... | collective-permute-start | bytes 294920 | tf_op jit(solution)/shard_map/ppermute | solution.py:425
  11.6 3.6 %collective-permute-start.9 = (bf16[384,128]{1,0:T(8,128)(2,1)S(1)}, bf16[384,128]{1,0:T(8,128)(2,1)S(1)}, u32[]{:S(2)}, u32[]{:S(2)}) collective-permute-start(bf16[384,128]{1,0:T(8,128)(2,1)S(1)} %collective-permute-done.1), channel_id=1, source_target_pairs={{0,8},{8,0},{1,9},{9,1},{2,10},{10,2},{3,11},{11,3},{4,12},{12,4},... | collective-permute-start | bytes 294920 | tf_op jit(solution)/shard_map/ppermute | solution.py:425
  12.1 3.1 %collective-permute-start.8 = (bf16[384,128]{1,0:T(8,128)(2,1)S(1)}, bf16[384,128]{1,0:T(8,128)(2,1)S(1)}, u32[]{:S(2)}, u32[]{:S(2)}) collective-permute-start(bf16[384,128]{1,0:T(8,128)(2,1)S(1)} %collective-permute-done), channel_id=1, source_target_pairs={{0,8},{8,0},{1,9},{9,1},{2,10},{10,2},{3,11},{11,3},{4,12},{12,4},... | collective-permute-start | bytes 294920 | tf_op jit(solution)/shard_map/ppermute | solution.py:425
  12.2 5.6 %collective-permute-start.4 = (bf16[384,128]{1,0:T(8,128)(2,1)S(1)}, bf16[384,128]{1,0:T(8,128)(2,1)S(1)}, u32[]{:S(2)}, u32[]{:S(2)}) collective-permute-start(bf16[384,128]{1,0:T(8,128)(2,1)S(1)} %collective-permute-done), channel_id=1, source_target_pairs={{0,64},{64,0},{1,65},{65,1},{2,66},{66,2},{3,67},{67,3},{4,68},{68... | collective-permute-start | bytes 294920 | tf_op jit(solution)/shard_map/ppermute | solution.py:430
  14.1 5.5 %collective-permute-start.6 = (bf16[384,128]{1,0:T(8,128)(2,1)S(1)}, bf16[384,128]{1,0:T(8,128)(2,1)S(1)}, u32[]{:S(2)}, u32[]{:S(2)}) collective-permute-start(bf16[384,128]{1,0:T(8,128)(2,1)S(1)} %collective-permute-done.2), channel_id=1, source_target_pairs={{0,64},{64,0},{1,65},{65,1},{2,66},{66,2},{3,67},{67,3},{4,68},{68... | collective-permute-start | bytes 294920 | tf_op jit(solution)/shard_map/ppermute | solution.py:430
  14.3 6.3 %collective-permute-start.5 = (bf16[384,128]{1,0:T(8,128)(2,1)S(1)}, bf16[384,128]{1,0:T(8,128)(2,1)S(1)}, u32[]{:S(2)}, u32[]{:S(2)}) collective-permute-start(bf16[384,128]{1,0:T(8,128)(2,1)S(1)} %collective-permute-done.3), channel_id=1, source_target_pairs={{0,32},{16,48},{32,0},{48,16},{1,33},{17,49},{33,1},{49,17},{2,34}... | collective-permute-start | bytes 294920 | tf_op jit(solution)/shard_map/ppermute | solution.py:430
  15.2 5.3 %collective-permute-start.10 = (bf16[384,128]{1,0:T(8,128)(2,1)S(1)}, bf16[384,128]{1,0:T(8,128)(2,1)S(1)}, u32[]{:S(2)}, u32[]{:S(2)}) collective-permute-start(bf16[384,128]{1,0:T(8,128)(2,1)S(1)} %collective-permute-done.2), channel_id=1, source_target_pairs={{0,8},{8,0},{1,9},{9,1},{2,10},{10,2},{3,11},{11,3},{4,12},{12,4},... | collective-permute-start | bytes 294920 | tf_op jit(solution)/shard_map/ppermute | solution.py:425
  15.2 5.3 %collective-permute-start.11 = (bf16[384,128]{1,0:T(8,128)(2,1)S(1)}, bf16[384,128]{1,0:T(8,128)(2,1)S(1)}, u32[]{:S(2)}, u32[]{:S(2)}) collective-permute-start(bf16[384,128]{1,0:T(8,128)(2,1)S(1)} %collective-permute-done.3), channel_id=1, source_target_pairs={{0,8},{8,0},{1,9},{9,1},{2,10},{10,2},{3,11},{11,3},{4,12},{12,4},... | collective-permute-start | bytes 294920 | tf_op jit(solution)/shard_map/ppermute | solution.py:425
  17.8 2.7 %collective-permute-start.12 = (bf16[384,128]{1,0:T(8,128)(2,1)S(1)}, bf16[384,128]{1,0:T(8,128)(2,1)S(1)}, u32[]{:S(2)}, u32[]{:S(2)}) collective-permute-start(bf16[384,128]{1,0:T(8,128)(2,1)S(1)} %collective-permute-done.4), channel_id=1, source_target_pairs={{0,8},{8,0},{1,9},{9,1},{2,10},{10,2},{3,11},{11,3},{4,12},{12,4},... | collective-permute-start | bytes 294920 | tf_op jit(solution)/shard_map/ppermute | solution.py:425
  19.6 1.3 %collective-permute-start.14 = (bf16[384,128]{1,0:T(8,128)(2,1)S(1)}, bf16[384,128]{1,0:T(8,128)(2,1)S(1)}, u32[]{:S(2)}, u32[]{:S(2)}) collective-permute-start(bf16[384,128]{1,0:T(8,128)(2,1)S(1)} %collective-permute-done.6), channel_id=1, source_target_pairs={{0,8},{8,0},{1,9},{9,1},{2,10},{10,2},{3,11},{11,3},{4,12},{12,4},... | collective-permute-start | bytes 294920 | tf_op jit(solution)/shard_map/ppermute | solution.py:425
  20.5 1.3 %collective-permute-start.13 = (bf16[384,128]{1,0:T(8,128)(2,1)S(1)}, bf16[384,128]{1,0:T(8,128)(2,1)S(1)}, u32[]{:S(2)}, u32[]{:S(2)}) collective-permute-start(bf16[384,128]{1,0:T(8,128)(2,1)S(1)} %collective-permute-done.5), channel_id=1, source_target_pairs={{0,8},{8,0},{1,9},{9,1},{2,10},{10,2},{3,11},{11,3},{4,12},{12,4},... | collective-permute-start | bytes 294920 | tf_op jit(solution)/shard_map/ppermute | solution.py:425
  25.0 12.6 %collective-permute-start.17 = (bf16[6,128,128]{2,1,0:T(8,128)(2,1)S(1)}, bf16[6,128,128]{2,1,0:T(8,128)(2,1)S(1)}, u32[]{:S(2)}, u32[]{:S(2)}) collective-permute-start(bf16[6,128,128]{2,1,0:T(8,128)(2,1)S(1)} %forward_next.1), channel_id=1, source_target_pairs={{0,3},{1,0},{2,1},{3,2},{4,7},{5,4},{6,5},{7,6},{8,11},{9,8},{10,9... | collective-permute-start | bytes 589832 | tf_op jit(solution)/shard_map/ppermute | solution.py:430
  28.0 10.7 %collective-permute-start.15 = (bf16[6,128,128]{2,1,0:T(8,128)(2,1)S(1)}, bf16[6,128,128]{2,1,0:T(8,128)(2,1)S(1)}, u32[]{:S(2)}, u32[]{:S(2)}) collective-permute-start(bf16[6,128,128]{2,1,0:T(8,128)(2,1)S(1)} %get-tuple-element.41), channel_id=1, source_target_pairs={{0,2},{1,3},{2,0},{3,1},{4,6},{5,7},{6,4},{7,5},{8,10},{9,11},{10,... | collective-permute-start | bytes 589832 | tf_op jit(solution)/shard_map/ppermute | solution.py:430
  32.9 14.8 %copy-start = (bf16[384,256]{1,0:T(8,128)(2,1)S(1)}, bf16[384,256]{1,0:T(8,128)(2,1)}, u32[]{:S(2)}) copy-start(bf16[384,256]{1,0:T(8,128)(2,1)} %cot.1) | copy-start | bytes 589828
  32.9 14.8 %copy-start.2 = (bf16[128,256]{1,0:T(8,128)(2,1)S(1)}, bf16[128,256]{1,0:T(8,128)(2,1)}, u32[]{:S(2)}) copy-start(bf16[128,256]{1,0:T(8,128)(2,1)} %weight.1) | copy-start | bytes 196612
  32.9 8.0 %collective-permute-start.16 = (bf16[6,128,128]{2,1,0:T(8,128)(2,1)S(1)}, bf16[6,128,128]{2,1,0:T(8,128)(2,1)S(1)}, u32[]{:S(2)}, u32[]{:S(2)}) collective-permute-start(bf16[6,128,128]{2,1,0:T(8,128)(2,1)S(1)} %get-tuple-element.42), channel_id=1, source_target_pairs={{0,1},{1,2},{2,3},{3,0},{4,5},{5,6},{6,7},{7,4},{8,9},{9,10},{10,1... | collective-permute-start | bytes 589832 | tf_op jit(solution)/shard_map/ppermute | solution.py:430
  41.0 6.7 %collective-permute-start.18 = (bf16[3,128,128]{2,1,0:T(8,128)(2,1)S(1)}, bf16[3,128,128]{2,1,0:T(8,128)(2,1)S(1)}, u32[]{:S(2)}, u32[]{:S(2)}) collective-permute-start(bf16[3,128,128]{2,1,0:T(8,128)(2,1)S(1)} %get-tuple-element.44), channel_id=1, source_target_pairs={{0,4},{4,0},{1,5},{5,1},{2,6},{6,2},{3,7},{7,3},{8,12},{12,8},{9,1... | collective-permute-start | bytes 294920 | tf_op jit(solution)/shard_map/ppermute | solution.py:430
  48.8 6.8 %collective-permute-start.19 = (bf16[5,128,128]{2,1,0:T(8,128)(2,1)S(1)}, bf16[5,128,128]{2,1,0:T(8,128)(2,1)S(1)}, u32[]{:S(2)}, u32[]{:S(2)}) collective-permute-start(bf16[5,128,128]{2,1,0:T(8,128)(2,1)S(1)} %get-tuple-element.47.own), channel_id=1, source_target_pairs={{0,4},{4,0},{1,5},{5,1},{2,6},{6,2},{3,7},{7,3},{8,12},{12,8},{9,1... | collective-permute-start | bytes 491528 | tf_op jit(solution)/shard_map/ppermute | solution.py:430
  55.7 12.7 %collective-permute-start.22 = (bf16[8,128,128]{2,1,0:T(8,128)(2,1)S(1)}, bf16[8,128,128]{2,1,0:T(8,128)(2,1)S(1)}, u32[]{:S(2)}, u32[]{:S(2)}) collective-permute-start(bf16[8,128,128]{2,1,0:T(8,128)(2,1)S(1)} %collect.1.first.near), channel_id=1, source_target_pairs={{0,1},{1,2},{2,3},{3,0},{4,5},{5,6},{6,7},{7,4},{8,9},{9,10},{10,1... | collective-permute-start | bytes 786440 | tf_op jit(solution)/shard_map/ppermute | solution.py:430
  57.4 12.6 %collective-permute-start.21 = (bf16[8,128,128]{2,1,0:T(8,128)(2,1)S(1)}, bf16[8,128,128]{2,1,0:T(8,128)(2,1)S(1)}, u32[]{:S(2)}, u32[]{:S(2)}) collective-permute-start(bf16[8,128,128]{2,1,0:T(8,128)(2,1)S(1)} %collect.1.first.near), channel_id=1, source_target_pairs={{0,3},{1,0},{2,1},{3,2},{4,7},{5,4},{6,5},{7,6},{8,11},{9,8},{10,9... | collective-permute-start | bytes 786440 | tf_op jit(solution)/shard_map/ppermute | solution.py:430
  59.0 11.0 %collective-permute-start.20 = (bf16[8,128,128]{2,1,0:T(8,128)(2,1)S(1)}, bf16[8,128,128]{2,1,0:T(8,128)(2,1)S(1)}, u32[]{:S(2)}, u32[]{:S(2)}) collective-permute-start(bf16[8,128,128]{2,1,0:T(8,128)(2,1)S(1)} %collect.1.first.near), channel_id=1, source_target_pairs={{0,2},{1,3},{2,0},{3,1},{4,6},{5,7},{6,4},{7,5},{8,10},{9,11},{10,... | collective-permute-start | bytes 786440 | tf_op jit(solution)/shard_map/ppermute | solution.py:430
  71.7 2.5 %collective-permute-start.23 = (bf16[24,128,128]{2,1,0:T(8,128)(2,1)S(1)}, bf16[24,128,128]{2,1,0:T(8,128)(2,1)S(1)}, u32[]{:S(2)}, u32[]{:S(2)}) collective-permute-start(bf16[24,128,128]{2,1,0:T(8,128)(2,1)S(1)} %get-tuple-element.48), channel_id=1, source_target_pairs={{0,8},{8,0},{1,9},{9,1},{2,10},{10,2},{3,11},{11,3},{4,12},{12,4},... | collective-permute-start | bytes 2359304 | tf_op jit(solution)/shard_map/ppermute | solution.py:425
  71.8 2.4 %collective-permute-start.24 = (bf16[2,128,128]{2,1,0:T(8,128)(2,1)S(1)}, bf16[2,128,128]{2,1,0:T(8,128)(2,1)S(1)}, u32[]{:S(2)}, u32[]{:S(2)}) collective-permute-start(bf16[2,128,128]{2,1,0:T(8,128)(2,1)S(1)} %get-tuple-element.49.grad), channel_id=1, source_target_pairs={{0,8},{8,0},{1,9},{9,1},{2,10},{10,2},{3,11},{11,3},{4,12},{12,4},... | collective-permute-start | bytes 196616 | tf_op jit(solution)/shard_map/ppermute | solution.py:425

commit v3 on v2

--- a/solution.py
+++ b/solution.py
@@ -117,6 +117,10 @@
     plan[0:1, places + targets :] = last
 
 
+def around(parts):
+    return (parts[0] + parts[2]) + (parts[1] + parts[3])
+
+
 def divided(value, by, most):
     return sum(jnp.where(value >= by * t, 1, 0) for t in range(1, most // by + 1))
 
@@ -151,7 +155,8 @@
     owner = owner >> 1
     turned = ((owner >> 2) ^ zl) * 4 + ((x - (owner & 3)) & 3)
     spot = side * half + turned * own_blocks + inner
-    dest = (1 - side) * half + owner * own_blocks + inner
+    ahead = ((owner & 3) - x) & 3
+    dest = (1 - side) * half + (ahead * 2 + ((owner >> 2) ^ zl)) * own_blocks + inner
 
     owner = divided(row, own_blocks, row_blocks - 1)
     inner = row - owner * own_blocks
@@ -216,6 +221,12 @@
     return pltpu.make_async_copy(tiles.at[at], held.at[at], sem)
 
 
+def fetch(plan, here, sem):
+    copy = pltpu.make_async_copy(plan, here, sem)
+    copy.start()
+    return copy
+
+
 def multiply(plan, phases, form, tiles, source, tile_first, total):
     group, unroll = form
     places = places_in(plan, form)
@@ -238,8 +249,9 @@
             )
 
 
-def forward_first_kernel(plan, count, tiles, _, *refs):
-    blocks, (out, after, held, feats, total, sem) = refs[:-6], refs[-6:]
+def forward_first_kernel(count, packed, tiles, _, *refs):
+    blocks, (out, after, held, feats, plan, plan_sem, total, sem) = refs[:-8], refs[-8:]
+    coming = fetch(packed, plan, plan_sem)
     lo, hi = chunks_of(count, tiles, 1)
 
     @pl.loop(lo, hi)
@@ -251,6 +263,7 @@
         feats[n * each : (n + 1) * each] = block[...]
     total[...] = jnp.zeros_like(total)
 
+    coming.wait()
     multiply(plan, (0, 1), FORWARD, held, feats, True, total)
 
     @pl.loop(lo, hi)
@@ -263,9 +276,11 @@
     after[...] = total[half : 2 * half].astype(jnp.bfloat16)
 
 
-def forward_next_kernel(phase, plan, held, feats, out, *scratch):
+def forward_next_kernel(phase, packed, held, feats, out, plan, sem, *scratch):
+    coming = fetch(packed, plan, sem)
     total = scratch[0] if scratch else out
     total[...] = jnp.zeros_like(total)
+    coming.wait()
     multiply(plan, (phase, phase + 1), FORWARD, held, feats, True, total)
     if scratch:
         out[...] = total[...].astype(jnp.bfloat16)
@@ -277,26 +292,36 @@
     source[each : 2 * each] = second[0:each]
 
 
-def backward_near_kernel(plan, held, first, second, total, source):
+def backward_near_kernel(packed, held, first, second, total, plan, sem, source):
+    coming = fetch(packed, plan, sem)
     put_sources(source, first, second)
     total[...] = jnp.zeros_like(total)
+    coming.wait()
     multiply(plan, (0, 1), BACKWARD, held, source, False, total)
 
 
-def backward_sib_kernel(plan, held, first, second, before, near, next_, out, both, source, total):
+def backward_sib_kernel(
+    packed, held, first, second, before, near, next_, out, both, plan, sem, source, total
+):
+    coming = fetch(packed, plan, sem)
     put_sources(source, first, second)
     each = source.shape[0] // 2
     parts = [block[each:].astype(jnp.float32) for block in (near, next_, first, second)]
-    both[...] = sum(parts).astype(jnp.bfloat16)
+    both[...] = around(parts).astype(jnp.bfloat16)
     total[...] = before[0 : total.shape[0]]
+    coming.wait()
     multiply(plan, (1, 2), BACKWARD, held, source, False, total)
     out[...] = total[...].astype(jnp.bfloat16)
 
 
-def backward_own_kernel(plan, held, first, second, before, out, source, total):
+def backward_own_kernel(
+    packed, held, first, second, before, out, plan, sem, source, total
+):
+    coming = fetch(packed, plan, sem)
     put_sources(source, first, second)
     half = total.shape[0]
     total[...] = before[half : 2 * half]
+    coming.wait()
     multiply(plan, (2, 3), BACKWARD, held, source, False, total)
     out[...] = total[...].astype(jnp.bfloat16)
 
@@ -337,6 +362,10 @@
     return jax.ShapeDtypeStruct((n, BS, BS), dtype)
 
 
+def plan_space(plan):
+    return [pltpu.SMEM(plan.shape, jnp.int32), pltpu.SemaphoreType.DMA]
+
+
 def sums(n):
     return pltpu.VMEM((n, BS, BS), jnp.float32)
 
@@ -370,59 +399,36 @@
         send[each + i] = grad[:, i * BS : (i + 1) * BS]
 
 
-def pair_kernel(own, sib, grad, other_grad, send):
-    n_half, lines, _ = send.shape
-    each = own.shape[0] // n_half
+def pair_kernel(own, sib, grad, other_grad, *sends):
     both = grad[...].astype(jnp.float32) + other_grad[...].astype(jnp.float32)
-    both = both.astype(jnp.bfloat16).reshape(-1, BS)
-    for n in range(n_half):
-        for j in range(each):
-            at = n * each + j
-            total = own[at].astype(jnp.float32) + sib[at].astype(jnp.float32)
-            send[n, j * BS : (j + 1) * BS] = total.astype(jnp.bfloat16)
-        send[n, each * BS : lines] = both
-
-
-def pair(own, sib, grad, other_grad, n_half):
-    lines = (own.shape[0] // n_half + grad.shape[0]) * BS
-    return pl.pallas_call(
-        pair_kernel,
-        out_shape=jax.ShapeDtypeStruct((n_half, lines, BS), jnp.bfloat16),
-        in_specs=[vmem()] * 4,
-        out_specs=vmem(),
-        compiler_params=pltpu.CompilerParams(vmem_limit_bytes=LIMIT),
-        name="pair",
-    )(own, sib, grad, other_grad)
-
-
-def last_kernel(got, grad_features, grad_weight):
-    nodes = grad_features.shape[0]
-    total = jnp.sum(got[...].astype(jnp.float32), axis=0)
-    for j in range(nodes // BS):
-        at = slice(j * BS, (j + 1) * BS)
-        grad_features[at] = total[at].T.astype(jnp.bfloat16)
-    rows = grad_weight.shape[0]
+    each = own.shape[0] // len(sends)
+    for n, send in enumerate(sends):
+        at = slice(n * each, (n + 1) * each)
+        total = own[at].astype(jnp.float32) + sib[at].astype(jnp.float32)
+        send[0:each] = total.astype(jnp.bfloat16)
+        send[each:] = both.astype(jnp.bfloat16)
+
+
+def gather_kernel(first, second, third, fourth, keep, send):
+    parts = (first, second, third, fourth)
+    each = keep.shape[0]
+    keep[...] = around([part[0:each].astype(jnp.float32) for part in parts])
+    rest = around([part[each:].astype(jnp.float32) for part in parts])
+    send[...] = rest.astype(jnp.bfloat16)
+
+
+def last_kernel(keep, send, got, grad_features, grad_weight):
+    each = keep.shape[0]
+    for j in range(each):
+        total = keep[j] + got[j].astype(jnp.float32)
+        grad_features[j * BS : (j + 1) * BS] = total.T.astype(jnp.bfloat16)
     for i in range(grad_weight.shape[1] // BS):
-        at = slice(nodes + i * rows, nodes + (i + 1) * rows)
-        grad_weight[:, i * BS : (i + 1) * BS] = total[at]
-
-
-def last(got, nodes, f_in, f_hid):
-    return pl.pallas_call(
-        last_kernel,
-        out_shape=(
-            jax.ShapeDtypeStruct((nodes, f_in), jnp.bfloat16),
-            jax.ShapeDtypeStruct((f_in, f_hid), jnp.float32),
-        ),
-        in_specs=[vmem()],
-        out_specs=(vmem(),) * 2,
-        compiler_params=pltpu.CompilerParams(vmem_limit_bytes=LIMIT),
-        name="last",
-    )(got)
+        total = send[each + i].astype(jnp.float32) + got[each + i].astype(jnp.float32)
+        grad_weight[:, i * BS : (i + 1) * BS] = total
 
 
 def swap_core(value):
-    return lax.ppermute(value, "core", [(0, 1), (1, 0)])
+    return shift(value, "core", 1)
 
 
 def shift(value, axis, by):
@@ -464,13 +470,13 @@
             pltpu.VMEM(held.shape, held.dtype),
             of_blocks(col_blocks),
         ],
-        2,
+        1,
+        tile_count,
         plan_f,
-        tile_count,
         tiles,
         held,
         *blocks,
-        scratch=[sums(2 * each), pltpu.SemaphoreType.DMA],
+        scratch=plan_space(plan_f) + [sums(2 * each), pltpu.SemaphoreType.DMA],
         aliases={3: 2},
         in_hbm=(2,),
     )
@@ -479,11 +485,11 @@
         functools.partial(forward_next_kernel, 2),
         "forward_next",
         [of_blocks(each)],
-        1,
+        0,
         plan_f,
         held,
         feats,
-        scratch=[sums(each)],
+        scratch=plan_space(plan_f) + [sums(each)],
     )
     got.append(shift(third, "y", 3))
     held, feats, third = lax.optimization_barrier((held, feats, third))
@@ -491,10 +497,11 @@
         functools.partial(forward_next_kernel, 3),
         "forward_here",
         [of_blocks(each, jnp.float32)],
-        1,
+        0,
         plan_f,
         held,
         feats,
+        scratch=plan_space(plan_f),
     )
     keep, send = kernel_call(
         add_kernel,
@@ -531,41 +538,69 @@
         backward_near_kernel,
         "backward_near",
         [of_blocks(col_blocks, jnp.float32)],
-        1,
+        0,
         plan_b,
         held,
         *near[:2],
-        scratch=[pltpu.VMEM((2 * each, BS, BS), jnp.bfloat16)],
+        scratch=plan_space(plan_b) + [pltpu.VMEM((2 * each, BS, BS), jnp.bfloat16)],
     )
     half = col_blocks // 2
     sib, grad = kernel_call(
         backward_sib_kernel,
         "backward_sib",
         [of_blocks(half), of_blocks(sent_blocks - own_blocks)],
-        1,
+        0,
         plan_b,
         held,
         *near[2:],
         total,
         *near[:2],
-        scratch=[pltpu.VMEM((2 * each, BS, BS), jnp.bfloat16), sums(half)],
+        scratch=plan_space(plan_b) + [pltpu.VMEM((2 * each, BS, BS), jnp.bfloat16), sums(half)],
     )
     other_sib, other_grad = swap_core(sib), swap_core(grad)
     (own,) = kernel_call(
         backward_own_kernel,
         "backward_own",
         [of_blocks(half)],
-        1,
+        0,
         plan_b,
         held,
         *near[2:],
         total,
-        scratch=[pltpu.VMEM((2 * each, BS, BS), jnp.bfloat16), sums(half)],
+        scratch=plan_space(plan_b) + [pltpu.VMEM((2 * each, BS, BS), jnp.bfloat16), sums(half)],
     )
     other_sib, other_grad, own = lax.optimization_barrier((other_sib, other_grad, own))
-    send = pair(own, other_sib, grad, other_grad, n_half)
-    got = lax.all_to_all(send.reshape(-1, BS), ("zl", "x"), 0, 0, tiled=True)
-    grad_features, grad_weight = last(got.reshape(send.shape), nodes, f_in, f_hid)
+    n_grad = sent_blocks - own_blocks
+    sends = kernel_call(
+        pair_kernel,
+        "pair",
+        [of_blocks(2 * own_blocks + n_grad)] * 4,
+        0,
+        own,
+        other_sib,
+        grad,
+        other_grad,
+    )
+    parts = [sends[0]] + [shift(sends[by], "x", by) for by in (1, 2, 3)]
+    keep, send = kernel_call(
+        gather_kernel,
+        "gather",
+        [of_blocks(own_blocks, jnp.float32), of_blocks(sent_blocks)],
+        0,
+        *parts,
+    )
+    grad_features, grad_weight = kernel_call(
+        last_kernel,
+        "last",
+        [
+            jax.ShapeDtypeStruct((nodes, f_in), jnp.bfloat16),
+            jax.ShapeDtypeStruct((f_in, f_hid), jnp.float32),
+        ],
+        0,
+        keep,
+        send,
+        shift(send, "zl", 1),
+    )
     return hidden, grad_weight, grad_features
 
 

time: 103 us -> 99 us (0.961); the launches traced: 101 us -> 99.3 us
  blocking collectives: 26 us -> 0 us
  waiting for transfers between devices: 27.3 us -> 49.5 us
  Pallas kernels: 14.5 us -> 15.6 us
    all_to_all x1 -> x0, blocking collectives: 26 us -> none  [local(): got = lax.all_to_all(send.reshape(-1, BS), ('zl', 'x'), 0, 0, tiled=True)]
    ppermute x15 -> x29, waiting for transfers between devices: 25.8 us -> 49.5 us  [shift(): return lax.ppermute(value, axis, [(i, (i + by) % n) for i in range(n)])]
    ppermute x15 -> x29, starting transfers between devices: 30.2 us -> 32.6 us  [shift(): return lax.ppermute(value, axis, [(i, (i + by) % n) for i in range(n)])]
    pallas_call x9 -> x12, Pallas kernels: 10.7 us -> 12.7 us  [kernel_call(): pl.pallas_call(kernel, out_shape=tuple(outs), in_specs=specs, out_specs=(...]
    ppermute x10 -> x0, starting transfers between devices: 1.69 us -> none  [swap_core(): return lax.ppermute(value, 'core', [(0, 1), (1, 0)])]
    ppermute x10 -> x0, waiting for transfers between devices: 1.52 us -> none  [swap_core(): return lax.ppermute(value, 'core', [(0, 1), (1, 0)])]
    pallas_call x2 -> x0, Pallas kernels: 1.08 us -> none  [the longest x1 0.88 us: last(): pl.pallas_call(last_kernel, out_shape=(jax.ShapeDtypeStruct((nodes, f_in)...]
  transfers between devices with their start and end apart: 25 -> 29, of which waited for: 13 -> 16; matrix products, arithmetic and copies ran while one was open for 0% -> 0% of each run, Pallas kernels for 7% -> 8%
where the time goes in v3:
time: 99 us; the launch traced here: 99.3 us
  waiting for transfers between devices  49.5 us (50%)
  starting transfers between devices  32.6 us (33%)
  Pallas kernels  15.6 us (16%)
  between operations  1.47 us (1%)
    ppermute x29, waiting for transfers between devices, shift(): return lax.ppermute(value, axis, [(i, (i + by) % n) for i in range(n)])  49.5 us
    ppermute x29, starting transfers between devices, shift(): return lax.ppermute(value, axis, [(i, (i + by) % n) for i in range(n)])  32.6 us
    pallas_call x12, Pallas kernels, kernel_call(): pl.pallas_call(kernel, out_shape=tuple(outs), in_specs=specs, out_specs=(...  12.7 us
    pallas_call x1, Pallas kernels, make_plans(): pl.pallas_call(functools.partial(plan_kernel, sizes), out_shape=(jax.Shap...  2.91 us
  transfers between devices with their start and end apart: 29, of which 16 were waited for; matrix products, arithmetic and copies ran while one was open for 0% of the time, Pallas kernels for 8%

profile of v3, /device:TPU:0, one launch (start us, length us, event | category | flops | bytes accessed | tf_op | source)
XLA Modules:
  0.0 99.3 jit_solution(10505196601428286708)
XLA Ops:
  0.6 2.9 %collective-permute-start.2 = (bf16[384,128]{1,0:T(8,128)(2,1)}, bf16[384,128]{1,0:T(8,128)(2,1)S(1)}, u32[]{:S(2)}, u32[]{:S(2)}) collective-permute-start(bf16[384,128]{1,0:T(8,128)(2,1)} %param.7), channel_id=1, source_target_pairs={{0,48},{16,0},{32,16},{48,32},{1,49},{17,1},{33,17},{49,33},{2,50}... | collective-permute-start | bytes 294920 | tf_op jit(solution)/shard_map/ppermute | solution.py:436
  3.6 0.8 collective-permute-start.1
  4.4 0.9 collective-permute-start
  5.2 1.9 %collective-permute-start.3 = (bf16[384,128]{1,0:T(8,128)(2,1)}, bf16[384,128]{1,0:T(8,128)(2,1)S(1)}, u32[]{:S(2)}, u32[]{:S(2)}) collective-permute-start(bf16[384,128]{1,0:T(8,128)(2,1)} %param.7), channel_id=1, source_target_pairs={{0,64},{64,0},{1,65},{65,1},{2,66},{66,2},{3,67},{67,3},{4,68},{68... | collective-permute-start | bytes 294920 | tf_op jit(solution)/shard_map/ppermute | solution.py:436
  7.9 2.9 %make_plans.1 = (s32[1,1664]{1,0:T(1,128)S(1)}, s32[1,1664]{1,0:T(1,128)S(1)}, bf16[513,128,128]{2,1,0:T(8,128)(2,1)S(1)}) custom-call(s32[5]{0:T(128)S(1)} %stack.23.where, s32[1,1]{1,0:T(1,128)S(6)} %copy.12.count, s32[1,512]{1,0:T(1,128)} %bitcast.46, s32[1,512]{1,0:T(1,128)} %bitcast.47, bf16[512,128,128]{2,1,0:T(8,128)(2,1)} %bitcast.44), custom_call_target="tpu_custom_call" | custom-call | bytes 8388608 | tf_op jit(solution)/shard_map/make_plans/pallas_call | solution.py:194
  10.8 0.8 collective-permute-done
  11.6 0.5 collective-permute-start.9
  12.1 0.1 collective-permute-start.8
  12.2 1.9 %collective-permute-start.4 = (bf16[384,128]{1,0:T(8,128)(2,1)S(1)}, bf16[384,128]{1,0:T(8,128)(2,1)S(1)}, u32[]{:S(2)}, u32[]{:S(2)}) collective-permute-start(bf16[384,128]{1,0:T(8,128)(2,1)S(1)} %collective-permute-done), channel_id=1, source_target_pairs={{0,64},{64,0},{1,65},{65,1},{2,66},{66,2},{3,67},{67,3},{4,68},{68... | collective-permute-start | bytes 294920 | tf_op jit(solution)/shard_map/ppermute | solution.py:436
  14.2 0.1 collective-permute-start.6
  14.3 0.9 collective-permute-start.5
  15.2 0.5 collective-permute-start.11
  15.7 2.1 %collective-permute-done.4 = bf16[384,128]{1,0:T(8,128)(2,1)S(1)} collective-permute-done((bf16[384,128]{1,0:T(8,128)(2,1)S(1)}, bf16[384,128]{1,0:T(8,128)(2,1)S(1)}, u32[]{:S(2)}, u32[]{:S(2)}) %collective-permute-start.4) | collective-permute-done | bytes 98336 | tf_op jit(solution)/shard_map/ppermute | solution.py:436
  17.8 1.8 %collective-permute-done.6 = bf16[384,128]{1,0:T(8,128)(2,1)S(1)} collective-permute-done((bf16[384,128]{1,0:T(8,128)(2,1)S(1)}, bf16[384,128]{1,0:T(8,128)(2,1)S(1)}, u32[]{:S(2)}, u32[]{:S(2)}) %collective-permute-start.6) | collective-permute-done | bytes 98336 | tf_op jit(solution)/shard_map/ppermute | solution.py:436
  19.6 0.9 collective-permute-done.5
  20.6 0.4 collective-permute-done.14
  20.9 0.9 collective-permute-done.13
  21.8 2.3 %forward_first.1 = (bf16[6,128,128]{2,1,0:T(8,128)(2,1)S(1)}, bf16[6,128,128]{2,1,0:T(8,128)(2,1)S(1)}, bf16[513,128,128]{2,1,0:T(8,128)(2,1)S(1)}, bf16[48,128,128]{2,1,0:T(8,128)(2,1)S(1)}) custom-call(s32[1,1]{1,0:T(1,128)S(6)} %copy.12.count, s32[1,1664]{1,0:T(1,128)S(1)} %get-tuple-element.35.packed, ...), custom_call_target="tpu_custom_call", output_to_operand_aliasing={{2}: (3, {})} | custom-call | flops 128 | bytes 128 | tf_op jit(solution)/shard_map/forward_first/pallas_call | solution.py:348
  24.1 1.5 %forward_next.1 = bf16[6,128,128]{2,1,0:T(8,128)(2,1)S(1)} custom-call(s32[1,1664]{1,0:T(1,128)S(1)} %get-tuple-element.35.packed, bf16[513,128,128]{2,1,0:T(8,128)(2,1)S(1)} %get-tuple-element.45.held, bf16[48,128,128]{2,1,0:T(8,128)(2,1)S(1)} %get-tuple-element.46.feats), custom_call_target="tpu_custom_call" | custom-call | flops 128 | bytes 128 | tf_op jit(solution)/shard_map/forward_next/pallas_call | solution.py:348
  25.6 2.3 %collective-permute-start.17 = (bf16[6,128,128]{2,1,0:T(8,128)(2,1)S(1)}, bf16[6,128,128]{2,1,0:T(8,128)(2,1)S(1)}, u32[]{:S(2)}, u32[]{:S(2)}) collective-permute-start(bf16[6,128,128]{2,1,0:T(8,128)(2,1)S(1)} %forward_next.1), channel_id=1, source_target_pairs={{0,3},{1,0},{2,1},{3,2},{4,7},{5,4},{6,5},{7,6},{8,11},{9,8},{10,9... | collective-permute-start | bytes 589832 | tf_op jit(solution)/shard_map/ppermute | solution.py:436
  27.9 0.6 collective-permute-start.15
  28.5 0.3 collective-permute-start.16
  28.9 1.4 %forward_here.1.total = f32[6,128,128]{2,1,0:T(8,128)S(1)} custom-call(s32[1,1664]{1,0:T(1,128)S(1)} %get-tuple-element.35.packed, bf16[513,128,128]{2,1,0:T(8,128)(2,1)S(1)} %get-tuple-element.45.held, bf16[48,128,128]{2,1,0:T(8,128)(2,1)S(1)} %get-tuple-element.46.feats), custom_call_target="tpu_custom_call" | custom-call | flops 128 | bytes 128 | tf_op jit(solution)/shard_map/forward_here/pallas_call | solution.py:348
  30.3 6.8 %collective-permute-done.17.third = bf16[6,128,128]{2,1,0:T(8,128)(2,1)S(1)} collective-permute-done((bf16[6,128,128]{2,1,0:T(8,128)(2,1)S(1)}, bf16[6,128,128]{2,1,0:T(8,128)(2,1)S(1)}, u32[]{:S(2)}, u32[]{:S(2)}) %collective-permute-start.17) | collective-permute-done | bytes 196640 | tf_op jit(solution)/shard_map/ppermute | solution.py:436
  37.2 3.7 %collective-permute-done.16.second = bf16[6,128,128]{2,1,0:T(8,128)(2,1)S(1)} collective-permute-done((bf16[6,128,128]{2,1,0:T(8,128)(2,1)S(1)}, bf16[6,128,128]{2,1,0:T(8,128)(2,1)S(1)}, u32[]{:S(2)}, u32[]{:S(2)}) %collective-permute-start.16) | collective-permute-done | bytes 196640 | tf_op jit(solution)/shard_map/ppermute | solution.py:436
  40.9 0.1 add.1
  41.0 3.7 %collective-permute-start.18 = (bf16[3,128,128]{2,1,0:T(8,128)(2,1)S(1)}, bf16[3,128,128]{2,1,0:T(8,128)(2,1)S(1)}, u32[]{:S(2)}, u32[]{:S(2)}) collective-permute-start(bf16[3,128,128]{2,1,0:T(8,128)(2,1)S(1)} %get-tuple-element.50), channel_id=1, source_target_pairs={{0,4},{4,0},{1,5},{5,1},{2,6},{6,2},{3,7},{7,3},{8,12},{12,8},{9,1... | collective-permute-start | bytes 294920 | tf_op jit(solution)/shard_map/ppermute | solution.py:436
  44.7 2.7 %collective-permute-done.18 = bf16[3,128,128]{2,1,0:T(8,128)(2,1)S(1)} collective-permute-done((bf16[3,128,128]{2,1,0:T(8,128)(2,1)S(1)}, bf16[3,128,128]{2,1,0:T(8,128)(2,1)S(1)}, u32[]{:S(2)}, u32[]{:S(2)}) %collective-permute-start.18) | collective-permute-done | bytes 98336 | tf_op jit(solution)/shard_map/ppermute | solution.py:436
  47.4 1.1 %middle.1 = (bf16[384,256]{1,0:T(8,128)(2,1)}, bf16[5,128,128]{2,1,0:T(8,128)(2,1)S(1)}) custom-call(bf16[128,256]{1,0:T(8,128)(2,1)S(1)} %copy-done.2, bf16[384,256]{1,0:T(8,128)(2,1)S(1)} %copy-done, f32[384,128]{1,0:T(8,128)S(1)} %bitcast.26, bf16[384,128]{1,0:T(8,128)(2,1)S(1)} %bitcast.43), custom_call_target="tpu_custom_call" | custom-call | flops 128 | bytes 128 | tf_op jit(solution)/shard_map/middle/pallas_call | solution.py:348
  48.5 3.5 %collective-permute-start.19 = (bf16[5,128,128]{2,1,0:T(8,128)(2,1)S(1)}, bf16[5,128,128]{2,1,0:T(8,128)(2,1)S(1)}, u32[]{:S(2)}, u32[]{:S(2)}) collective-permute-start(bf16[5,128,128]{2,1,0:T(8,128)(2,1)S(1)} %get-tuple-element.53.own), channel_id=1, source_target_pairs={{0,4},{4,0},{1,5},{5,1},{2,6},{6,2},{3,7},{7,3},{8,12},{12,8},{9,1... | collective-permute-start | bytes 491528 | tf_op jit(solution)/shard_map/ppermute | solution.py:436
  51.9 3.4 %collective-permute-done.19.other = bf16[5,128,128]{2,1,0:T(8,128)(2,1)S(1)} collective-permute-done((bf16[5,128,128]{2,1,0:T(8,128)(2,1)S(1)}, bf16[5,128,128]{2,1,0:T(8,128)(2,1)S(1)}, u32[]{:S(2)}, u32[]{:S(2)}) %collective-permute-start.19) | collective-permute-done | bytes 163872 | tf_op jit(solution)/shard_map/ppermute | solution.py:436
  55.4 3.2 %collective-permute-start.21 = (bf16[8,128,128]{2,1,0:T(8,128)(2,1)S(1)}, bf16[8,128,128]{2,1,0:T(8,128)(2,1)S(1)}, u32[]{:S(2)}, u32[]{:S(2)}) collective-permute-start(bf16[8,128,128]{2,1,0:T(8,128)(2,1)S(1)} %collect.1.first.near), channel_id=1, source_target_pairs={{0,3},{1,0},{2,1},{3,2},{4,7},{5,4},{6,5},{7,6},{8,11},{9,8},{10,9... | collective-permute-start | bytes 786440 | tf_op jit(solution)/shard_map/ppermute | solution.py:436
  58.7 9.9 %collective-permute-done.22.second.next_ = bf16[8,128,128]{2,1,0:T(8,128)(2,1)S(1)} collective-permute-done((bf16[8,128,128]{2,1,0:T(8,128)(2,1)S(1)}, bf16[8,128,128]{2,1,0:T(8,128)(2,1)S(1)}, u32[]{:S(2)}, u32[]{:S(2)}) %collective-permute-start.22) | collective-permute-done | bytes 262176 | tf_op jit(solution)/shard_map/ppermute | solution.py:436
  68.6 2.2 %backward_near.1.before = f32[48,128,128]{2,1,0:T(8,128)S(1)} custom-call(s32[1,1664]{1,0:T(1,128)S(1)} %get-tuple-element.52.packed, bf16[513,128,128]{2,1,0:T(8,128)(2,1)S(1)} %get-tuple-element.45.held, bf16[8,128,128]{2,1,0:T(8,128)(2,1)S(1)} %collect.1.first.near, bf16[8,128,128]{2,1,0:T(8,128)(2,1)S(1)} %collective-permute-done.22.second.next_), custom_call_target="tpu_custom_call" | custom-call | flops 128 | bytes 128 | tf_op jit(solution)/shard_map/backward_near/pallas_call | solution.py:348
  70.9 1.5 %backward_sib.1 = (bf16[24,128,128]{2,1,0:T(8,128)(2,1)S(1)}, bf16[2,128,128]{2,1,0:T(8,128)(2,1)S(1)}) custom-call(s32[1,1664]{1,0:T(1,128)S(1)} %get-tuple-element.52.packed, bf16[513,128,128]{2,1,0:T(8,128)(2,1)S(1)} %get-tuple-element.45.held, bf16[8,128,128]{2,1,0:T(8,128)(2,1)S(1)} %collective-permute-done.20.first, ...), custom_call_target="tpu_custom_call" | custom-call | flops 128 | bytes 128 | tf_op jit(solution)/shard_map/backward_sib/pallas_call | solution.py:348
  72.5 0.5 collective-permute-start.24
  73.0 1.5 %backward_own.1.own = bf16[24,128,128]{2,1,0:T(8,128)(2,1)S(1)} custom-call(s32[1,1664]{1,0:T(1,128)S(1)} %get-tuple-element.52.packed, bf16[513,128,128]{2,1,0:T(8,128)(2,1)S(1)} %get-tuple-element.45.held, bf16[8,128,128]{2,1,0:T(8,128)(2,1)S(1)} %collective-permute-done.20.first, bf16[8,128,128]{2,1,0:T(8,128)(2,1)S(1)} %collective-permute-done.21.second, ...), custom_call_target="tpu_custom_call" | custom-call | flops 128 | bytes 128 | tf_op jit(solution)/shard_map/backward_own/pallas_call | solution.py:348
  74.5 0.3 collective-permute-done.24.other_grad
  74.9 0.2 pair.1
  75.1 1.1 %collective-permute-start.25 = (bf16[8,128,128]{2,1,0:T(8,128)(2,1)S(1)}, bf16[8,128,128]{2,1,0:T(8,128)(2,1)S(1)}, u32[]{:S(2)}, u32[]{:S(2)}) collective-permute-start(bf16[8,128,128]{2,1,0:T(8,128)(2,1)S(1)} %get-tuple-element.60), channel_id=1, source_target_pairs={{0,16},{16,32},{32,48},{48,0},{1,17},{17,33},{33,49},{49,1},{2,18}... | collective-permute-start | bytes 786440 | tf_op jit(solution)/shard_map/ppermute | solution.py:436
  76.2 1.3 %collective-permute-start.26 = (bf16[8,128,128]{2,1,0:T(8,128)(2,1)S(1)}, bf16[8,128,128]{2,1,0:T(8,128)(2,1)S(1)}, u32[]{:S(2)}, u32[]{:S(2)}) collective-permute-start(bf16[8,128,128]{2,1,0:T(8,128)(2,1)S(1)} %get-tuple-element.61), channel_id=1, source_target_pairs={{0,32},{16,48},{32,0},{48,16},{1,33},{17,49},{33,1},{49,17},{2,34}... | collective-permute-start | bytes 786440 | tf_op jit(solution)/shard_map/ppermute | solution.py:436
  77.5 1.5 %collective-permute-start.27 = (bf16[8,128,128]{2,1,0:T(8,128)(2,1)S(1)}, bf16[8,128,128]{2,1,0:T(8,128)(2,1)S(1)}, u32[]{:S(2)}, u32[]{:S(2)}) collective-permute-start(bf16[8,128,128]{2,1,0:T(8,128)(2,1)S(1)} %get-tuple-element.62), channel_id=1, source_target_pairs={{0,48},{16,0},{32,16},{48,32},{1,49},{17,1},{33,17},{49,33},{2,50}... | collective-permute-start | bytes 786440 | tf_op jit(solution)/shard_map/ppermute | solution.py:436
  79.0 11.8 %collective-permute-done.25.second = bf16[8,128,128]{2,1,0:T(8,128)(2,1)S(1)} collective-permute-done((bf16[8,128,128]{2,1,0:T(8,128)(2,1)S(1)}, bf16[8,128,128]{2,1,0:T(8,128)(2,1)S(1)}, u32[]{:S(2)}, u32[]{:S(2)}) %collective-permute-start.25) | collective-permute-done | bytes 262176 | tf_op jit(solution)/shard_map/ppermute | solution.py:436
  90.7 0.6 collective-permute-done.27.fourth
  91.4 0.1 gather.1
  91.5 3.8 %collective-permute-start.28 = (bf16[5,128,128]{2,1,0:T(8,128)(2,1)S(1)}, bf16[5,128,128]{2,1,0:T(8,128)(2,1)S(1)}, u32[]{:S(2)}, u32[]{:S(2)}) collective-permute-start(bf16[5,128,128]{2,1,0:T(8,128)(2,1)S(1)} %get-tuple-element.64.send), channel_id=1, source_target_pairs={{0,64},{64,0},{1,65},{65,1},{2,66},{66,2},{3,67},{67,3},{4,68},{68... | collective-permute-start | bytes 491528 | tf_op jit(solution)/shard_map/ppermute | solution.py:436
  95.3 3.3 %collective-permute-done.28.got = bf16[5,128,128]{2,1,0:T(8,128)(2,1)S(1)} collective-permute-done((bf16[5,128,128]{2,1,0:T(8,128)(2,1)S(1)}, bf16[5,128,128]{2,1,0:T(8,128)(2,1)S(1)}, u32[]{:S(2)}, u32[]{:S(2)}) %collective-permute-start.28) | collective-permute-done | bytes 163872 | tf_op jit(solution)/shard_map/ppermute | solution.py:436
  98.6 0.8 last.1
  (30 shorter events, 0.5 us)
Async XLA Ops:
  0.6 11.0 %copy-start.1 = (bf16[384,128]{1,0:T(8,128)(2,1)S(1)}, bf16[384,128]{1,0:T(8,128)(2,1)}, u32[]{:S(2)}) copy-start(bf16[384,128]{1,0:T(8,128)(2,1)} %param.7) | copy-start | bytes 294916
  0.6 10.2 %collective-permute-start.2 = (bf16[384,128]{1,0:T(8,128)(2,1)}, bf16[384,128]{1,0:T(8,128)(2,1)S(1)}, u32[]{:S(2)}, u32[]{:S(2)}) collective-permute-start(bf16[384,128]{1,0:T(8,128)(2,1)} %param.7), channel_id=1, source_target_pairs={{0,48},{16,0},{32,16},{48,32},{1,49},{17,1},{33,17},{49,33},{2,50}... | collective-permute-start | bytes 294920 | tf_op jit(solution)/shard_map/ppermute | solution.py:436
  3.6 7.3 %collective-permute-start.1 = (bf16[384,128]{1,0:T(8,128)(2,1)}, bf16[384,128]{1,0:T(8,128)(2,1)S(1)}, u32[]{:S(2)}, u32[]{:S(2)}) collective-permute-start(bf16[384,128]{1,0:T(8,128)(2,1)} %param.7), channel_id=1, source_target_pairs={{0,32},{16,48},{32,0},{48,16},{1,33},{17,49},{33,1},{49,17},{2,34}... | collective-permute-start | bytes 294920 | tf_op jit(solution)/shard_map/ppermute | solution.py:436
  4.4 7.3 %collective-permute-start = (bf16[384,128]{1,0:T(8,128)(2,1)}, bf16[384,128]{1,0:T(8,128)(2,1)S(1)}, u32[]{:S(2)}, u32[]{:S(2)}) collective-permute-start(bf16[384,128]{1,0:T(8,128)(2,1)} %param.7), channel_id=1, source_target_pairs={{0,16},{16,32},{32,48},{48,0},{1,17},{17,33},{33,49},{49,1},{2,18}... | collective-permute-start | bytes 294920 | tf_op jit(solution)/shard_map/ppermute | solution.py:436
  5.2 6.4 %collective-permute-start.3 = (bf16[384,128]{1,0:T(8,128)(2,1)}, bf16[384,128]{1,0:T(8,128)(2,1)S(1)}, u32[]{:S(2)}, u32[]{:S(2)}) collective-permute-start(bf16[384,128]{1,0:T(8,128)(2,1)} %param.7), channel_id=1, source_target_pairs={{0,64},{64,0},{1,65},{65,1},{2,66},{66,2},{3,67},{67,3},{4,68},{68... | collective-permute-start | bytes 294920 | tf_op jit(solution)/shard_map/ppermute | solution.py:436
  11.6 2.6 %collective-permute-start.7 = (bf16[384,128]{1,0:T(8,128)(2,1)S(1)}, bf16[384,128]{1,0:T(8,128)(2,1)S(1)}, u32[]{:S(2)}, u32[]{:S(2)}) collective-permute-start(bf16[384,128]{1,0:T(8,128)(2,1)S(1)} %copy-done.1), channel_id=1, source_target_pairs={{0,8},{8,0},{1,9},{9,1},{2,10},{10,2},{3,11},{11,3},{4,12},{12,4},... | collective-permute-start | bytes 294920 | tf_op jit(solution)/shard_map/ppermute | solution.py:436
  11.6 3.6 %collective-permute-start.9 = (bf16[384,128]{1,0:T(8,128)(2,1)S(1)}, bf16[384,128]{1,0:T(8,128)(2,1)S(1)}, u32[]{:S(2)}, u32[]{:S(2)}) collective-permute-start(bf16[384,128]{1,0:T(8,128)(2,1)S(1)} %collective-permute-done.1), channel_id=1, source_target_pairs={{0,8},{8,0},{1,9},{9,1},{2,10},{10,2},{3,11},{11,3},{4,12},{12,4},... | collective-permute-start | bytes 294920 | tf_op jit(solution)/shard_map/ppermute | solution.py:436
  12.1 3.1 %collective-permute-start.8 = (bf16[384,128]{1,0:T(8,128)(2,1)S(1)}, bf16[384,128]{1,0:T(8,128)(2,1)S(1)}, u32[]{:S(2)}, u32[]{:S(2)}) collective-permute-start(bf16[384,128]{1,0:T(8,128)(2,1)S(1)} %collective-permute-done), channel_id=1, source_target_pairs={{0,8},{8,0},{1,9},{9,1},{2,10},{10,2},{3,11},{11,3},{4,12},{12,4},... | collective-permute-start | bytes 294920 | tf_op jit(solution)/shard_map/ppermute | solution.py:436
  12.2 5.6 %collective-permute-start.4 = (bf16[384,128]{1,0:T(8,128)(2,1)S(1)}, bf16[384,128]{1,0:T(8,128)(2,1)S(1)}, u32[]{:S(2)}, u32[]{:S(2)}) collective-permute-start(bf16[384,128]{1,0:T(8,128)(2,1)S(1)} %collective-permute-done), channel_id=1, source_target_pairs={{0,64},{64,0},{1,65},{65,1},{2,66},{66,2},{3,67},{67,3},{4,68},{68... | collective-permute-start | bytes 294920 | tf_op jit(solution)/shard_map/ppermute | solution.py:436
  14.2 5.5 %collective-permute-start.6 = (bf16[384,128]{1,0:T(8,128)(2,1)S(1)}, bf16[384,128]{1,0:T(8,128)(2,1)S(1)}, u32[]{:S(2)}, u32[]{:S(2)}) collective-permute-start(bf16[384,128]{1,0:T(8,128)(2,1)S(1)} %collective-permute-done.2), channel_id=1, source_target_pairs={{0,64},{64,0},{1,65},{65,1},{2,66},{66,2},{3,67},{67,3},{4,68},{68... | collective-permute-start | bytes 294920 | tf_op jit(solution)/shard_map/ppermute | solution.py:436
  14.3 6.3 %collective-permute-start.5 = (bf16[384,128]{1,0:T(8,128)(2,1)S(1)}, bf16[384,128]{1,0:T(8,128)(2,1)S(1)}, u32[]{:S(2)}, u32[]{:S(2)}) collective-permute-start(bf16[384,128]{1,0:T(8,128)(2,1)S(1)} %collective-permute-done.3), channel_id=1, source_target_pairs={{0,32},{16,48},{32,0},{48,16},{1,33},{17,49},{33,1},{49,17},{2,34}... | collective-permute-start | bytes 294920 | tf_op jit(solution)/shard_map/ppermute | solution.py:436
  15.2 5.3 %collective-permute-start.10 = (bf16[384,128]{1,0:T(8,128)(2,1)S(1)}, bf16[384,128]{1,0:T(8,128)(2,1)S(1)}, u32[]{:S(2)}, u32[]{:S(2)}) collective-permute-start(bf16[384,128]{1,0:T(8,128)(2,1)S(1)} %collective-permute-done.2), channel_id=1, source_target_pairs={{0,8},{8,0},{1,9},{9,1},{2,10},{10,2},{3,11},{11,3},{4,12},{12,4},... | collective-permute-start | bytes 294920 | tf_op jit(solution)/shard_map/ppermute | solution.py:436
  15.2 5.3 %collective-permute-start.11 = (bf16[384,128]{1,0:T(8,128)(2,1)S(1)}, bf16[384,128]{1,0:T(8,128)(2,1)S(1)}, u32[]{:S(2)}, u32[]{:S(2)}) collective-permute-start(bf16[384,128]{1,0:T(8,128)(2,1)S(1)} %collective-permute-done.3), channel_id=1, source_target_pairs={{0,8},{8,0},{1,9},{9,1},{2,10},{10,2},{3,11},{11,3},{4,12},{12,4},... | collective-permute-start | bytes 294920 | tf_op jit(solution)/shard_map/ppermute | solution.py:436
  17.8 2.7 %collective-permute-start.12 = (bf16[384,128]{1,0:T(8,128)(2,1)S(1)}, bf16[384,128]{1,0:T(8,128)(2,1)S(1)}, u32[]{:S(2)}, u32[]{:S(2)}) collective-permute-start(bf16[384,128]{1,0:T(8,128)(2,1)S(1)} %collective-permute-done.4), channel_id=1, source_target_pairs={{0,8},{8,0},{1,9},{9,1},{2,10},{10,2},{3,11},{11,3},{4,12},{12,4},... | collective-permute-start | bytes 294920 | tf_op jit(solution)/shard_map/ppermute | solution.py:436
  19.6 1.3 %collective-permute-start.14 = (bf16[384,128]{1,0:T(8,128)(2,1)S(1)}, bf16[384,128]{1,0:T(8,128)(2,1)S(1)}, u32[]{:S(2)}, u32[]{:S(2)}) collective-permute-start(bf16[384,128]{1,0:T(8,128)(2,1)S(1)} %collective-permute-done.6), channel_id=1, source_target_pairs={{0,8},{8,0},{1,9},{9,1},{2,10},{10,2},{3,11},{11,3},{4,12},{12,4},... | collective-permute-start | bytes 294920 | tf_op jit(solution)/shard_map/ppermute | solution.py:436
  20.5 1.3 %collective-permute-start.13 = (bf16[384,128]{1,0:T(8,128)(2,1)S(1)}, bf16[384,128]{1,0:T(8,128)(2,1)S(1)}, u32[]{:S(2)}, u32[]{:S(2)}) collective-permute-start(bf16[384,128]{1,0:T(8,128)(2,1)S(1)} %collective-permute-done.5), channel_id=1, source_target_pairs={{0,8},{8,0},{1,9},{9,1},{2,10},{10,2},{3,11},{11,3},{4,12},{12,4},... | collective-permute-start | bytes 294920 | tf_op jit(solution)/shard_map/ppermute | solution.py:436
  24.1 23.2 %copy-start = (bf16[384,256]{1,0:T(8,128)(2,1)S(1)}, bf16[384,256]{1,0:T(8,128)(2,1)}, u32[]{:S(2)}) copy-start(bf16[384,256]{1,0:T(8,128)(2,1)} %cot.1) | copy-start | bytes 589828
  24.1 23.2 %copy-start.2 = (bf16[128,256]{1,0:T(8,128)(2,1)S(1)}, bf16[128,256]{1,0:T(8,128)(2,1)}, u32[]{:S(2)}) copy-start(bf16[128,256]{1,0:T(8,128)(2,1)} %weight.1) | copy-start | bytes 196612
  25.6 11.5 %collective-permute-start.17 = (bf16[6,128,128]{2,1,0:T(8,128)(2,1)S(1)}, bf16[6,128,128]{2,1,0:T(8,128)(2,1)S(1)}, u32[]{:S(2)}, u32[]{:S(2)}) collective-permute-start(bf16[6,128,128]{2,1,0:T(8,128)(2,1)S(1)} %forward_next.1), channel_id=1, source_target_pairs={{0,3},{1,0},{2,1},{3,2},{4,7},{5,4},{6,5},{7,6},{8,11},{9,8},{10,9... | collective-permute-start | bytes 589832 | tf_op jit(solution)/shard_map/ppermute | solution.py:436
  27.9 9.3 %collective-permute-start.15 = (bf16[6,128,128]{2,1,0:T(8,128)(2,1)S(1)}, bf16[6,128,128]{2,1,0:T(8,128)(2,1)S(1)}, u32[]{:S(2)}, u32[]{:S(2)}) collective-permute-start(bf16[6,128,128]{2,1,0:T(8,128)(2,1)S(1)} %get-tuple-element.47), channel_id=1, source_target_pairs={{0,2},{1,3},{2,0},{3,1},{4,6},{5,7},{6,4},{7,5},{8,10},{9,11},{10,... | collective-permute-start | bytes 589832 | tf_op jit(solution)/shard_map/ppermute | solution.py:436
  28.5 12.3 %collective-permute-start.16 = (bf16[6,128,128]{2,1,0:T(8,128)(2,1)S(1)}, bf16[6,128,128]{2,1,0:T(8,128)(2,1)S(1)}, u32[]{:S(2)}, u32[]{:S(2)}) collective-permute-start(bf16[6,128,128]{2,1,0:T(8,128)(2,1)S(1)} %get-tuple-element.48), channel_id=1, source_target_pairs={{0,1},{1,2},{2,3},{3,0},{4,5},{5,6},{6,7},{7,4},{8,9},{9,10},{10,1... | collective-permute-start | bytes 589832 | tf_op jit(solution)/shard_map/ppermute | solution.py:436
  41.0 6.4 %collective-permute-start.18 = (bf16[3,128,128]{2,1,0:T(8,128)(2,1)S(1)}, bf16[3,128,128]{2,1,0:T(8,128)(2,1)S(1)}, u32[]{:S(2)}, u32[]{:S(2)}) collective-permute-start(bf16[3,128,128]{2,1,0:T(8,128)(2,1)S(1)} %get-tuple-element.50), channel_id=1, source_target_pairs={{0,4},{4,0},{1,5},{5,1},{2,6},{6,2},{3,7},{7,3},{8,12},{12,8},{9,1... | collective-permute-start | bytes 294920 | tf_op jit(solution)/shard_map/ppermute | solution.py:436
  48.5 6.8 %collective-permute-start.19 = (bf16[5,128,128]{2,1,0:T(8,128)(2,1)S(1)}, bf16[5,128,128]{2,1,0:T(8,128)(2,1)S(1)}, u32[]{:S(2)}, u32[]{:S(2)}) collective-permute-start(bf16[5,128,128]{2,1,0:T(8,128)(2,1)S(1)} %get-tuple-element.53.own), channel_id=1, source_target_pairs={{0,4},{4,0},{1,5},{5,1},{2,6},{6,2},{3,7},{7,3},{8,12},{12,8},{9,1... | collective-permute-start | bytes 491528 | tf_op jit(solution)/shard_map/ppermute | solution.py:436
  55.3 13.3 %collective-permute-start.22 = (bf16[8,128,128]{2,1,0:T(8,128)(2,1)S(1)}, bf16[8,128,128]{2,1,0:T(8,128)(2,1)S(1)}, u32[]{:S(2)}, u32[]{:S(2)}) collective-permute-start(bf16[8,128,128]{2,1,0:T(8,128)(2,1)S(1)} %collect.1.first.near), channel_id=1, source_target_pairs={{0,1},{1,2},{2,3},{3,0},{4,5},{5,6},{6,7},{7,4},{8,9},{9,10},{10,1... | collective-permute-start | bytes 786440 | tf_op jit(solution)/shard_map/ppermute | solution.py:436
  55.4 15.4 %collective-permute-start.21 = (bf16[8,128,128]{2,1,0:T(8,128)(2,1)S(1)}, bf16[8,128,128]{2,1,0:T(8,128)(2,1)S(1)}, u32[]{:S(2)}, u32[]{:S(2)}) collective-permute-start(bf16[8,128,128]{2,1,0:T(8,128)(2,1)S(1)} %collect.1.first.near), channel_id=1, source_target_pairs={{0,3},{1,0},{2,1},{3,2},{4,7},{5,4},{6,5},{7,6},{8,11},{9,8},{10,9... | collective-permute-start | bytes 786440 | tf_op jit(solution)/shard_map/ppermute | solution.py:436
  58.6 12.2 %collective-permute-start.20 = (bf16[8,128,128]{2,1,0:T(8,128)(2,1)S(1)}, bf16[8,128,128]{2,1,0:T(8,128)(2,1)S(1)}, u32[]{:S(2)}, u32[]{:S(2)}) collective-permute-start(bf16[8,128,128]{2,1,0:T(8,128)(2,1)S(1)} %collect.1.first.near), channel_id=1, source_target_pairs={{0,2},{1,3},{2,0},{3,1},{4,6},{5,7},{6,4},{7,5},{8,10},{9,11},{10,... | collective-permute-start | bytes 786440 | tf_op jit(solution)/shard_map/ppermute | solution.py:436
  72.4 2.5 %collective-permute-start.23 = (bf16[24,128,128]{2,1,0:T(8,128)(2,1)S(1)}, bf16[24,128,128]{2,1,0:T(8,128)(2,1)S(1)}, u32[]{:S(2)}, u32[]{:S(2)}) collective-permute-start(bf16[24,128,128]{2,1,0:T(8,128)(2,1)S(1)} %get-tuple-element.54), channel_id=1, source_target_pairs={{0,8},{8,0},{1,9},{9,1},{2,10},{10,2},{3,11},{11,3},{4,12},{12,4},... | collective-permute-start | bytes 2359304 | tf_op jit(solution)/shard_map/ppermute | solution.py:436
  72.5 2.4 %collective-permute-start.24 = (bf16[2,128,128]{2,1,0:T(8,128)(2,1)S(1)}, bf16[2,128,128]{2,1,0:T(8,128)(2,1)S(1)}, u32[]{:S(2)}, u32[]{:S(2)}) collective-permute-start(bf16[2,128,128]{2,1,0:T(8,128)(2,1)S(1)} %get-tuple-element.55.grad), channel_id=1, source_target_pairs={{0,8},{8,0},{1,9},{9,1},{2,10},{10,2},{3,11},{11,3},{4,12},{12,4},... | collective-permute-start | bytes 196616 | tf_op jit(solution)/shard_map/ppermute | solution.py:436
  75.1 15.7 %collective-permute-start.25 = (bf16[8,128,128]{2,1,0:T(8,128)(2,1)S(1)}, bf16[8,128,128]{2,1,0:T(8,128)(2,1)S(1)}, u32[]{:S(2)}, u32[]{:S(2)}) collective-permute-start(bf16[8,128,128]{2,1,0:T(8,128)(2,1)S(1)} %get-tuple-element.60), channel_id=1, source_target_pairs={{0,16},{16,32},{32,48},{48,0},{1,17},{17,33},{33,49},{49,1},{2,18}... | collective-permute-start | bytes 786440 | tf_op jit(solution)/shard_map/ppermute | solution.py:436
  76.2 14.5 %collective-permute-start.26 = (bf16[8,128,128]{2,1,0:T(8,128)(2,1)S(1)}, bf16[8,128,128]{2,1,0:T(8,128)(2,1)S(1)}, u32[]{:S(2)}, u32[]{:S(2)}) collective-permute-start(bf16[8,128,128]{2,1,0:T(8,128)(2,1)S(1)} %get-tuple-element.61), channel_id=1, source_target_pairs={{0,32},{16,48},{32,0},{48,16},{1,33},{17,49},{33,1},{49,17},{2,34}... | collective-permute-start | bytes 786440 | tf_op jit(solution)/shard_map/ppermute | solution.py:436
  77.5 13.9 %collective-permute-start.27 = (bf16[8,128,128]{2,1,0:T(8,128)(2,1)S(1)}, bf16[8,128,128]{2,1,0:T(8,128)(2,1)S(1)}, u32[]{:S(2)}, u32[]{:S(2)}) collective-permute-start(bf16[8,128,128]{2,1,0:T(8,128)(2,1)S(1)} %get-tuple-element.62), channel_id=1, source_target_pairs={{0,48},{16,0},{32,16},{48,32},{1,49},{17,1},{33,17},{49,33},{2,50}... | collective-permute-start | bytes 786440 | tf_op jit(solution)/shard_map/ppermute | solution.py:436
  91.5 7.1 %collective-permute-start.28 = (bf16[5,128,128]{2,1,0:T(8,128)(2,1)S(1)}, bf16[5,128,128]{2,1,0:T(8,128)(2,1)S(1)}, u32[]{:S(2)}, u32[]{:S(2)}) collective-permute-start(bf16[5,128,128]{2,1,0:T(8,128)(2,1)S(1)} %get-tuple-element.64.send), channel_id=1, source_target_pairs={{0,64},{64,0},{1,65},{65,1},{2,66},{66,2},{3,67},{67,3},{4,68},{68... | collective-permute-start | bytes 491528 | tf_op jit(solution)/shard_map/ppermute | solution.py:436

commit v4 on v3

--- a/solution.py
+++ b/solution.py
@@ -156,19 +156,19 @@
     turned = ((owner >> 2) ^ zl) * 4 + ((x - (owner & 3)) & 3)
     spot = side * half + turned * own_blocks + inner
     ahead = ((owner & 3) - x) & 3
-    dest = (1 - side) * half + (ahead * 2 + ((owner >> 2) ^ zl)) * own_blocks + inner
+    order = (1 - ((owner >> 2) ^ zl)) * 4 + ahead
+    dest = (1 - side) * half + order * own_blocks + inner
 
     owner = divided(row, own_blocks, row_blocks - 1)
     inner = row - owner * own_blocks
-    inner = inner + ((owner >> 2) ^ zh) * own_blocks
+    away = (owner >> 2) ^ zh
     each = row_blocks // 4
-    later = jnp.where(iota(row.shape, 1) >= row.shape[1] // 2, 2, 0)
-    ahead = ((owner & 3) - y) & 3
-    turn = jnp.where(ahead == 2, later, jnp.where(ahead == 1, later + 1, 4))
-    key = jnp.where(ahead == 0, 5, turn) * each + inner
+    later = jnp.where(iota(row.shape, 1) >= row.shape[1] // 2, 1, 0)
+    turn = jnp.where(away == 1, later, 2)
+    key = (turn * 4 + (((owner & 3) - y) & 3)) * own_blocks + inner
     make_plan(key, forward_bounds(sizes), spot, live, FORWARD, plan_f)
     behind = (y - (owner & 3)) & 3
-    spot = (behind & 1) * each + inner
+    spot = (behind & 1) * each + away * own_blocks + inner
     key = dest + jnp.where(behind >= 2, col_blocks, 0)
     make_plan(key, backward_bounds(sizes), spot, live, BACKWARD, plan_b)
 
@@ -179,7 +179,7 @@
 
 def forward_bounds(sizes):
     each = sizes[1] // 4
-    return (0, 2 * each, 4 * each, 5 * each, 6 * each)
+    return (0, 2 * each, 4 * each, 6 * each)
 
 
 def backward_bounds(sizes):
@@ -249,8 +249,9 @@
             )
 
 
-def forward_first_kernel(count, packed, tiles, _, *refs):
-    blocks, (out, after, held, feats, plan, plan_sem, total, sem) = refs[:-8], refs[-8:]
+def forward_away_kernel(count, packed, tiles, _, *refs):
+    blocks, outs, refs = refs[:-10], refs[-10:-6], refs[-6:]
+    held, feats, plan, plan_sem, total, sem = refs
     coming = fetch(packed, plan, plan_sem)
     lo, hi = chunks_of(count, tiles, 1)
 
@@ -271,19 +272,18 @@
         chunk_copy(tiles, held, sem, i).wait()
 
     multiply(plan, (1, 2), FORWARD, held, feats, True, total)
-    half = out.shape[0]
-    out[...] = total[0:half].astype(jnp.bfloat16)
-    after[...] = total[half : 2 * half].astype(jnp.bfloat16)
-
-
-def forward_next_kernel(phase, packed, held, feats, out, plan, sem, *scratch):
+    for n, out in enumerate(outs):
+        out[...] = total[n * out.shape[0] : (n + 1) * out.shape[0]].astype(out.dtype)
+
+
+def forward_here_kernel(packed, held, feats, *refs):
+    outs, (plan, sem, total) = refs[:4], refs[4:]
     coming = fetch(packed, plan, sem)
-    total = scratch[0] if scratch else out
     total[...] = jnp.zeros_like(total)
     coming.wait()
-    multiply(plan, (phase, phase + 1), FORWARD, held, feats, True, total)
-    if scratch:
-        out[...] = total[...].astype(jnp.bfloat16)
+    multiply(plan, (2, 3), FORWARD, held, feats, True, total)
+    for n, out in enumerate(outs):
+        out[...] = total[n * out.shape[0] : (n + 1) * out.shape[0]].astype(out.dtype)
 
 
 def put_sources(source, first, second):
@@ -326,12 +326,9 @@
     out[...] = total[...].astype(jnp.bfloat16)
 
 
-def add_kernel(total, first, second, third, keep, send):
-    parts = [part[...].astype(jnp.float32) for part in (first, second, third)]
-    total = total[...] + sum(parts)
-    each = keep.shape[0]
-    keep[...] = total[0:each]
-    send[...] = total[each : 2 * each].astype(jnp.bfloat16)
+def add_kernel(first, second, third, fourth, send):
+    parts = [part[...].astype(jnp.float32) for part in (first, second, third, fourth)]
+    send[...] = sum(parts).astype(jnp.bfloat16)
 
 
 def collect_kernel(own, other, send):
@@ -406,21 +403,23 @@
         at = slice(n * each, (n + 1) * each)
         total = own[at].astype(jnp.float32) + sib[at].astype(jnp.float32)
         send[0:each] = total.astype(jnp.bfloat16)
-        send[each:] = both.astype(jnp.bfloat16)
-
-
-def gather_kernel(first, second, third, fourth, keep, send):
+        if n < len(sends) // 2:
+            send[each:] = both.astype(jnp.bfloat16)
+
+
+def gather_kernel(first, second, third, fourth, send):
     parts = (first, second, third, fourth)
-    each = keep.shape[0]
-    keep[...] = around([part[0:each].astype(jnp.float32) for part in parts])
-    rest = around([part[each:].astype(jnp.float32) for part in parts])
-    send[...] = rest.astype(jnp.bfloat16)
-
-
-def last_kernel(keep, send, got, grad_features, grad_weight):
-    each = keep.shape[0]
+    send[...] = around([part[...].astype(jnp.float32) for part in parts]).astype(
+        jnp.bfloat16
+    )
+
+
+def last_kernel(send, got, first, second, third, fourth, grad_features, grad_weight):
+    parts = (first, second, third, fourth)
+    each = first.shape[0]
     for j in range(each):
-        total = keep[j] + got[j].astype(jnp.float32)
+        total = around([part[j].astype(jnp.float32) for part in parts])
+        total = total + got[j].astype(jnp.float32)
         grad_features[j * BS : (j + 1) * BS] = total.T.astype(jnp.bfloat16)
     for i in range(grad_weight.shape[1] // BS):
         total = send[each + i].astype(jnp.float32) + got[each + i].astype(jnp.float32)
@@ -461,15 +460,12 @@
     blocks = [b.reshape(own_blocks, BS, f_in) for b in near + far + other]
 
     each = row_blocks // 4
-    first, second, held, feats = kernel_call(
-        forward_first_kernel,
-        "forward_first",
-        [
-            of_blocks(each),
-            of_blocks(each),
-            pltpu.VMEM(held.shape, held.dtype),
-            of_blocks(col_blocks),
-        ],
+    *sends, held, feats = kernel_call(
+        forward_away_kernel,
+        "forward_away",
+        [of_blocks(own_blocks, jnp.float32)]
+        + [of_blocks(own_blocks)] * 3
+        + [pltpu.VMEM(held.shape, held.dtype), of_blocks(col_blocks)],
         1,
         tile_count,
         plan_f,
@@ -477,41 +473,23 @@
         held,
         *blocks,
         scratch=plan_space(plan_f) + [sums(2 * each), pltpu.SemaphoreType.DMA],
-        aliases={3: 2},
+        aliases={3: 4},
         in_hbm=(2,),
     )
-    got = [shift(first, "y", 2), shift(second, "y", 1)]
-    (third,) = kernel_call(
-        functools.partial(forward_next_kernel, 2),
-        "forward_next",
-        [of_blocks(each)],
+    away = [sends[0]] + [shift(sends[by], "y", by) for by in (1, 2, 3)]
+    sends = kernel_call(
+        forward_here_kernel,
+        "forward_here",
+        [of_blocks(own_blocks, jnp.float32)] + [of_blocks(own_blocks)] * 3,
         0,
         plan_f,
         held,
         feats,
-        scratch=plan_space(plan_f) + [sums(each)],
-    )
-    got.append(shift(third, "y", 3))
-    held, feats, third = lax.optimization_barrier((held, feats, third))
-    (total,) = kernel_call(
-        functools.partial(forward_next_kernel, 3),
-        "forward_here",
-        [of_blocks(each, jnp.float32)],
-        0,
-        plan_f,
-        held,
-        feats,
-        scratch=plan_space(plan_f),
-    )
-    keep, send = kernel_call(
-        add_kernel,
-        "add",
-        [of_blocks(own_blocks, jnp.float32), of_blocks(own_blocks)],
-        0,
-        total,
-        *got,
-    )
-    parts = [part.reshape(nodes, f_in) for part in (keep, shift(send, "zh", 1))]
+        scratch=plan_space(plan_f) + [sums(2 * each)],
+    )
+    here = [sends[0]] + [shift(sends[by], "y", by) for by in (1, 2, 3)]
+    (send,) = kernel_call(add_kernel, "add", [of_blocks(own_blocks)], 0, *away)
+    parts = [part.reshape(nodes, f_in) for part in here + [shift(send, "zh", 1)]]
     hidden, send = kernel_call(
         middle_kernel,
         "middle",
@@ -574,20 +552,24 @@
     sends = kernel_call(
         pair_kernel,
         "pair",
-        [of_blocks(2 * own_blocks + n_grad)] * 4,
+        [of_blocks(own_blocks + n_grad)] * 4 + [of_blocks(own_blocks)] * 4,
         0,
         own,
         other_sib,
         grad,
         other_grad,
     )
-    parts = [sends[0]] + [shift(sends[by], "x", by) for by in (1, 2, 3)]
-    keep, send = kernel_call(
+    away = [sends[0]] + [shift(sends[by], "x", by) for by in (2, 1, 3)]
+    here = [sends[4]] + [shift(sends[4 + by], "x", by) for by in (2, 1, 3)]
+    (send,) = kernel_call(
         gather_kernel,
         "gather",
-        [of_blocks(own_blocks, jnp.float32), of_blocks(sent_blocks)],
-        0,
-        *parts,
+        [of_blocks(sent_blocks)],
+        0,
+        away[0],
+        away[2],
+        away[1],
+        away[3],
     )
     grad_features, grad_weight = kernel_call(
         last_kernel,
@@ -597,9 +579,12 @@
             jax.ShapeDtypeStruct((f_in, f_hid), jnp.float32),
         ],
         0,
-        keep,
         send,
         shift(send, "zl", 1),
+        here[0],
+        here[2],
+        here[1],
+        here[3],
     )
     return hidden, grad_weight, grad_features
 

time: 99 us -> 94.3 us (0.953)
  waiting for transfers between devices: 49.5 us -> 28.2 us
  starting transfers between devices: 32.6 us -> 48.3 us
    ppermute x29 -> x35, waiting for transfers between devices: 49.5 us -> 28.2 us  [shift(): return lax.ppermute(value, axis, [(i, (i + by) % n) for i in range(n)])]
    ppermute x29 -> x35, starting transfers between devices: 32.6 us -> 48.3 us  [shift(): return lax.ppermute(value, axis, [(i, (i + by) % n) for i in range(n)])]
    pallas_call x12 -> x11, Pallas kernels: 12.7 us -> 12.8 us  [kernel_call(): pl.pallas_call(kernel, out_shape=tuple(outs), in_specs=specs, out_specs=(...]
  transfers between devices with their start and end apart: 29 -> 35, of which waited for: 16 -> 13; matrix products, arithmetic and copies ran while one was open for 0% -> 0% of each run, Pallas kernels for 8% -> 11%
where the time goes in v4:
time: 94.3 us
  starting transfers between devices  48.3 us (51%)
  waiting for transfers between devices  28.2 us (30%)
  Pallas kernels  16.2 us (17%)
  between operations  1.5 us (2%)
    ppermute x35, starting transfers between devices, shift(): return lax.ppermute(value, axis, [(i, (i + by) % n) for i in range(n)])  48.3 us
    ppermute x35, waiting for transfers between devices, shift(): return lax.ppermute(value, axis, [(i, (i + by) % n) for i in range(n)])  28.2 us
    pallas_call x11, Pallas kernels, kernel_call(): pl.pallas_call(kernel, out_shape=tuple(outs), in_specs=specs, out_specs=(...  12.8 us
    pallas_call x1, Pallas kernels, make_plans(): pl.pallas_call(functools.partial(plan_kernel, sizes), out_shape=(jax.Shap...  3.38 us
  transfers between devices with their start and end apart: 35, of which 13 were waited for; matrix products, arithmetic and copies ran while one was open for 0% of the time, Pallas kernels for 11%

profile of v4, /device:TPU:0, one launch (start us, length us, event | category | flops | bytes accessed | tf_op | source)
XLA Modules:
  0.0 94.3 jit_solution(10424092059128121468)
XLA Ops:
  0.6 2.9 %collective-permute-start.2 = (bf16[384,128]{1,0:T(8,128)(2,1)}, bf16[384,128]{1,0:T(8,128)(2,1)S(1)}, u32[]{:S(2)}, u32[]{:S(2)}) collective-permute-start(bf16[384,128]{1,0:T(8,128)(2,1)} %param.7), channel_id=1, source_target_pairs={{0,48},{16,0},{32,16},{48,32},{1,49},{17,1},{33,17},{49,33},{2,50}... | collective-permute-start | bytes 294920 | tf_op jit(solution)/shard_map/ppermute | solution.py:435
  3.6 0.8 collective-permute-start.1
  4.4 0.9 collective-permute-start
  5.2 1.9 %collective-permute-start.3 = (bf16[384,128]{1,0:T(8,128)(2,1)}, bf16[384,128]{1,0:T(8,128)(2,1)S(1)}, u32[]{:S(2)}, u32[]{:S(2)}) collective-permute-start(bf16[384,128]{1,0:T(8,128)(2,1)} %param.7), channel_id=1, source_target_pairs={{0,64},{64,0},{1,65},{65,1},{2,66},{66,2},{3,67},{67,3},{4,68},{68... | collective-permute-start | bytes 294920 | tf_op jit(solution)/shard_map/ppermute | solution.py:435
  7.9 3.4 %make_plans.1 = (s32[1,1280]{1,0:T(1,128)S(1)}, s32[1,1664]{1,0:T(1,128)S(1)}, bf16[513,128,128]{2,1,0:T(8,128)(2,1)S(1)}) custom-call(s32[5]{0:T(128)S(1)} %stack.23.where, s32[1,1]{1,0:T(1,128)S(6)} %copy.12.count, s32[1,512]{1,0:T(1,128)} %bitcast.52, s32[1,512]{1,0:T(1,128)} %bitcast.53, bf16[512,128,128]{2,1,0:T(8,128)(2,1)} %bitcast.50), custom_call_target="tpu_custom_call" | custom-call | bytes 8388608 | tf_op jit(solution)/shard_map/make_plans/pallas_call | solution.py:194
  11.3 0.3 collective-permute-done
  11.6 0.5 collective-permute-start.9
  12.1 0.1 collective-permute-start.8
  12.2 1.9 %collective-permute-start.4 = (bf16[384,128]{1,0:T(8,128)(2,1)S(1)}, bf16[384,128]{1,0:T(8,128)(2,1)S(1)}, u32[]{:S(2)}, u32[]{:S(2)}) collective-permute-start(bf16[384,128]{1,0:T(8,128)(2,1)S(1)} %collective-permute-done), channel_id=1, source_target_pairs={{0,64},{64,0},{1,65},{65,1},{2,66},{66,2},{3,67},{67,3},{4,68},{68... | collective-permute-start | bytes 294920 | tf_op jit(solution)/shard_map/ppermute | solution.py:435
  14.2 0.1 collective-permute-start.6
  14.3 0.9 collective-permute-start.5
  15.1 0.5 collective-permute-start.11
  15.7 2.2 %collective-permute-done.4 = bf16[384,128]{1,0:T(8,128)(2,1)S(1)} collective-permute-done((bf16[384,128]{1,0:T(8,128)(2,1)S(1)}, bf16[384,128]{1,0:T(8,128)(2,1)S(1)}, u32[]{:S(2)}, u32[]{:S(2)}) %collective-permute-start.4) | collective-permute-done | bytes 98336 | tf_op jit(solution)/shard_map/ppermute | solution.py:435
  17.8 1.8 %collective-permute-done.6 = bf16[384,128]{1,0:T(8,128)(2,1)S(1)} collective-permute-done((bf16[384,128]{1,0:T(8,128)(2,1)S(1)}, bf16[384,128]{1,0:T(8,128)(2,1)S(1)}, u32[]{:S(2)}, u32[]{:S(2)}) %collective-permute-start.6) | collective-permute-done | bytes 98336 | tf_op jit(solution)/shard_map/ppermute | solution.py:435
  19.6 0.9 collective-permute-done.5
  20.6 0.4 collective-permute-done.14
  20.9 0.9 collective-permute-done.13
  21.8 2.2 %forward_away.1 = (f32[3,128,128]{2,1,0:T(8,128)S(1)}, bf16[3,128,128]{2,1,0:T(8,128)(2,1)S(1)}, bf16[3,128,128]{2,1,0:T(8,128)(2,1)S(1)}, bf16[3,128,128]{2,1,0...) custom-call(s32[1,1]{1,0:T(1,128)S(6)} %copy.12.count, ...), custom_call_target="tpu_custom_call", output_to_operand_aliasing={{4}: (3, {})} | custom-call | flops 128 | bytes 128 | tf_op jit(solution)/shard_map/forward_away/pallas_call | solution.py:345
  24.1 0.9 collective-permute-start.18
  25.0 2.9 %collective-permute-start.19 = (bf16[3,128,128]{2,1,0:T(8,128)(2,1)S(1)}, bf16[3,128,128]{2,1,0:T(8,128)(2,1)S(1)}, u32[]{:S(2)}, u32[]{:S(2)}) collective-permute-start(bf16[3,128,128]{2,1,0:T(8,128)(2,1)S(1)} %get-tuple-element.55), channel_id=1, source_target_pairs={{0,2},{1,3},{2,0},{3,1},{4,6},{5,7},{6,4},{7,5},{8,10},{9,11},{10,... | collective-permute-start | bytes 294920 | tf_op jit(solution)/shard_map/ppermute | solution.py:435
  27.9 1.3 %collective-permute-start.20 = (bf16[3,128,128]{2,1,0:T(8,128)(2,1)S(1)}, bf16[3,128,128]{2,1,0:T(8,128)(2,1)S(1)}, u32[]{:S(2)}, u32[]{:S(2)}) collective-permute-start(bf16[3,128,128]{2,1,0:T(8,128)(2,1)S(1)} %get-tuple-element.56), channel_id=1, source_target_pairs={{0,3},{1,0},{2,1},{3,2},{4,7},{5,4},{6,5},{7,6},{8,11},{9,8},{10,9... | collective-permute-start | bytes 294920 | tf_op jit(solution)/shard_map/ppermute | solution.py:435
  29.2 2.2 %forward_here.1 = (f32[3,128,128]{2,1,0:T(8,128)S(1)}, bf16[3,128,128]{2,1,0:T(8,128)(2,1)S(1)}, bf16[3,128,128]{2,1,0:T(8,128)(2,1)S(1)}, bf16[3,128,128]{2,1,0:T(8,128)(2,1)S(1)}) custom-call(s32[1,1280]{1,0:T(1,128)S(1)} %get-tuple-element.39.packed, bf16[513,128,128]{2,1,0:T(8,128)(2,1)S(1)} %get-tuple-element.47.held, ...), custom_call_target="tpu_custom_call" | custom-call | flops 128 | bytes 128 | tf_op jit(solution)/shard_map/forward_here/pallas_call | solution.py:345
  31.5 0.7 collective-permute-start.16
  32.2 2.5 %collective-permute-start.17 = (bf16[3,128,128]{2,1,0:T(8,128)(2,1)S(1)}, bf16[3,128,128]{2,1,0:T(8,128)(2,1)S(1)}, u32[]{:S(2)}, u32[]{:S(2)}) collective-permute-start(bf16[3,128,128]{2,1,0:T(8,128)(2,1)S(1)} %get-tuple-element.52), channel_id=1, source_target_pairs={{0,3},{1,0},{2,1},{3,2},{4,7},{5,4},{6,5},{7,6},{8,11},{9,8},{10,9... | collective-permute-start | bytes 294920 | tf_op jit(solution)/shard_map/ppermute | solution.py:435
  34.8 6.2 %collective-permute-start.21 = (bf16[3,128,128]{2,1,0:T(8,128)(2,1)S(1)}, bf16[3,128,128]{2,1,0:T(8,128)(2,1)S(1)}, u32[]{:S(2)}, u32[]{:S(2)}) collective-permute-start(bf16[3,128,128]{2,1,0:T(8,128)(2,1)S(1)} %add.1), channel_id=1, source_target_pairs={{0,4},{4,0},{1,5},{5,1},{2,6},{6,2},{3,7},{7,3},{8,12},{12,8},{9,1... | collective-permute-start | bytes 294920 | tf_op jit(solution)/shard_map/ppermute | solution.py:435
  41.1 2.6 %collective-permute-done.21 = bf16[3,128,128]{2,1,0:T(8,128)(2,1)S(1)} collective-permute-done((bf16[3,128,128]{2,1,0:T(8,128)(2,1)S(1)}, bf16[3,128,128]{2,1,0:T(8,128)(2,1)S(1)}, u32[]{:S(2)}, u32[]{:S(2)}) %collective-permute-start.21) | collective-permute-done | bytes 98336 | tf_op jit(solution)/shard_map/ppermute | solution.py:435
  43.7 1.1 %middle.1 = (bf16[384,256]{1,0:T(8,128)(2,1)}, bf16[5,128,128]{2,1,0:T(8,128)(2,1)S(1)}) custom-call(bf16[128,256]{1,0:T(8,128)(2,1)S(1)} %copy-done.2, bf16[384,256]{1,0:T(8,128)(2,1)S(1)} %copy-done, f32[384,128]{1,0:T(8,128)S(1)} %bitcast.29, bf16[384,128]{1,0:T(8,128)(2,1)S(1)} %bitcast.46, bf16[384,128]{1,0:T(8,128)(2,1)S(1)} %bitcast.47, ...), custom_call_target="tpu_custom_call" | custom-call | flops 128 | bytes 128 | tf_op jit(solution)/shard_map/middle/pallas_call | solution.py:345
  44.8 3.5 %collective-permute-start.22 = (bf16[5,128,128]{2,1,0:T(8,128)(2,1)S(1)}, bf16[5,128,128]{2,1,0:T(8,128)(2,1)S(1)}, u32[]{:S(2)}, u32[]{:S(2)}) collective-permute-start(bf16[5,128,128]{2,1,0:T(8,128)(2,1)S(1)} %get-tuple-element.59.own), channel_id=1, source_target_pairs={{0,4},{4,0},{1,5},{5,1},{2,6},{6,2},{3,7},{7,3},{8,12},{12,8},{9,1... | collective-permute-start | bytes 491528 | tf_op jit(solution)/shard_map/ppermute | solution.py:435
  48.3 3.3 %collective-permute-done.22.other = bf16[5,128,128]{2,1,0:T(8,128)(2,1)S(1)} collective-permute-done((bf16[5,128,128]{2,1,0:T(8,128)(2,1)S(1)}, bf16[5,128,128]{2,1,0:T(8,128)(2,1)S(1)}, u32[]{:S(2)}, u32[]{:S(2)}) %collective-permute-start.22) | collective-permute-done | bytes 163872 | tf_op jit(solution)/shard_map/ppermute | solution.py:435
  51.6 0.9 collective-permute-start.25
  52.6 2.4 %collective-permute-start.24 = (bf16[8,128,128]{2,1,0:T(8,128)(2,1)S(1)}, bf16[8,128,128]{2,1,0:T(8,128)(2,1)S(1)}, u32[]{:S(2)}, u32[]{:S(2)}) collective-permute-start(bf16[8,128,128]{2,1,0:T(8,128)(2,1)S(1)} %collect.1.first.near), channel_id=1, source_target_pairs={{0,3},{1,0},{2,1},{3,2},{4,7},{5,4},{6,5},{7,6},{8,11},{9,8},{10,9... | collective-permute-start | bytes 786440 | tf_op jit(solution)/shard_map/ppermute | solution.py:435
  54.9 1.7 %collective-permute-start.23 = (bf16[8,128,128]{2,1,0:T(8,128)(2,1)S(1)}, bf16[8,128,128]{2,1,0:T(8,128)(2,1)S(1)}, u32[]{:S(2)}, u32[]{:S(2)}) collective-permute-start(bf16[8,128,128]{2,1,0:T(8,128)(2,1)S(1)} %collect.1.first.near), channel_id=1, source_target_pairs={{0,2},{1,3},{2,0},{3,1},{4,6},{5,7},{6,4},{7,5},{8,10},{9,11},{10,... | collective-permute-start | bytes 786440 | tf_op jit(solution)/shard_map/ppermute | solution.py:435
  56.6 7.6 %collective-permute-done.25.second.next_ = bf16[8,128,128]{2,1,0:T(8,128)(2,1)S(1)} collective-permute-done((bf16[8,128,128]{2,1,0:T(8,128)(2,1)S(1)}, bf16[8,128,128]{2,1,0:T(8,128)(2,1)S(1)}, u32[]{:S(2)}, u32[]{:S(2)}) %collective-permute-start.25) | collective-permute-done | bytes 262176 | tf_op jit(solution)/shard_map/ppermute | solution.py:435
  64.2 2.2 %backward_near.1.before = f32[48,128,128]{2,1,0:T(8,128)S(1)} custom-call(s32[1,1664]{1,0:T(1,128)S(1)} %get-tuple-element.58.packed, bf16[513,128,128]{2,1,0:T(8,128)(2,1)S(1)} %get-tuple-element.47.held, bf16[8,128,128]{2,1,0:T(8,128)(2,1)S(1)} %collect.1.first.near, bf16[8,128,128]{2,1,0:T(8,128)(2,1)S(1)} %collective-permute-done.25.second.next_), custom_call_target="tpu_custom_call" | custom-call | flops 128 | bytes 128 | tf_op jit(solution)/shard_map/backward_near/pallas_call | solution.py:345
  66.5 1.5 %backward_sib.1 = (bf16[24,128,128]{2,1,0:T(8,128)(2,1)S(1)}, bf16[2,128,128]{2,1,0:T(8,128)(2,1)S(1)}) custom-call(s32[1,1664]{1,0:T(1,128)S(1)} %get-tuple-element.58.packed, bf16[513,128,128]{2,1,0:T(8,128)(2,1)S(1)} %get-tuple-element.47.held, bf16[8,128,128]{2,1,0:T(8,128)(2,1)S(1)} %collective-permute-done.23.first, ...), custom_call_target="tpu_custom_call" | custom-call | flops 128 | bytes 128 | tf_op jit(solution)/shard_map/backward_sib/pallas_call | solution.py:345
  68.1 0.5 collective-permute-start.27
  68.6 2.3 %backward_own.1.own = bf16[24,128,128]{2,1,0:T(8,128)(2,1)S(1)} custom-call(s32[1,1664]{1,0:T(1,128)S(1)} %get-tuple-element.58.packed, bf16[513,128,128]{2,1,0:T(8,128)(2,1)S(1)} %get-tuple-element.47.held, bf16[8,128,128]{2,1,0:T(8,128)(2,1)S(1)} %collective-permute-done.23.first, bf16[8,128,128]{2,1,0:T(8,128)(2,1)S(1)} %collective-permute-done.24.second, ...), custom_call_target="tpu_custom_call" | custom-call | flops 128 | bytes 128 | tf_op jit(solution)/shard_map/backward_own/pallas_call | solution.py:345
  70.9 0.2 pair.1
  71.2 4.6 %collective-permute-start.28 = (bf16[5,128,128]{2,1,0:T(8,128)(2,1)S(1)}, bf16[5,128,128]{2,1,0:T(8,128)(2,1)S(1)}, u32[]{:S(2)}, u32[]{:S(2)}) collective-permute-start(bf16[5,128,128]{2,1,0:T(8,128)(2,1)S(1)} %get-tuple-element.66), channel_id=1, source_target_pairs={{0,16},{16,32},{32,48},{48,0},{1,17},{17,33},{33,49},{49,1},{2,18}... | collective-permute-start | bytes 491528 | tf_op jit(solution)/shard_map/ppermute | solution.py:435
  75.8 2.8 %collective-permute-start.30 = (bf16[5,128,128]{2,1,0:T(8,128)(2,1)S(1)}, bf16[5,128,128]{2,1,0:T(8,128)(2,1)S(1)}, u32[]{:S(2)}, u32[]{:S(2)}) collective-permute-start(bf16[5,128,128]{2,1,0:T(8,128)(2,1)S(1)} %get-tuple-element.68), channel_id=1, source_target_pairs={{0,48},{16,0},{32,16},{48,32},{1,49},{17,1},{33,17},{49,33},{2,50}... | collective-permute-start | bytes 491528 | tf_op jit(solution)/shard_map/ppermute | solution.py:435
  78.5 1.7 %collective-permute-done.28.second = bf16[5,128,128]{2,1,0:T(8,128)(2,1)S(1)} collective-permute-done((bf16[5,128,128]{2,1,0:T(8,128)(2,1)S(1)}, bf16[5,128,128]{2,1,0:T(8,128)(2,1)S(1)}, u32[]{:S(2)}, u32[]{:S(2)}) %collective-permute-start.28) | collective-permute-done | bytes 163872 | tf_op jit(solution)/shard_map/ppermute | solution.py:435
  80.3 3.4 %collective-permute-done.29.third = bf16[5,128,128]{2,1,0:T(8,128)(2,1)S(1)} collective-permute-done((bf16[5,128,128]{2,1,0:T(8,128)(2,1)S(1)}, bf16[5,128,128]{2,1,0:T(8,128)(2,1)S(1)}, u32[]{:S(2)}, u32[]{:S(2)}) %collective-permute-start.29) | collective-permute-done | bytes 163872 | tf_op jit(solution)/shard_map/ppermute | solution.py:435
  83.7 0.6 collective-permute-done.30.fourth
  84.5 2.9 %collective-permute-start.32 = (bf16[3,128,128]{2,1,0:T(8,128)(2,1)S(1)}, bf16[3,128,128]{2,1,0:T(8,128)(2,1)S(1)}, u32[]{:S(2)}, u32[]{:S(2)}) collective-permute-start(bf16[3,128,128]{2,1,0:T(8,128)(2,1)S(1)} %get-tuple-element.70), channel_id=1, source_target_pairs={{0,16},{16,32},{32,48},{48,0},{1,17},{17,33},{33,49},{49,1},{2,18}... | collective-permute-start | bytes 294920 | tf_op jit(solution)/shard_map/ppermute | solution.py:435
  87.4 1.3 %collective-permute-start.33 = (bf16[3,128,128]{2,1,0:T(8,128)(2,1)S(1)}, bf16[3,128,128]{2,1,0:T(8,128)(2,1)S(1)}, u32[]{:S(2)}, u32[]{:S(2)}) collective-permute-start(bf16[3,128,128]{2,1,0:T(8,128)(2,1)S(1)} %get-tuple-element.71), channel_id=1, source_target_pairs={{0,32},{16,48},{32,0},{48,16},{1,33},{17,49},{33,1},{49,17},{2,34}... | collective-permute-start | bytes 294920 | tf_op jit(solution)/shard_map/ppermute | solution.py:435
  88.7 2.4 %collective-permute-start.34 = (bf16[3,128,128]{2,1,0:T(8,128)(2,1)S(1)}, bf16[3,128,128]{2,1,0:T(8,128)(2,1)S(1)}, u32[]{:S(2)}, u32[]{:S(2)}) collective-permute-start(bf16[3,128,128]{2,1,0:T(8,128)(2,1)S(1)} %get-tuple-element.72), channel_id=1, source_target_pairs={{0,48},{16,0},{32,16},{48,32},{1,49},{17,1},{33,17},{49,33},{2,50}... | collective-permute-start | bytes 294920 | tf_op jit(solution)/shard_map/ppermute | solution.py:435
  91.1 2.4 %collective-permute-done.33.third = bf16[3,128,128]{2,1,0:T(8,128)(2,1)S(1)} collective-permute-done((bf16[3,128,128]{2,1,0:T(8,128)(2,1)S(1)}, bf16[3,128,128]{2,1,0:T(8,128)(2,1)S(1)}, u32[]{:S(2)}, u32[]{:S(2)}) %collective-permute-start.33) | collective-permute-done | bytes 98336 | tf_op jit(solution)/shard_map/ppermute | solution.py:435
  93.5 0.8 last.1
  (41 shorter events, 0.6 us)
Async XLA Ops:
  0.6 11.0 %copy-start.1 = (bf16[384,128]{1,0:T(8,128)(2,1)S(1)}, bf16[384,128]{1,0:T(8,128)(2,1)}, u32[]{:S(2)}) copy-start(bf16[384,128]{1,0:T(8,128)(2,1)} %param.7) | copy-start | bytes 294916
  0.6 10.6 %collective-permute-start.2 = (bf16[384,128]{1,0:T(8,128)(2,1)}, bf16[384,128]{1,0:T(8,128)(2,1)S(1)}, u32[]{:S(2)}, u32[]{:S(2)}) collective-permute-start(bf16[384,128]{1,0:T(8,128)(2,1)} %param.7), channel_id=1, source_target_pairs={{0,48},{16,0},{32,16},{48,32},{1,49},{17,1},{33,17},{49,33},{2,50}... | collective-permute-start | bytes 294920 | tf_op jit(solution)/shard_map/ppermute | solution.py:435
  3.6 7.7 %collective-permute-start.1 = (bf16[384,128]{1,0:T(8,128)(2,1)}, bf16[384,128]{1,0:T(8,128)(2,1)S(1)}, u32[]{:S(2)}, u32[]{:S(2)}) collective-permute-start(bf16[384,128]{1,0:T(8,128)(2,1)} %param.7), channel_id=1, source_target_pairs={{0,32},{16,48},{32,0},{48,16},{1,33},{17,49},{33,1},{49,17},{2,34}... | collective-permute-start | bytes 294920 | tf_op jit(solution)/shard_map/ppermute | solution.py:435
  4.4 7.3 %collective-permute-start = (bf16[384,128]{1,0:T(8,128)(2,1)}, bf16[384,128]{1,0:T(8,128)(2,1)S(1)}, u32[]{:S(2)}, u32[]{:S(2)}) collective-permute-start(bf16[384,128]{1,0:T(8,128)(2,1)} %param.7), channel_id=1, source_target_pairs={{0,16},{16,32},{32,48},{48,0},{1,17},{17,33},{33,49},{49,1},{2,18}... | collective-permute-start | bytes 294920 | tf_op jit(solution)/shard_map/ppermute | solution.py:435
  5.2 6.4 %collective-permute-start.3 = (bf16[384,128]{1,0:T(8,128)(2,1)}, bf16[384,128]{1,0:T(8,128)(2,1)S(1)}, u32[]{:S(2)}, u32[]{:S(2)}) collective-permute-start(bf16[384,128]{1,0:T(8,128)(2,1)} %param.7), channel_id=1, source_target_pairs={{0,64},{64,0},{1,65},{65,1},{2,66},{66,2},{3,67},{67,3},{4,68},{68... | collective-permute-start | bytes 294920 | tf_op jit(solution)/shard_map/ppermute | solution.py:435
  11.6 2.6 %collective-permute-start.7 = (bf16[384,128]{1,0:T(8,128)(2,1)S(1)}, bf16[384,128]{1,0:T(8,128)(2,1)S(1)}, u32[]{:S(2)}, u32[]{:S(2)}) collective-permute-start(bf16[384,128]{1,0:T(8,128)(2,1)S(1)} %copy-done.1), channel_id=1, source_target_pairs={{0,8},{8,0},{1,9},{9,1},{2,10},{10,2},{3,11},{11,3},{4,12},{12,4},... | collective-permute-start | bytes 294920 | tf_op jit(solution)/shard_map/ppermute | solution.py:435
  11.6 3.5 %collective-permute-start.9 = (bf16[384,128]{1,0:T(8,128)(2,1)S(1)}, bf16[384,128]{1,0:T(8,128)(2,1)S(1)}, u32[]{:S(2)}, u32[]{:S(2)}) collective-permute-start(bf16[384,128]{1,0:T(8,128)(2,1)S(1)} %collective-permute-done.1), channel_id=1, source_target_pairs={{0,8},{8,0},{1,9},{9,1},{2,10},{10,2},{3,11},{11,3},{4,12},{12,4},... | collective-permute-start | bytes 294920 | tf_op jit(solution)/shard_map/ppermute | solution.py:435
  12.1 3.0 %collective-permute-start.8 = (bf16[384,128]{1,0:T(8,128)(2,1)S(1)}, bf16[384,128]{1,0:T(8,128)(2,1)S(1)}, u32[]{:S(2)}, u32[]{:S(2)}) collective-permute-start(bf16[384,128]{1,0:T(8,128)(2,1)S(1)} %collective-permute-done), channel_id=1, source_target_pairs={{0,8},{8,0},{1,9},{9,1},{2,10},{10,2},{3,11},{11,3},{4,12},{12,4},... | collective-permute-start | bytes 294920 | tf_op jit(solution)/shard_map/ppermute | solution.py:435
  12.2 5.6 %collective-permute-start.4 = (bf16[384,128]{1,0:T(8,128)(2,1)S(1)}, bf16[384,128]{1,0:T(8,128)(2,1)S(1)}, u32[]{:S(2)}, u32[]{:S(2)}) collective-permute-start(bf16[384,128]{1,0:T(8,128)(2,1)S(1)} %collective-permute-done), channel_id=1, source_target_pairs={{0,64},{64,0},{1,65},{65,1},{2,66},{66,2},{3,67},{67,3},{4,68},{68... | collective-permute-start | bytes 294920 | tf_op jit(solution)/shard_map/ppermute | solution.py:435
  14.2 5.5 %collective-permute-start.6 = (bf16[384,128]{1,0:T(8,128)(2,1)S(1)}, bf16[384,128]{1,0:T(8,128)(2,1)S(1)}, u32[]{:S(2)}, u32[]{:S(2)}) collective-permute-start(bf16[384,128]{1,0:T(8,128)(2,1)S(1)} %collective-permute-done.2), channel_id=1, source_target_pairs={{0,64},{64,0},{1,65},{65,1},{2,66},{66,2},{3,67},{67,3},{4,68},{68... | collective-permute-start | bytes 294920 | tf_op jit(solution)/shard_map/ppermute | solution.py:435
  14.3 6.3 %collective-permute-start.5 = (bf16[384,128]{1,0:T(8,128)(2,1)S(1)}, bf16[384,128]{1,0:T(8,128)(2,1)S(1)}, u32[]{:S(2)}, u32[]{:S(2)}) collective-permute-start(bf16[384,128]{1,0:T(8,128)(2,1)S(1)} %collective-permute-done.3), channel_id=1, source_target_pairs={{0,32},{16,48},{32,0},{48,16},{1,33},{17,49},{33,1},{49,17},{2,34}... | collective-permute-start | bytes 294920 | tf_op jit(solution)/shard_map/ppermute | solution.py:435
  15.1 5.4 %collective-permute-start.10 = (bf16[384,128]{1,0:T(8,128)(2,1)S(1)}, bf16[384,128]{1,0:T(8,128)(2,1)S(1)}, u32[]{:S(2)}, u32[]{:S(2)}) collective-permute-start(bf16[384,128]{1,0:T(8,128)(2,1)S(1)} %collective-permute-done.2), channel_id=1, source_target_pairs={{0,8},{8,0},{1,9},{9,1},{2,10},{10,2},{3,11},{11,3},{4,12},{12,4},... | collective-permute-start | bytes 294920 | tf_op jit(solution)/shard_map/ppermute | solution.py:435
  15.1 5.4 %collective-permute-start.11 = (bf16[384,128]{1,0:T(8,128)(2,1)S(1)}, bf16[384,128]{1,0:T(8,128)(2,1)S(1)}, u32[]{:S(2)}, u32[]{:S(2)}) collective-permute-start(bf16[384,128]{1,0:T(8,128)(2,1)S(1)} %collective-permute-done.3), channel_id=1, source_target_pairs={{0,8},{8,0},{1,9},{9,1},{2,10},{10,2},{3,11},{11,3},{4,12},{12,4},... | collective-permute-start | bytes 294920 | tf_op jit(solution)/shard_map/ppermute | solution.py:435
  17.8 2.7 %collective-permute-start.12 = (bf16[384,128]{1,0:T(8,128)(2,1)S(1)}, bf16[384,128]{1,0:T(8,128)(2,1)S(1)}, u32[]{:S(2)}, u32[]{:S(2)}) collective-permute-start(bf16[384,128]{1,0:T(8,128)(2,1)S(1)} %collective-permute-done.4), channel_id=1, source_target_pairs={{0,8},{8,0},{1,9},{9,1},{2,10},{10,2},{3,11},{11,3},{4,12},{12,4},... | collective-permute-start | bytes 294920 | tf_op jit(solution)/shard_map/ppermute | solution.py:435
  19.6 1.3 %collective-permute-start.14 = (bf16[384,128]{1,0:T(8,128)(2,1)S(1)}, bf16[384,128]{1,0:T(8,128)(2,1)S(1)}, u32[]{:S(2)}, u32[]{:S(2)}) collective-permute-start(bf16[384,128]{1,0:T(8,128)(2,1)S(1)} %collective-permute-done.6), channel_id=1, source_target_pairs={{0,8},{8,0},{1,9},{9,1},{2,10},{10,2},{3,11},{11,3},{4,12},{12,4},... | collective-permute-start | bytes 294920 | tf_op jit(solution)/shard_map/ppermute | solution.py:435
  20.5 1.3 %collective-permute-start.13 = (bf16[384,128]{1,0:T(8,128)(2,1)S(1)}, bf16[384,128]{1,0:T(8,128)(2,1)S(1)}, u32[]{:S(2)}, u32[]{:S(2)}) collective-permute-start(bf16[384,128]{1,0:T(8,128)(2,1)S(1)} %collective-permute-done.5), channel_id=1, source_target_pairs={{0,8},{8,0},{1,9},{9,1},{2,10},{10,2},{3,11},{11,3},{4,12},{12,4},... | collective-permute-start | bytes 294920 | tf_op jit(solution)/shard_map/ppermute | solution.py:435
  24.1 19.6 %copy-start = (bf16[384,256]{1,0:T(8,128)(2,1)S(1)}, bf16[384,256]{1,0:T(8,128)(2,1)}, u32[]{:S(2)}) copy-start(bf16[384,256]{1,0:T(8,128)(2,1)} %cot.1) | copy-start | bytes 589828
  24.1 19.6 %copy-start.2 = (bf16[128,256]{1,0:T(8,128)(2,1)S(1)}, bf16[128,256]{1,0:T(8,128)(2,1)}, u32[]{:S(2)}) copy-start(bf16[128,256]{1,0:T(8,128)(2,1)} %weight.1) | copy-start | bytes 196612
  24.1 8.1 %collective-permute-start.18 = (bf16[3,128,128]{2,1,0:T(8,128)(2,1)S(1)}, bf16[3,128,128]{2,1,0:T(8,128)(2,1)S(1)}, u32[]{:S(2)}, u32[]{:S(2)}) collective-permute-start(bf16[3,128,128]{2,1,0:T(8,128)(2,1)S(1)} %get-tuple-element.54), channel_id=1, source_target_pairs={{0,1},{1,2},{2,3},{3,0},{4,5},{5,6},{6,7},{7,4},{8,9},{9,10},{10,1... | collective-permute-start | bytes 294920 | tf_op jit(solution)/shard_map/ppermute | solution.py:435
  25.0 9.8 %collective-permute-start.19 = (bf16[3,128,128]{2,1,0:T(8,128)(2,1)S(1)}, bf16[3,128,128]{2,1,0:T(8,128)(2,1)S(1)}, u32[]{:S(2)}, u32[]{:S(2)}) collective-permute-start(bf16[3,128,128]{2,1,0:T(8,128)(2,1)S(1)} %get-tuple-element.55), channel_id=1, source_target_pairs={{0,2},{1,3},{2,0},{3,1},{4,6},{5,7},{6,4},{7,5},{8,10},{9,11},{10,... | collective-permute-start | bytes 294920 | tf_op jit(solution)/shard_map/ppermute | solution.py:435
  27.9 6.9 %collective-permute-start.20 = (bf16[3,128,128]{2,1,0:T(8,128)(2,1)S(1)}, bf16[3,128,128]{2,1,0:T(8,128)(2,1)S(1)}, u32[]{:S(2)}, u32[]{:S(2)}) collective-permute-start(bf16[3,128,128]{2,1,0:T(8,128)(2,1)S(1)} %get-tuple-element.56), channel_id=1, source_target_pairs={{0,3},{1,0},{2,1},{3,2},{4,7},{5,4},{6,5},{7,6},{8,11},{9,8},{10,9... | collective-permute-start | bytes 294920 | tf_op jit(solution)/shard_map/ppermute | solution.py:435
  31.5 9.6 %collective-permute-start.15 = (bf16[3,128,128]{2,1,0:T(8,128)(2,1)S(1)}, bf16[3,128,128]{2,1,0:T(8,128)(2,1)S(1)}, u32[]{:S(2)}, u32[]{:S(2)}) collective-permute-start(bf16[3,128,128]{2,1,0:T(8,128)(2,1)S(1)} %get-tuple-element.50), channel_id=1, source_target_pairs={{0,1},{1,2},{2,3},{3,0},{4,5},{5,6},{6,7},{7,4},{8,9},{9,10},{10,1... | collective-permute-start | bytes 294920 | tf_op jit(solution)/shard_map/ppermute | solution.py:435
  31.5 9.5 %collective-permute-start.16 = (bf16[3,128,128]{2,1,0:T(8,128)(2,1)S(1)}, bf16[3,128,128]{2,1,0:T(8,128)(2,1)S(1)}, u32[]{:S(2)}, u32[]{:S(2)}) collective-permute-start(bf16[3,128,128]{2,1,0:T(8,128)(2,1)S(1)} %get-tuple-element.51), channel_id=1, source_target_pairs={{0,2},{1,3},{2,0},{3,1},{4,6},{5,7},{6,4},{7,5},{8,10},{9,11},{10,... | collective-permute-start | bytes 294920 | tf_op jit(solution)/shard_map/ppermute | solution.py:435
  32.2 8.8 %collective-permute-start.17 = (bf16[3,128,128]{2,1,0:T(8,128)(2,1)S(1)}, bf16[3,128,128]{2,1,0:T(8,128)(2,1)S(1)}, u32[]{:S(2)}, u32[]{:S(2)}) collective-permute-start(bf16[3,128,128]{2,1,0:T(8,128)(2,1)S(1)} %get-tuple-element.52), channel_id=1, source_target_pairs={{0,3},{1,0},{2,1},{3,2},{4,7},{5,4},{6,5},{7,6},{8,11},{9,8},{10,9... | collective-permute-start | bytes 294920 | tf_op jit(solution)/shard_map/ppermute | solution.py:435
  34.8 8.8 %collective-permute-start.21 = (bf16[3,128,128]{2,1,0:T(8,128)(2,1)S(1)}, bf16[3,128,128]{2,1,0:T(8,128)(2,1)S(1)}, u32[]{:S(2)}, u32[]{:S(2)}) collective-permute-start(bf16[3,128,128]{2,1,0:T(8,128)(2,1)S(1)} %add.1), channel_id=1, source_target_pairs={{0,4},{4,0},{1,5},{5,1},{2,6},{6,2},{3,7},{7,3},{8,12},{12,8},{9,1... | collective-permute-start | bytes 294920 | tf_op jit(solution)/shard_map/ppermute | solution.py:435
  44.8 6.8 %collective-permute-start.22 = (bf16[5,128,128]{2,1,0:T(8,128)(2,1)S(1)}, bf16[5,128,128]{2,1,0:T(8,128)(2,1)S(1)}, u32[]{:S(2)}, u32[]{:S(2)}) collective-permute-start(bf16[5,128,128]{2,1,0:T(8,128)(2,1)S(1)} %get-tuple-element.59.own), channel_id=1, source_target_pairs={{0,4},{4,0},{1,5},{5,1},{2,6},{6,2},{3,7},{7,3},{8,12},{12,8},{9,1... | collective-permute-start | bytes 491528 | tf_op jit(solution)/shard_map/ppermute | solution.py:435
  51.6 12.6 %collective-permute-start.25 = (bf16[8,128,128]{2,1,0:T(8,128)(2,1)S(1)}, bf16[8,128,128]{2,1,0:T(8,128)(2,1)S(1)}, u32[]{:S(2)}, u32[]{:S(2)}) collective-permute-start(bf16[8,128,128]{2,1,0:T(8,128)(2,1)S(1)} %collect.1.first.near), channel_id=1, source_target_pairs={{0,1},{1,2},{2,3},{3,0},{4,5},{5,6},{6,7},{7,4},{8,9},{9,10},{10,1... | collective-permute-start | bytes 786440 | tf_op jit(solution)/shard_map/ppermute | solution.py:435
  52.6 13.9 %collective-permute-start.24 = (bf16[8,128,128]{2,1,0:T(8,128)(2,1)S(1)}, bf16[8,128,128]{2,1,0:T(8,128)(2,1)S(1)}, u32[]{:S(2)}, u32[]{:S(2)}) collective-permute-start(bf16[8,128,128]{2,1,0:T(8,128)(2,1)S(1)} %collect.1.first.near), channel_id=1, source_target_pairs={{0,3},{1,0},{2,1},{3,2},{4,7},{5,4},{6,5},{7,6},{8,11},{9,8},{10,9... | collective-permute-start | bytes 786440 | tf_op jit(solution)/shard_map/ppermute | solution.py:435
  54.9 11.5 %collective-permute-start.23 = (bf16[8,128,128]{2,1,0:T(8,128)(2,1)S(1)}, bf16[8,128,128]{2,1,0:T(8,128)(2,1)S(1)}, u32[]{:S(2)}, u32[]{:S(2)}) collective-permute-start(bf16[8,128,128]{2,1,0:T(8,128)(2,1)S(1)} %collect.1.first.near), channel_id=1, source_target_pairs={{0,2},{1,3},{2,0},{3,1},{4,6},{5,7},{6,4},{7,5},{8,10},{9,11},{10,... | collective-permute-start | bytes 786440 | tf_op jit(solution)/shard_map/ppermute | solution.py:435
  68.0 2.9 %collective-permute-start.26 = (bf16[24,128,128]{2,1,0:T(8,128)(2,1)S(1)}, bf16[24,128,128]{2,1,0:T(8,128)(2,1)S(1)}, u32[]{:S(2)}, u32[]{:S(2)}) collective-permute-start(bf16[24,128,128]{2,1,0:T(8,128)(2,1)S(1)} %get-tuple-element.60), channel_id=1, source_target_pairs={{0,8},{8,0},{1,9},{9,1},{2,10},{10,2},{3,11},{11,3},{4,12},{12,4},... | collective-permute-start | bytes 2359304 | tf_op jit(solution)/shard_map/ppermute | solution.py:435
  68.1 2.8 %collective-permute-start.27 = (bf16[2,128,128]{2,1,0:T(8,128)(2,1)S(1)}, bf16[2,128,128]{2,1,0:T(8,128)(2,1)S(1)}, u32[]{:S(2)}, u32[]{:S(2)}) collective-permute-start(bf16[2,128,128]{2,1,0:T(8,128)(2,1)S(1)} %get-tuple-element.61.grad), channel_id=1, source_target_pairs={{0,8},{8,0},{1,9},{9,1},{2,10},{10,2},{3,11},{11,3},{4,12},{12,4},... | collective-permute-start | bytes 196616 | tf_op jit(solution)/shard_map/ppermute | solution.py:435
  71.2 9.1 %collective-permute-start.28 = (bf16[5,128,128]{2,1,0:T(8,128)(2,1)S(1)}, bf16[5,128,128]{2,1,0:T(8,128)(2,1)S(1)}, u32[]{:S(2)}, u32[]{:S(2)}) collective-permute-start(bf16[5,128,128]{2,1,0:T(8,128)(2,1)S(1)} %get-tuple-element.66), channel_id=1, source_target_pairs={{0,16},{16,32},{32,48},{48,0},{1,17},{17,33},{33,49},{49,1},{2,18}... | collective-permute-start | bytes 491528 | tf_op jit(solution)/shard_map/ppermute | solution.py:435
  75.7 7.9 %collective-permute-start.29 = (bf16[5,128,128]{2,1,0:T(8,128)(2,1)S(1)}, bf16[5,128,128]{2,1,0:T(8,128)(2,1)S(1)}, u32[]{:S(2)}, u32[]{:S(2)}) collective-permute-start(bf16[5,128,128]{2,1,0:T(8,128)(2,1)S(1)} %get-tuple-element.67), channel_id=1, source_target_pairs={{0,32},{16,48},{32,0},{48,16},{1,33},{17,49},{33,1},{49,17},{2,34}... | collective-permute-start | bytes 491528 | tf_op jit(solution)/shard_map/ppermute | solution.py:435
  75.8 8.5 %collective-permute-start.30 = (bf16[5,128,128]{2,1,0:T(8,128)(2,1)S(1)}, bf16[5,128,128]{2,1,0:T(8,128)(2,1)S(1)}, u32[]{:S(2)}, u32[]{:S(2)}) collective-permute-start(bf16[5,128,128]{2,1,0:T(8,128)(2,1)S(1)} %get-tuple-element.68), channel_id=1, source_target_pairs={{0,48},{16,0},{32,16},{48,32},{1,49},{17,1},{33,17},{49,33},{2,50}... | collective-permute-start | bytes 491528 | tf_op jit(solution)/shard_map/ppermute | solution.py:435
  84.4 9.1 %collective-permute-start.31 = (bf16[5,128,128]{2,1,0:T(8,128)(2,1)S(1)}, bf16[5,128,128]{2,1,0:T(8,128)(2,1)S(1)}, u32[]{:S(2)}, u32[]{:S(2)}) collective-permute-start(bf16[5,128,128]{2,1,0:T(8,128)(2,1)S(1)} %gather.1.send), channel_id=1, source_target_pairs={{0,64},{64,0},{1,65},{65,1},{2,66},{66,2},{3,67},{67,3},{4,68},{68... | collective-permute-start | bytes 491528 | tf_op jit(solution)/shard_map/ppermute | solution.py:435
  84.5 6.6 %collective-permute-start.32 = (bf16[3,128,128]{2,1,0:T(8,128)(2,1)S(1)}, bf16[3,128,128]{2,1,0:T(8,128)(2,1)S(1)}, u32[]{:S(2)}, u32[]{:S(2)}) collective-permute-start(bf16[3,128,128]{2,1,0:T(8,128)(2,1)S(1)} %get-tuple-element.70), channel_id=1, source_target_pairs={{0,16},{16,32},{32,48},{48,0},{1,17},{17,33},{33,49},{49,1},{2,18}... | collective-permute-start | bytes 294920 | tf_op jit(solution)/shard_map/ppermute | solution.py:435
  87.4 6.1 %collective-permute-start.33 = (bf16[3,128,128]{2,1,0:T(8,128)(2,1)S(1)}, bf16[3,128,128]{2,1,0:T(8,128)(2,1)S(1)}, u32[]{:S(2)}, u32[]{:S(2)}) collective-permute-start(bf16[3,128,128]{2,1,0:T(8,128)(2,1)S(1)} %get-tuple-element.71), channel_id=1, source_target_pairs={{0,32},{16,48},{32,0},{48,16},{1,33},{17,49},{33,1},{49,17},{2,34}... | collective-permute-start | bytes 294920 | tf_op jit(solution)/shard_map/ppermute | solution.py:435
  88.7 4.8 %collective-permute-start.34 = (bf16[3,128,128]{2,1,0:T(8,128)(2,1)S(1)}, bf16[3,128,128]{2,1,0:T(8,128)(2,1)S(1)}, u32[]{:S(2)}, u32[]{:S(2)}) collective-permute-start(bf16[3,128,128]{2,1,0:T(8,128)(2,1)S(1)} %get-tuple-element.72), channel_id=1, source_target_pairs={{0,48},{16,0},{32,16},{48,32},{1,49},{17,1},{33,17},{49,33},{2,50}... | collective-permute-start | bytes 294920 | tf_op jit(solution)/shard_map/ppermute | solution.py:435
